TPU v7x, 32 devices: a whole 2x2x4 slice. The times are simulated.
32 devices in a mesh: mem: 4 (over z), reg: 8 (over y, x, core).
Axes of the slice: x: 2, y: 2, z: 4, core: 2. Of those that a mesh axis runs over, the one named last changes fastest.
Arguments:
- prior_sample_set: bfloat16 [128, 69, 32, 256], P('mem', None, 'reg'), may hold values from -6 to 6
- kernel_in: bfloat16 [2, 9, 128, 69], replicated, may hold values from -0.25 to 0.25
- bias_in: float32 [2, 128], replicated, may hold values from -3 to 3
- kernel_out: bfloat16 [2, 69, 128], replicated, may hold values from -0.5 to 0.5
- observed_cell: int32 [8, 1024], replicated, may hold values from 0 to 1023
- sensor_position_variable: int32 [8, 1024], replicated, may hold values from 0 to 68
- observed_count: int32 [8], replicated, may hold values from 1 to 1024, 4096 in all
- observed_value: float32 [8, 1024], replicated, may hold values from -6 to 6
- error_variance: float32 [8, 1024], replicated, may hold values from 0.5 to 8
- radius: int32 [8], replicated, may hold values from 4 to 16
Outputs:
- analysis: bfloat16 [128, 69, 32, 256], P(None, None, 'reg', 'mem')
Inputs may be any that keep to these rules, and one draw needn't show every extreme that they name: Slots 0 to observed_count - 1 of a band hold observations and the rest are unused; some band uses all 1024 slots.
All inputs are finite; a program needn't handle non-finite values.
Results may differ from a plain program's by a relative error of at most 0.0063.
Values may be sent and summed in bfloat16 or wider, within the bound.
A program may use at most 128 MiB of HBM per device.

v0:
```python
import math

import jax
import jax.numpy as jnp
from jax import lax
from jax.sharding import PartitionSpec as P

NBLK = 2
NS_ITERS = 4


def padded_2(block, sides, width):
    for axis, dim in sides:
        count = lax.axis_size(axis)
        forward = [(i, i + 1) for i in range(count - 1)]
        backward = [(target, source) for source, target in forward]
        low = lax.ppermute(
            lax.slice_in_dim(block, block.shape[dim] - width, None, axis=dim), axis, forward
        )
        high = lax.ppermute(lax.slice_in_dim(block, 0, width, axis=dim), axis, backward)
        block = jnp.concatenate([low, block, high], axis=dim)
    return block


def apply_block(padded_state, kernel_mix, bias_mix, kernel_back):
    members_here = padded_state.shape[0]
    group_size = math.gcd(members_here, 8)
    grouped = padded_state.reshape(
        (members_here // group_size, group_size) + padded_state.shape[1:]
    )

    def group_step(group_state):
        height = group_state.shape[2] - 2
        col_views = jnp.stack(
            [jnp.roll(group_state, 1 - col_shift, axis=3) for col_shift in range(3)], 1
        )
        pre_act = jnp.zeros(
            (group_state.shape[0], kernel_mix.shape[1], height, group_state.shape[3]), jnp.float32
        )
        for row_shift in range(3):
            window = col_views[:, :, :, row_shift : row_shift + height, :]
            taps = kernel_mix[3 * row_shift : 3 * row_shift + 3]
            pre_act = pre_act + jnp.einsum(
                "gcfpl,chf->ghpl", window, taps, preferred_element_type=jnp.float32
            )
        pre_act = pre_act + bias_mix[None, :, None, None]
        hidden = jax.nn.gelu(pre_act).astype(jnp.bfloat16)
        branch = jnp.einsum(
            "ghpl,fh->gfpl", hidden, kernel_back, preferred_element_type=jnp.float32
        )
        return (group_state[:, :, 1:-1, :].astype(jnp.float32) + branch).astype(jnp.bfloat16)

    result = lax.map(group_step, grouped)
    return result.reshape((members_here,) + result.shape[2:])


def region_transform(
    drawn_entries,
    cells,
    counts,
    values,
    variances,
    radius_cells,
    band_first,
    patch_fourth,
    rows_dev,
    lon_total,
    quart_width,
    ns_iters,
):
    members = drawn_entries.shape[1]
    slots = drawn_entries.shape[2]
    live = jnp.arange(slots, dtype=jnp.int32)[None, :] < counts[:, None]
    band_ids = band_first + jnp.arange(3, dtype=jnp.int32)
    lat_obs = (band_ids[:, None] * rows_dev + cells // lon_total).astype(drawn_entries.dtype)
    lon_obs = (cells % lon_total).astype(drawn_entries.dtype)
    center_lat = ((band_first + 1) * rows_dev).astype(drawn_entries.dtype) + (rows_dev - 1) / 2.0
    center_lon = (patch_fourth * quart_width).astype(drawn_entries.dtype) + (quart_width - 1) / 2.0
    lat_gap = lat_obs - center_lat
    lon_gap = jnp.abs(lon_obs - center_lon)
    lon_gap = jnp.minimum(lon_gap, lon_total - lon_gap)
    spread = radius_cells.astype(drawn_entries.dtype)
    weight = jnp.where(
        live,
        jnp.exp(-(lat_gap * lat_gap + lon_gap * lon_gap) / (2.0 * spread * spread)) / variances,
        0.0,
    )
    mean_obs = jnp.mean(drawn_entries, axis=1)
    perturb = drawn_entries - mean_obs[:, None, :]
    innov = values - mean_obs
    flat_pert = jnp.transpose(perturb, (1, 0, 2)).reshape(members, 3 * slots)
    flat_weight = weight.reshape(-1)
    flat_innov = innov.reshape(-1)
    identity = jnp.eye(members, dtype=drawn_entries.dtype)
    gram_matrix = (
        jnp.dot(flat_pert * flat_weight[None, :], flat_pert.T, precision=lax.Precision.HIGHEST)
        + (members - 1.0) * identity
    )
    norm_scale = jnp.sqrt(jnp.sum(gram_matrix * gram_matrix))
    scaled = gram_matrix / norm_scale

    def newton_step(step_index, carry):
        root_part, inv_part = carry
        middle = 1.5 * identity - 0.5 * jnp.dot(
            inv_part, root_part, precision=lax.Precision.HIGHEST
        )
        return (
            jnp.dot(root_part, middle, precision=lax.Precision.HIGHEST),
            jnp.dot(middle, inv_part, precision=lax.Precision.HIGHEST),
        )

    root_part, inv_part = lax.fori_loop(0, ns_iters, newton_step, (scaled, identity))
    inverse = jnp.dot(inv_part, inv_part, precision=lax.Precision.HIGHEST) / norm_scale
    projected = jnp.dot(flat_pert, flat_weight * flat_innov, precision=lax.Precision.HIGHEST)
    mean_shift = jnp.dot(inverse, projected, precision=lax.Precision.HIGHEST)
    return jnp.sqrt(members - 1.0) * inv_part / jnp.sqrt(norm_scale) + mean_shift[:, None]


def body(
    prior_sample_set,
    kernel_in,
    bias_in,
    kernel_out,
    observed_cell,
    sensor_position_variable,
    observed_count,
    observed_value,
    error_variance,
    radius,
):
    parallel_strip = lax.axis_index("reg")
    patch_fourth = lax.axis_index("mem")
    rows_here = prior_sample_set.shape[2]
    lon_total = prior_sample_set.shape[3]
    current = prior_sample_set
    for layer_index in range(NBLK):
        padded = padded_2(current, (("reg", 2),), 1)
        current = apply_block(
            padded, kernel_in[layer_index], bias_in[layer_index], kernel_out[layer_index]
        )
    members_here = current.shape[0]
    fields = current.shape[1]
    field_row = lax.dynamic_slice_in_dim(sensor_position_variable, parallel_strip, 1, 0)[0]
    cell_row = lax.dynamic_slice_in_dim(observed_cell, parallel_strip, 1, 0)[0]
    flat_state = current.reshape(members_here, fields * rows_here * lon_total)
    positions = field_row * (rows_here * lon_total) + cell_row
    picked = jnp.take(flat_state, positions, axis=1)
    every_member = lax.all_gather(picked[None], "mem", axis=1, tiled=True)
    three_bands = padded_2(every_member, (("reg", 0),), 1)
    cells_pad = jnp.pad(observed_cell, ((1, 1), (0, 0)))
    counts_pad = jnp.pad(observed_count, ((1, 1),))
    values_pad = jnp.pad(observed_value, ((1, 1), (0, 0)))
    variance_pad = jnp.pad(error_variance, ((1, 1), (0, 0)), constant_values=1.0)
    quart_width = lon_total // lax.axis_size("mem")
    weights_matrix = region_transform(
        three_bands.astype(jnp.float32),
        lax.dynamic_slice_in_dim(cells_pad, parallel_strip, 3, 0),
        lax.dynamic_slice_in_dim(counts_pad, parallel_strip, 3, 0),
        lax.dynamic_slice_in_dim(values_pad, parallel_strip, 3, 0),
        lax.dynamic_slice_in_dim(variance_pad, parallel_strip, 3, 0),
        lax.dynamic_slice_in_dim(radius, parallel_strip, 1, 0)[0],
        parallel_strip - 1,
        patch_fourth,
        rows_here,
        lon_total,
        quart_width,
        NS_ITERS,
    )
    region_part = lax.all_to_all(current, "mem", split_axis=3, concat_axis=0, tiled=True)
    shape_here = region_part.shape
    flat_part = region_part.reshape(
        shape_here[0], shape_here[1] * shape_here[2] * shape_here[3]
    ).astype(jnp.float32)
    mean_state = jnp.mean(flat_part, axis=0)
    anomalies = flat_part - mean_state[None]
    mixed = lax.dot_general(
        weights_matrix, anomalies, (((0,), (0,)), ((), ())), precision=lax.Precision.HIGHEST
    )
    updated = (mean_state[None] + mixed).astype(jnp.bfloat16)
    return updated.reshape(shape_here)


def solution(mesh):
    return jax.shard_map(
        body,
        mesh=mesh,
        in_specs=(P("mem", None, "reg", None), P(), P(), P(), P(), P(), P(), P(), P(), P()),
        out_specs=P(None, None, "reg", "mem"),
        check_vma=False,
    )
```

profile of v0, /device:TPU:2, one launch (start us, length us, event | category | flops | bytes accessed | tf_op | source)
XLA Modules:
  0.0 568.2 jit_solution(17400211164863477808)
XLA Ops:
  0.0 7.1 %fusion.116 = (bf16[32,69,1,256]{3,2,1,0:T(2,128)(2,1)S(1)}, bf16[32,69,1,256]{3,2,1,0:T(2,128)(2,1)S(1)}) fusion(bf16[32,69,4,256]{3,2,1,0:T(4,128)(2,1)} %param.16), kind=kLoop, calls=%fused_computation.158 | loop fusion | bytes 4521984 | tf_op jit(solution)/shard_map/slice | solution.py:18
  10.6 3.6 collective-permute-start.1
  16.2 8.2 %collective-permute-done = bf16[32,69,1,256]{3,0,2,1:T(8,128)(2,1)S(1)} collective-permute-done((bf16[32,69,1,256]{3,0,2,1:T(8,128)(2,1)S(1)}, bf16[32,69,1,256]{3,0,2,1:T(8,128)(2,1)S(1)}, u32[]{:S(2)}, u32[]{:S(2)}) %collective-permute-start) | collective-permute-done | bytes 1130528 | tf_op jit(solution)/shard_map/ppermute | solution.py:17
  26.2 9.5 %collective-permute-done.1 = bf16[32,69,1,256]{3,0,2,1:T(8,128)(2,1)} collective-permute-done((bf16[32,69,1,256]{3,0,2,1:T(8,128)(2,1)}, bf16[32,69,1,256]{3,0,2,1:T(8,128)(2,1)}, u32[]{:S(2)}, u32[]{:S(2)}) %collective-permute-start.1) | collective-permute-done | bytes 1130528 | tf_op jit(solution)/shard_map/ppermute | solution.py:20
  38.6 9.3 %pad_maximum_fusion.10 = bf16[32,69,6,256]{3,2,1,0:T(8,128)(2,1)S(1)} fusion(bf16[32,69,1,256]{3,2,1,0:T(2,128)(2,1)S(1)} %copy.136, bf16[32,69,4,256]{3,2,1,0:T(4,128)(2,1)} %param.16, bf16[32,69,1,256]{3,2,1,0:T(2,128)(2,1)S(1)} %copy.135), kind=kLoop, calls=%fused_computation.78 | loop fusion | flops 20348928 | bytes 13565952 | tf_op jit(solution)/shard_map/concatenate | solution.py:21
  47.9 4.9 copy.137
  55.5 76.3 %while.33 = (s32[]{:T(128)}, bf16[4,8,69,4,256]{4,2,3,1,0:T(8,128)(2,1)}, bf16[4,8,69,6,256]{4,2,3,1,0:T(8,128)(2,1)}, bf16[9,128,69]{1,2,0:T(8,128)(2,1)}, f32[...) while((s32[]{:T(128)}, bf16[4,8,69,4,256]{4,2,3,1,0:T(8,128)(2,1)}, ...), condition=%wide.region_1.2_spmd, body=%wide.region_0.1_spmd.sunk | while | flops 1513881600 | bytes 67979424 | solution.py:53
  63.3 3.4 fusion.163
  66.7 7.8 %fusion.165 = bf16[4,8,69,4,256]{4,2,3,1,0:T(8,128)(2,1)} fusion(bf16[4,8,69,4,256]{4,2,3,1,0:T(8,128)(2,1)} %get-tuple-element.322, s32[]{:T(128)} %get-tuple-element.321, f32[8,4,256,128,1]{3,2,4,1,0:T(8,128)} %fusion.163, f32[8,4,256,128,1]{3,2,4,1,0:T(8,128)} %fusion.164, f32[128]{0:T(128)S(1)} %bitcast.336, ...), kind=kOutput, calls=%fused_computation.23.clone.1 | convolution fusion | flops 608354304 | bytes 16008192 | tf_op jit(solution)/shard_map/while/body/eval_jaxpr/ghpl,fh->gfpl/dot_general | solution.py:48
  79.1 3.3 fusion.164
  82.4 3.4 fusion.163
  85.8 7.8 %fusion.165 = bf16[4,8,69,4,256]{4,2,3,1,0:T(8,128)(2,1)} fusion(bf16[4,8,69,4,256]{4,2,3,1,0:T(8,128)(2,1)} %get-tuple-element.322, s32[]{:T(128)} %get-tuple-element.321, f32[8,4,256,128,1]{3,2,4,1,0:T(8,128)} %fusion.163, f32[8,4,256,128,1]{3,2,4,1,0:T(8,128)} %fusion.164, f32[128]{0:T(128)S(1)} %bitcast.336, ...), kind=kOutput, calls=%fused_computation.23.clone.1 | convolution fusion | flops 608354304 | bytes 16008192 | tf_op jit(solution)/shard_map/while/body/eval_jaxpr/ghpl,fh->gfpl/dot_general | solution.py:48
  101.4 3.4 fusion.163
  104.8 7.8 %fusion.165 = bf16[4,8,69,4,256]{4,2,3,1,0:T(8,128)(2,1)} fusion(bf16[4,8,69,4,256]{4,2,3,1,0:T(8,128)(2,1)} %get-tuple-element.322, s32[]{:T(128)} %get-tuple-element.321, f32[8,4,256,128,1]{3,2,4,1,0:T(8,128)} %fusion.163, f32[8,4,256,128,1]{3,2,4,1,0:T(8,128)} %fusion.164, f32[128]{0:T(128)S(1)} %bitcast.336, ...), kind=kOutput, calls=%fused_computation.23.clone.1 | convolution fusion | flops 608354304 | bytes 16008192 | tf_op jit(solution)/shard_map/while/body/eval_jaxpr/ghpl,fh->gfpl/dot_general | solution.py:48
  120.5 3.4 fusion.163
  123.9 7.8 %fusion.165 = bf16[4,8,69,4,256]{4,2,3,1,0:T(8,128)(2,1)} fusion(bf16[4,8,69,4,256]{4,2,3,1,0:T(8,128)(2,1)} %get-tuple-element.322, s32[]{:T(128)} %get-tuple-element.321, f32[8,4,256,128,1]{3,2,4,1,0:T(8,128)} %fusion.163, f32[8,4,256,128,1]{3,2,4,1,0:T(8,128)} %fusion.164, f32[128]{0:T(128)S(1)} %bitcast.336, ...), kind=kOutput, calls=%fused_computation.23.clone.1 | convolution fusion | flops 608354304 | bytes 16008192 | tf_op jit(solution)/shard_map/while/body/eval_jaxpr/ghpl,fh->gfpl/dot_general | solution.py:48
  131.8 4.9 copy.189
  137.0 3.7 collective-permute-start.2
  142.7 11.5 %collective-permute-done.2 = bf16[32,69,1,256]{3,0,2,1:T(8,128)(2,1)} collective-permute-done((bf16[32,69,1,256]{3,0,2,1:T(8,128)(2,1)S(1)}, bf16[32,69,1,256]{3,0,2,1:T(8,128)(2,1)}, u32[]{:S(2)}, u32[]{:S(2)}) %collective-permute-start.2) | collective-permute-done | bytes 1130528 | tf_op jit(solution)/shard_map/ppermute | solution.py:17
  156.1 9.1 %collective-permute-done.3 = bf16[32,69,1,256]{3,0,2,1:T(8,128)(2,1)S(1)} collective-permute-done((bf16[32,69,1,256]{3,0,2,1:T(8,128)(2,1)S(1)}, bf16[32,69,1,256]{3,0,2,1:T(8,128)(2,1)S(1)}, u32[]{:S(2)}, u32[]{:S(2)}) %collective-permute-start.3) | collective-permute-done | bytes 1130528 | tf_op jit(solution)/shard_map/ppermute | solution.py:20
  165.9 5.9 %pad_maximum_fusion.11 = bf16[4,8,69,6,256]{4,2,3,1,0:T(8,128)(2,1)} fusion(bf16[4,8,69,1,256]{4,2,3,1,0:T(8,128)(2,1)S(1)} %copy.142, bf16[4,8,69,4,256]{4,2,3,1,0:T(8,128)(2,1)} %get-tuple-element.91, bf16[4,8,69,1,256]{4,2,3,1,0:T(8,128)(2,1)S(1)} %copy.141), kind=kLoop, calls=%fused_computation.80 | loop fusion | flops 6782976 | bytes 13565952 | tf_op jit(solution)/shard_map/concatenate | solution.py:21
  174.5 76.2 %while.34 = (s32[]{:T(128)}, bf16[4,8,69,4,256]{4,2,3,1,0:T(8,128)(2,1)}, bf16[4,8,69,6,256]{4,2,3,1,0:T(8,128)(2,1)}, bf16[9,128,69]{1,2,0:T(8,128)(2,1)}, f32[...) while((s32[]{:T(128)}, bf16[4,8,69,4,256]{4,2,3,1,0:T(8,128)(2,1)}, ...), condition=%wide.region_3.4_spmd, body=%wide.region_2.3_spmd.sunk | while | flops 1513881600 | bytes 67979424 | solution.py:53
  182.3 3.4 fusion.172
  185.7 7.8 %fusion.174 = bf16[4,8,69,4,256]{4,2,3,1,0:T(8,128)(2,1)} fusion(bf16[4,8,69,4,256]{4,2,3,1,0:T(8,128)(2,1)} %get-tuple-element.343, s32[]{:T(128)} %get-tuple-element.342, f32[8,4,256,128,1]{3,2,4,1,0:T(8,128)} %fusion.172, f32[8,4,256,128,1]{3,2,4,1,0:T(8,128)} %fusion.173, f32[128]{0:T(128)S(1)} %bitcast.335, ...), kind=kOutput, calls=%fused_computation.58.clone.1 | convolution fusion | flops 608354304 | bytes 16008192 | tf_op jit(solution)/shard_map/while/body/eval_jaxpr/ghpl,fh->gfpl/dot_general | solution.py:48
  198.1 3.3 fusion.173
  201.4 3.4 fusion.172
  204.8 7.8 %fusion.174 = bf16[4,8,69,4,256]{4,2,3,1,0:T(8,128)(2,1)} fusion(bf16[4,8,69,4,256]{4,2,3,1,0:T(8,128)(2,1)} %get-tuple-element.343, s32[]{:T(128)} %get-tuple-element.342, f32[8,4,256,128,1]{3,2,4,1,0:T(8,128)} %fusion.172, f32[8,4,256,128,1]{3,2,4,1,0:T(8,128)} %fusion.173, f32[128]{0:T(128)S(1)} %bitcast.335, ...), kind=kOutput, calls=%fused_computation.58.clone.1 | convolution fusion | flops 608354304 | bytes 16008192 | tf_op jit(solution)/shard_map/while/body/eval_jaxpr/ghpl,fh->gfpl/dot_general | solution.py:48
  217.1 3.3 fusion.173
  220.5 3.4 fusion.172
  223.9 7.8 %fusion.174 = bf16[4,8,69,4,256]{4,2,3,1,0:T(8,128)(2,1)} fusion(bf16[4,8,69,4,256]{4,2,3,1,0:T(8,128)(2,1)} %get-tuple-element.343, s32[]{:T(128)} %get-tuple-element.342, f32[8,4,256,128,1]{3,2,4,1,0:T(8,128)} %fusion.172, f32[8,4,256,128,1]{3,2,4,1,0:T(8,128)} %fusion.173, f32[128]{0:T(128)S(1)} %bitcast.335, ...), kind=kOutput, calls=%fused_computation.58.clone.1 | convolution fusion | flops 608354304 | bytes 16008192 | tf_op jit(solution)/shard_map/while/body/eval_jaxpr/ghpl,fh->gfpl/dot_general | solution.py:48
  239.5 3.4 fusion.172
  242.9 7.8 %fusion.174 = bf16[4,8,69,4,256]{4,2,3,1,0:T(8,128)(2,1)} fusion(bf16[4,8,69,4,256]{4,2,3,1,0:T(8,128)(2,1)} %get-tuple-element.343, s32[]{:T(128)} %get-tuple-element.342, f32[8,4,256,128,1]{3,2,4,1,0:T(8,128)} %fusion.172, f32[8,4,256,128,1]{3,2,4,1,0:T(8,128)} %fusion.173, f32[128]{0:T(128)S(1)} %bitcast.335, ...), kind=kOutput, calls=%fused_computation.58.clone.1 | convolution fusion | flops 608354304 | bytes 16008192 | tf_op jit(solution)/shard_map/while/body/eval_jaxpr/ghpl,fh->gfpl/dot_general | solution.py:48
  250.7 14.1 %copy.146 = bf16[32,69,4,256]{1,0,2,3:T(8,128)(2,1)} copy(bf16[32,69,4,256]{3,1,2,0:T(8,128)(2,1)} %bitcast.329) | data formatting | bytes 9043968 | tf_op jit(solution)/shard_map/reshape | solution.py:54
  264.8 6.0 %all-to-all-start = ((bf16[32,69,4,256]{1,0,2,3:T(8,128)(2,1)}), bf16[32,69,4,256]{1,0,2,3:T(8,128)(2,1)}, u32[]{:S(2)}, u32[]{:S(2)}) async-start(bf16[32,69,4,256]{1,0,2,3:T(8,128)(2,1)} %copy.146), calls=%async_computation | async-start | bytes 16777216 | tf_op jit(solution)/shard_map/all_to_all | solution.py:169
  271.6 6.2 %copy.151 = bf16[4,8,69,4,256]{4,3,2,1,0:T(4,128)(2,1)} copy(bf16[4,8,69,4,256]{4,2,3,1,0:T(8,128)(2,1)} %get-tuple-element.92) | data formatting | bytes 9043968 | tf_op jit(solution)/shard_map/while | solution.py:53
  277.8 6.7 %reshape_reshape.3 = bf16[32,70656]{1,0:T(8,128)(2,1)} reshape(bf16[4,8,69,4,256]{4,3,2,1,0:T(4,128)(2,1)} %copy.151) | data formatting | bytes 9043968 | tf_op jit(solution)/shard_map/reshape;reshape | solution.py:145
  284.5 14.5 %copy.152 = bf16[32,70656]{0,1:T(8,128)(2,1)} copy(bf16[32,70656]{1,0:T(8,128)(2,1)} %reshape_reshape.3) | data formatting | bytes 9043968 | tf_op jit(solution)/shard_map/reshape;reshape | solution.py:145
  298.9 11.3 %gather_fusion = bf16[1024,32]{1,0:T(8,128)(2,1)S(1)} fusion(bf16[32,70656]{0,1:T(8,128)(2,1)} %copy.152, s32[1024]{0:T(1024)S(1)} %broadcast_clamp_fusion), kind=kCustom, calls=%fused_computation | custom fusion | bytes 135168 | tf_op jit(solution)/shard_map/jit(_take)/gather | solution.py:147
  310.6 150.4 %all_gather.3 = bf16[1,128,1024]{2,1,0:T(8,128)(2,1)S(1)} all-gather(bf16[1,32,1024]{2,1,0:T(8,128)(2,1)S(1)} %copy.153), channel_id=1, replica_groups=mesh['mem'=4,'reg'=8] {'mem'}, dimensions={1}, use_global_device_ids=true | all-gather | bytes 327680 | tf_op jit(solution)/shard_map/all_gather | solution.py:148
  463.0 3.6 collective-permute-start.5
  475.3 3.5 while.35
  479.2 14.5 %copy.147 = bf16[32,69,4,256]{3,0,2,1:T(8,128)(2,1)} copy(bf16[32,69,4,256]{1,0,2,3:T(8,128)(2,1)} %all-to-all-done) | data formatting | bytes 9043968 | tf_op jit(solution)/shard_map/all_to_all | solution.py:169
  493.7 14.6 %reshape.136 = f32[32,69,4,4,64]{4,3,0,2,1:T(4,128)} reshape(bf16[32,69,4,256]{3,0,2,1:T(8,128)(2,1)} %copy.147) | data formatting | bytes 13565952 | tf_op jit(solution)/shard_map/convert_element_type | solution.py:173
  508.3 4.4 convert_reduce_fusion
  512.7 19.0 %copy.155 = f32[4,32,69,4,64]{4,3,2,1,0:T(4,128)} copy(f32[4,32,69,4,64]{4,0,1,3,2:T(4,128)} %bitcast.328) | data formatting | bytes 18087936 | tf_op jit(solution)/shard_map/convert_element_type | solution.py:173
  531.7 15.8 %reshape.135 = f32[128,17664]{1,0:T(8,128)} reshape(f32[4,32,69,4,64]{4,3,2,1,0:T(4,128)} %copy.155) | data formatting | bytes 18087936 | tf_op jit(solution)/shard_map/convert_element_type | solution.py:173
  548.5 12.7 %fusion.59 = bf16[128,17664]{1,0:T(8,128)(2,1)} fusion(f32[128,17664]{1,0:T(8,128)} %reshape.135, f32[17664]{0:T(1024)S(1)} %div.53, f32[128,128]{1,0:T(8,128)S(1)} %get-tuple-element.93, f32[128]{0:T(128)S(1)} %convolution_bitcast_fusion.1, f32[]{:T(128)S(6)} %sqrt.7), kind=kOutput, calls=%fused_computation.77 | convolution fusion | flops 3479715840 | bytes 13702660 | tf_op jit(solution)/shard_map/dot_general | solution.py:176
  561.2 6.5 %copy.156 = bf16[128,17664]{0,1:T(8,128)(2,1)} copy(bf16[128,17664]{1,0:T(8,128)(2,1)} %fusion.59) | data formatting | bytes 9043968 | tf_op jit(solution)/shard_map/convert_element_type | solution.py:179
  (164 shorter events, 87.3 us)
Async XLA Ops:
  7.1 7.1 %copy-start.11 = (f32[2,128]{1,0:T(2,128)S(1)}, f32[2,128]{1,0:T(2,128)}, u32[]{:S(2)}) copy-start(f32[2,128]{1,0:T(2,128)} %param.18) | copy-start | bytes 3076
  7.1 7.1 %copy-start.7 = (bf16[2,69,128]{2,0,1:T(2,128)(2,1)S(1)}, bf16[2,69,128]{2,0,1:T(2,128)(2,1)}, u32[]{:S(2)}) copy-start(bf16[2,69,128]{2,0,1:T(2,128)(2,1)} %param.19) | copy-start | bytes 105988
  7.2 7.8 %copy-start.4 = (bf16[2,9,128,69]{2,0,3,1:T(2,128)(2,1)S(1)}, bf16[2,9,128,69]{2,0,3,1:T(2,128)(2,1)}, u32[]{:S(2)}) copy-start(bf16[2,9,128,69]{2,0,3,1:T(2,128)(2,1)} %param.17) | copy-start | bytes 953860
  7.4 17.0 %collective-permute-start = (bf16[32,69,1,256]{3,0,2,1:T(8,128)(2,1)S(1)}, bf16[32,69,1,256]{3,0,2,1:T(8,128)(2,1)S(1)}, u32[]{:S(2)}, u32[]{:S(2)}) collective-permute-start(bf16[32,69,1,256]{3,0,2,1:T(8,128)(2,1)S(1)} %copy.176), channel_id=1, source_target_pairs={{0,1},{1,2},{2,3},{3,4},{4,5},{5,6},{6,7},{8,9},{9,10},{10,11},{11... | collective-permute-start | bytes 3391496 | tf_op jit(solution)/shard_map/ppermute | solution.py:17
  10.6 25.0 %collective-permute-start.1 = (bf16[32,69,1,256]{3,0,2,1:T(8,128)(2,1)}, bf16[32,69,1,256]{3,0,2,1:T(8,128)(2,1)}, u32[]{:S(2)}, u32[]{:S(2)}) collective-permute-start(bf16[32,69,1,256]{3,0,2,1:T(8,128)(2,1)} %copy.177), channel_id=1, source_target_pairs={{1,0},{2,1},{3,2},{4,3},{5,4},{6,5},{7,6},{9,8},{10,9},{11,10},{12... | collective-permute-start | bytes 3391496 | tf_op jit(solution)/shard_map/ppermute | solution.py:20
  58.5 1.5 copy-start.6
  60.0 3.4 copy-start
  60.0 3.3 copy-start.1
  77.6 1.5 copy-start.6
  79.0 3.4 copy-start
  79.0 3.3 copy-start.1
  96.6 1.5 copy-start.6
  98.1 3.4 copy-start
  98.1 3.3 copy-start.1
  115.6 1.5 copy-start.6
  117.1 3.4 copy-start
  117.1 3.3 copy-start.1
  137.0 17.3 %collective-permute-start.2 = (bf16[32,69,1,256]{3,0,2,1:T(8,128)(2,1)S(1)}, bf16[32,69,1,256]{3,0,2,1:T(8,128)(2,1)}, u32[]{:S(2)}, u32[]{:S(2)}) collective-permute-start(bf16[32,69,1,256]{3,0,2,1:T(8,128)(2,1)S(1)} %get-tuple-element.170), channel_id=1, source_target_pairs={{0,1},{1,2},{2,3},{3,4},{4,5},{5,6},{6,7},{8,9},{9,10},{10,11},{11... | collective-permute-start | bytes 3391496 | tf_op jit(solution)/shard_map/ppermute | solution.py:17
  140.7 24.6 %collective-permute-start.3 = (bf16[32,69,1,256]{3,0,2,1:T(8,128)(2,1)S(1)}, bf16[32,69,1,256]{3,0,2,1:T(8,128)(2,1)S(1)}, u32[]{:S(2)}, u32[]{:S(2)}) collective-permute-start(bf16[32,69,1,256]{3,0,2,1:T(8,128)(2,1)S(1)} %get-tuple-element.171), channel_id=1, source_target_pairs={{1,0},{2,1},{3,2},{4,3},{5,4},{6,5},{7,6},{9,8},{10,9},{11,10},{12... | collective-permute-start | bytes 3391496 | tf_op jit(solution)/shard_map/ppermute | solution.py:20
  177.5 1.5 copy-start.5
  179.0 3.4 copy-start.2
  179.0 3.3 copy-start.3
  196.6 1.5 copy-start.5
  198.1 3.4 copy-start.2
  198.1 3.3 copy-start.3
  215.6 1.5 copy-start.5
  217.1 3.4 copy-start.2
  217.1 3.4 copy-start.3
  234.7 1.5 copy-start.5
  236.2 3.4 copy-start.2
  236.2 3.3 copy-start.3
  264.8 6.0 %copy-start.8 = (s32[8,1024]{1,0:T(8,128)S(1)}, s32[8,1024]{1,0:T(8,128)}, u32[]{:S(2)}) copy-start(s32[8,1024]{1,0:T(8,128)} %param.20) | copy-start | bytes 98308
  264.8 214.4 %all-to-all-start = ((bf16[32,69,4,256]{1,0,2,3:T(8,128)(2,1)}), bf16[32,69,4,256]{1,0,2,3:T(8,128)(2,1)}, u32[]{:S(2)}, u32[]{:S(2)}) async-start(bf16[32,69,4,256]{1,0,2,3:T(8,128)(2,1)} %copy.146), calls=%async_computation | async-start | bytes 16777216 | tf_op jit(solution)/shard_map/all_to_all | solution.py:169
  284.5 182.2 %copy-start.13 = (s32[8]{0:T(128)S(1)}, s32[8]{0:T(128)}, u32[]{:S(2)}) copy-start(s32[8]{0:T(128)} %param.25) | copy-start | bytes 100
  284.5 183.4 %copy-start.12 = (s32[8]{0:T(128)S(1)}, s32[8]{0:T(128)}, u32[]{:S(2)}) copy-start(s32[8]{0:T(128)} %param.22) | copy-start | bytes 100
  284.5 186.2 %copy-start.9 = (f32[8,1024]{1,0:T(8,128)S(1)}, f32[8,1024]{1,0:T(8,128)}, u32[]{:S(2)}) copy-start(f32[8,1024]{1,0:T(8,128)} %param.23) | copy-start | bytes 98308
  284.5 186.2 %copy-start.10 = (f32[8,1024]{1,0:T(8,128)S(1)}, f32[8,1024]{1,0:T(8,128)}, u32[]{:S(2)}) copy-start(f32[8,1024]{1,0:T(8,128)} %param.24) | copy-start | bytes 98308
  461.1 7.7 %collective-permute-start.4 = (bf16[1,128,1024]{2,1,0:T(8,128)(2,1)S(1)}, bf16[1,128,1024]{2,1,0:T(8,128)(2,1)S(1)}, u32[]{:S(2)}, u32[]{:S(2)}) collective-permute-start(bf16[1,128,1024]{2,1,0:T(8,128)(2,1)S(1)} %all_gather.3), channel_id=1, source_target_pairs={{0,1},{1,2},{2,3},{3,4},{4,5},{5,6},{6,7},{8,9},{9,10},{10,11},{11... | collective-permute-start | bytes 786440 | tf_op jit(solution)/shard_map/ppermute | solution.py:17
  463.0 7.5 %collective-permute-start.5 = (bf16[1,128,1024]{2,1,0:T(8,128)(2,1)S(1)}, bf16[1,128,1024]{2,1,0:T(8,128)(2,1)S(1)}, u32[]{:S(2)}, u32[]{:S(2)}) collective-permute-start(bf16[1,128,1024]{2,1,0:T(8,128)(2,1)S(1)} %all_gather.3), channel_id=1, source_target_pairs={{1,0},{2,1},{3,2},{4,3},{5,4},{6,5},{7,6},{9,8},{10,9},{11,10},{12... | collective-permute-start | bytes 786440 | tf_op jit(solution)/shard_map/ppermute | solution.py:20
where the time goes:
time: 578 us; the launch traced here: 568 us
  local copies, waits for them, and re-layouts  182 us (31%)
  blocking collectives  150 us (26%)
  matrix products  136 us (24%)
  waiting for transfers between devices  40.8 us (7%)
  other arithmetic  33 us (6%)
  starting transfers between devices  22.8 us (4%)
    all_gather x1, blocking collectives, body(): every_member = lax.all_gather(picked[None], 'mem', axis=1, tiled=True)  150 us
    dot_general x8, matrix products, group_step(): jnp.einsum('ghpl,fh->gfpl', hidden, kernel_back, preferred_element_type=j...  62.5 us
    dot_general x16, matrix products, group_step(): jnp.einsum('gcfpl,chf->ghpl', window, taps, preferred_element_type=jnp.fl...  53.7 us
    convert_element_type x3, local copies, waits for them, and re-layouts, body(): flat_part = region_part.reshape(shape_here[0], shape_here[1] * shape_here...  49.4 us
    another operation x2, local copies, waits for them, and re-layouts, body(): flat_state = current.reshape(members_here, fields * rows_here * lon_total)  21.2 us
    ppermute x3, waiting for transfers between devices, padded_2(): lax.ppermute(lax.slice_in_dim(block, block.shape[dim] - width, None, axis...  20.5 us
    ppermute x3, waiting for transfers between devices, padded_2(): lax.ppermute(lax.slice_in_dim(block, 0, width, axis=dim), axis, backward)  20.4 us
    concatenate x2, other arithmetic, padded_2(): block = jnp.concatenate([low, block, high], axis=dim)  15.2 us
  transfers between devices with their start and end apart: 7, of which 6 were waited for; matrix products, arithmetic and copies ran while one was open for 10% of the time, Pallas kernels for 0%

commit v1 on v0

v1 whole, which is shorter than its diff:
```python
import jax
import jax.numpy as jnp
from jax import lax
from jax.experimental import pallas as pl
from jax.experimental.pallas import tpu as pltpu
from jax.sharding import PartitionSpec as P

NBLK = 2
NS_ITERS = 4
CHUNKS = 2
FPAD = 72
STEP = 2
VMEM = 48 * 1024 * 1024


def shift_lists(axis):
    count = lax.axis_size(axis)
    forward = [(i, i + 1) for i in range(count - 1)]
    backward = [(target, source) for source, target in forward]
    return forward, backward


def conv_rows(rows, mix, bias, back):
    stacks = [
        jnp.concatenate(
            [pltpu.roll(row, 1, 1), row, pltpu.roll(row, row.shape[1] - 1, 1)], axis=0
        ).astype(jnp.bfloat16)
        for row in rows
    ]
    height = len(rows) - 2
    hid = bias.shape[0]
    sums = [bias for _ in range(height)]
    for s, stack in enumerate(stacks):
        taps = [p for p in range(3) if 0 <= s - p < height]
        part = jnp.dot(
            mix[taps[0] * hid : (taps[-1] + 1) * hid],
            stack,
            preferred_element_type=jnp.float32,
        )
        for n, p in enumerate(taps):
            sums[s - p] = sums[s - p] + part[n * hid : (n + 1) * hid]
    results = []
    for i in range(height):
        hidden = jax.nn.gelu(sums[i]).astype(jnp.bfloat16)
        results.append(rows[i + 1] + jnp.dot(back, hidden, preferred_element_type=jnp.float32))
    return results


def first_kernel(x_ref, low_ref, high_ref, mix_ref, bias_ref, back_ref, y_ref, top_ref, bot_ref, scr):
    fields, height = x_ref.shape[1], x_ref.shape[2]
    scr[...] = jnp.zeros_like(scr)
    for u in range(x_ref.shape[0]):
        x = x_ref[u].astype(jnp.float32)
        scr[u, 0, 0:fields, :] = low_ref[u].astype(jnp.float32)
        scr[u, height + 1, 0:fields, :] = high_ref[u].astype(jnp.float32)
        for p in range(height):
            scr[u, p + 1, 0:fields, :] = x[:, p, :]
    for u in range(x_ref.shape[0]):
        rows = [scr[u, s] for s in range(height + 2)]
        out = conv_rows(rows, mix_ref[...], bias_ref[...], back_ref[...])
        for p in range(height):
            y_ref[u, p] = out[p].astype(jnp.bfloat16)
        top_ref[u] = out[0].astype(jnp.bfloat16)
        bot_ref[u] = out[height - 1].astype(jnp.bfloat16)


def second_kernel(y_ref, low_ref, high_ref, mix_ref, bias_ref, back_ref, z_ref, scr):
    height = y_ref.shape[1]
    group, fields = z_ref.shape[3], z_ref.shape[1]
    step = pl.program_id(0)
    for u in range(y_ref.shape[0]):
        rows = [low_ref[u]] + [y_ref[u, p] for p in range(height)] + [high_ref[u]]
        rows = [row.astype(jnp.float32) for row in rows]
        out = conv_rows(rows, mix_ref[...], bias_ref[...], back_ref[...])
        member = step * y_ref.shape[0] + u
        for p in range(height):
            for h in range(2):
                scr[p, h, pl.ds(member, FPAD, stride=group), :] = out[p][:, h * 128 : (h + 1) * 128]

    @pl.when(step == pl.num_programs(0) - 1)
    def _():
        span = (fields // 3) * group
        keep = lax.broadcasted_iota(jnp.int32, (span, 128), 1) < 64
        for part in range(3):
            for pp in range(height // 2):
                for h in range(2):
                    a = scr[2 * pp, h, pl.ds(part * span, span), :]
                    b = scr[2 * pp + 1, h, pl.ds(part * span, span), :]
                    even = jnp.where(keep, a, pltpu.roll(b, 64, 1)).astype(jnp.bfloat16)
                    odd = jnp.where(keep, pltpu.roll(a, 64, 1), b).astype(jnp.bfloat16)
                    rows = pl.ds(part * (fields // 3), fields // 3)
                    z_ref[2 * h, rows, pp] = even.reshape(fields // 3, group, 128)
                    z_ref[2 * h + 1, rows, pp] = odd.reshape(fields // 3, group, 128)


def sample_kernel(z_ref, cell_ref, field_ref, out_ref, hot):
    quarters, fields, pairs, group, lanes = z_ref.shape
    slots = cell_ref.shape[1]
    cell = cell_ref[...]
    lane = lax.broadcasted_iota(jnp.int32, (lanes, slots), 0)
    for q in range(quarters):
        for pp in range(pairs):
            here = (2 * pp + lane // 64) * 256 + q * 64 + lane % 64
            hot[pl.ds((q * pairs + pp) * lanes, lanes), :] = jnp.where(here == cell, 1.0, 0.0).astype(
                jnp.bfloat16
            )
    wanted = field_ref[...]
    block = fields // 3

    def part(i, total):
        rows = pl.ds(i * block, block)
        left = jnp.concatenate(
            [
                z_ref[q, rows, pp].reshape(block * group, lanes)
                for q in range(quarters)
                for pp in range(pairs)
            ],
            axis=1,
        )
        for n in range(slots // 256):
            cols = slice(n * 256, (n + 1) * 256)
            found = jnp.dot(left, hot[:, cols], preferred_element_type=jnp.float32)
            piece = total[n]
            for f in range(block):
                piece = jnp.where(
                    wanted[:, cols] == i * block + f, found[f * group : (f + 1) * group], piece
                )
            total = total[:n] + (piece,) + total[n + 1 :]
        return total

    zero = tuple(jnp.zeros((group, 256), jnp.float32) for _ in range(slots // 256))
    total = lax.fori_loop(0, 3, part, zero)
    for n in range(slots // 256):
        out_ref[:, n * 256 : (n + 1) * 256] = total[n].astype(jnp.bfloat16)


def mix_kernel(*refs):
    parts, w_ref, out_ref = refs[:-2], refs[-2], refs[-1]
    fields, pairs = parts[0].shape[1], parts[0].shape[2]
    weights = w_ref[...]

    def one(f, carry):
        for pp in range(pairs):
            left = jnp.concatenate(
                [part[s, f, pp] for part in parts for s in range(part.shape[0])], axis=0
            )
            left = jnp.concatenate([left, left], axis=0)
            mixed = lax.dot_general(
                left, weights, (((0,), (0,)), ((), ())), preferred_element_type=jnp.float32
            ).astype(jnp.bfloat16)
            out_ref[f, 2 * pp] = mixed[:64]
            out_ref[f, 2 * pp + 1] = mixed[64:]
        return carry

    lax.fori_loop(0, fields, one, 0)


def call(kernel, grid, in_specs, out_shape, out_specs, scratch=(), flops=0, moved=0):
    return pl.pallas_call(
        kernel,
        grid=grid,
        in_specs=in_specs,
        out_shape=out_shape,
        out_specs=out_specs,
        scratch_shapes=list(scratch),
        compiler_params=pltpu.CompilerParams(vmem_limit_bytes=VMEM),
        cost_estimate=pl.CostEstimate(flops=flops, bytes_accessed=moved, transcendentals=0),
    )


def whole(shape):
    return pl.BlockSpec(shape, lambda i: (0,) * len(shape))


def region_transform(
    drawn_entries,
    cells,
    counts,
    values,
    variances,
    radius_cells,
    band_first,
    patch_fourth,
    rows_dev,
    lon_total,
    quart_width,
    ns_iters,
):
    members = drawn_entries.shape[1]
    slots = drawn_entries.shape[2]
    live = jnp.arange(slots, dtype=jnp.int32)[None, :] < counts[:, None]
    band_ids = band_first + jnp.arange(3, dtype=jnp.int32)
    lat_obs = (band_ids[:, None] * rows_dev + cells // lon_total).astype(drawn_entries.dtype)
    lon_obs = (cells % lon_total).astype(drawn_entries.dtype)
    center_lat = ((band_first + 1) * rows_dev).astype(drawn_entries.dtype) + (rows_dev - 1) / 2.0
    center_lon = (patch_fourth * quart_width).astype(drawn_entries.dtype) + (quart_width - 1) / 2.0
    lat_gap = lat_obs - center_lat
    lon_gap = jnp.abs(lon_obs - center_lon)
    lon_gap = jnp.minimum(lon_gap, lon_total - lon_gap)
    spread = radius_cells.astype(drawn_entries.dtype)
    weight = jnp.where(
        live,
        jnp.exp(-(lat_gap * lat_gap + lon_gap * lon_gap) / (2.0 * spread * spread)) / variances,
        0.0,
    )
    mean_obs = jnp.mean(drawn_entries, axis=1)
    perturb = drawn_entries - mean_obs[:, None, :]
    innov = values - mean_obs
    flat_pert = jnp.transpose(perturb, (1, 0, 2)).reshape(members, 3 * slots)
    flat_weight = weight.reshape(-1)
    flat_innov = innov.reshape(-1)
    identity = jnp.eye(members, dtype=drawn_entries.dtype)
    gram_matrix = (
        jnp.dot(flat_pert * flat_weight[None, :], flat_pert.T, precision=lax.Precision.HIGHEST)
        + (members - 1.0) * identity
    )
    norm_scale = jnp.sqrt(jnp.sum(gram_matrix * gram_matrix))
    scaled = gram_matrix / norm_scale

    def newton_step(step_index, carry):
        root_part, inv_part = carry
        middle = 1.5 * identity - 0.5 * jnp.dot(
            inv_part, root_part, precision=lax.Precision.HIGHEST
        )
        return (
            jnp.dot(root_part, middle, precision=lax.Precision.HIGHEST),
            jnp.dot(middle, inv_part, precision=lax.Precision.HIGHEST),
        )

    root_part, inv_part = lax.fori_loop(0, ns_iters, newton_step, (scaled, identity))
    inverse = jnp.dot(inv_part, inv_part, precision=lax.Precision.HIGHEST) / norm_scale
    projected = jnp.dot(flat_pert, flat_weight * flat_innov, precision=lax.Precision.HIGHEST)
    mean_shift = jnp.dot(inverse, projected, precision=lax.Precision.HIGHEST)
    return jnp.sqrt(members - 1.0) * inv_part / jnp.sqrt(norm_scale) + mean_shift[:, None]


def body(
    prior_sample_set,
    kernel_in,
    bias_in,
    kernel_out,
    observed_cell,
    sensor_position_variable,
    observed_count,
    observed_value,
    error_variance,
    radius,
):
    parallel_strip = lax.axis_index("reg")
    patch_fourth = lax.axis_index("mem")
    members_here, fields, rows_here, lon_total = prior_sample_set.shape
    slots = observed_cell.shape[1]
    hid = kernel_in.shape[2]
    mem_count = lax.axis_size("mem")
    members = members_here * mem_count
    group = members_here // CHUNKS
    pairs = rows_here // 2
    forward, backward = shift_lists("reg")
    room = FPAD - fields
    mixes = jnp.pad(kernel_in, ((0, 0), (0, 0), (0, 0), (0, room)))
    mixes = mixes.reshape(NBLK, 3, 3, hid, FPAD).transpose(0, 1, 3, 2, 4)
    mixes = mixes.reshape(NBLK, 3 * hid, 3 * FPAD)
    backs = jnp.pad(kernel_out, ((0, 0), (0, room), (0, 0)))
    biases = bias_in[:, :, None]
    low = lax.ppermute(prior_sample_set[:, :, rows_here - 1, :], "reg", forward)
    high = lax.ppermute(prior_sample_set[:, :, 0, :], "reg", backward)
    flops = group * rows_here * lon_total * hid * fields * 20
    bf = jnp.bfloat16
    steps = group // STEP
    weight_specs = [whole((3 * hid, 3 * FPAD)), whole((hid, 1)), whole((FPAD, hid))]
    edge = pl.BlockSpec((STEP, FPAD, lon_total), lambda i: (i, 0, 0))
    middle = pl.BlockSpec((STEP, rows_here, FPAD, lon_total), lambda i: (i, 0, 0, 0))
    firsts = []
    for c in range(CHUNKS):
        outer = pl.BlockSpec((STEP, fields, lon_total), lambda i, c=c: (i + c * steps, 0, 0))
        firsts.append(
            call(
                first_kernel,
                (steps,),
                [
                    pl.BlockSpec(
                        (STEP, fields, rows_here, lon_total), lambda i, c=c: (i + c * steps, 0, 0, 0)
                    ),
                    outer,
                    outer,
                ]
                + weight_specs,
                [
                    jax.ShapeDtypeStruct((group, rows_here, FPAD, lon_total), bf),
                    jax.ShapeDtypeStruct((group, FPAD, lon_total), bf),
                    jax.ShapeDtypeStruct((group, FPAD, lon_total), bf),
                ],
                [middle, edge, edge],
                [pltpu.VMEM((STEP, rows_here + 2, FPAD, lon_total), jnp.float32)],
                flops,
                group * 6 * fields * lon_total * 4,
            )(prior_sample_set, low, high, mixes[0], biases[0], backs[0])
        )
    edges = [
        (lax.ppermute(bot, "reg", forward), lax.ppermute(top, "reg", backward))
        for _, top, bot in firsts
    ]
    parts = []
    zshape = (mem_count, fields, pairs, group, 128)
    for c in range(CHUNKS):
        parts.append(
            call(
                second_kernel,
                (steps,),
                [middle, edge, edge] + weight_specs,
                jax.ShapeDtypeStruct(zshape, bf),
                whole(zshape),
                [pltpu.VMEM((rows_here, 2, FPAD * group, 128), jnp.float32)],
                flops,
                group * 6 * fields * lon_total * 4,
            )(firsts[c][0], edges[c][0], edges[c][1], mixes[1], biases[1], backs[1])
        )
    arrived = [lax.all_to_all(z, "mem", split_axis=0, concat_axis=0, tiled=True) for z in parts]
    field_row = lax.dynamic_slice_in_dim(sensor_position_variable, parallel_strip, 1, 0)
    cell_row = lax.dynamic_slice_in_dim(observed_cell, parallel_strip, 1, 0)
    picked = jnp.concatenate(
        [
            call(
                sample_kernel,
                (1,),
                [whole(zshape), whole((1, slots)), whole((1, slots))],
                jax.ShapeDtypeStruct((group, slots), bf),
                whole((group, slots)),
                [pltpu.VMEM((rows_here * lon_total, slots), bf)],
                2 * group * fields * 1024 * slots,
                group * fields * 2048,
            )(z, cell_row, field_row)
            for z in parts
        ],
        axis=0,
    )
    every_member = lax.all_gather(picked[None], "mem", axis=1, tiled=True)
    three_bands = jnp.concatenate(
        [
            lax.ppermute(every_member, "reg", forward),
            every_member,
            lax.ppermute(every_member, "reg", backward),
        ],
        axis=0,
    )
    cells_pad = jnp.pad(observed_cell, ((1, 1), (0, 0)))
    counts_pad = jnp.pad(observed_count, ((1, 1),))
    values_pad = jnp.pad(observed_value, ((1, 1), (0, 0)))
    variance_pad = jnp.pad(error_variance, ((1, 1), (0, 0)), constant_values=1.0)
    weights_matrix = region_transform(
        three_bands.astype(jnp.float32),
        lax.dynamic_slice_in_dim(cells_pad, parallel_strip, 3, 0),
        lax.dynamic_slice_in_dim(counts_pad, parallel_strip, 3, 0),
        lax.dynamic_slice_in_dim(values_pad, parallel_strip, 3, 0),
        lax.dynamic_slice_in_dim(variance_pad, parallel_strip, 3, 0),
        lax.dynamic_slice_in_dim(radius, parallel_strip, 1, 0)[0],
        parallel_strip - 1,
        patch_fourth,
        rows_here,
        lon_total,
        lon_total // mem_count,
        NS_ITERS,
    )
    folded = weights_matrix + (1.0 - jnp.sum(weights_matrix, axis=0, keepdims=True)) / members
    folded = folded.reshape(mem_count, CHUNKS, group, members).transpose(1, 0, 2, 3)
    folded = folded.reshape(members, members)
    coarse = folded.astype(bf)
    fine = (folded - coarse.astype(jnp.float32)).astype(bf)
    third = fields // 3
    updated = call(
        mix_kernel,
        (3,),
        [pl.BlockSpec((mem_count, third, pairs, group, 128), lambda i: (0, i, 0, 0, 0))] * CHUNKS
        + [whole((2 * members, members))],
        jax.ShapeDtypeStruct((fields, rows_here, lon_total // mem_count, members), bf),
        pl.BlockSpec((third, rows_here, lon_total // mem_count, members), lambda i: (i, 0, 0, 0)),
        (),
        4 * members * members * fields * 256,
        members * fields * 1024,
    )(*arrived, jnp.concatenate([coarse, fine], axis=0))
    return updated.transpose(3, 0, 1, 2)


def solution(mesh):
    return jax.shard_map(
        body,
        mesh=mesh,
        in_specs=(P("mem", None, "reg", None), P(), P(), P(), P(), P(), P(), P(), P(), P()),
        out_specs=P(None, None, "reg", "mem"),
        check_vma=False,
    )
```

time: 578 us -> 242 us (0.42); the launches traced: 568 us -> 241 us
  local copies, waits for them, and re-layouts: 182 us -> 26.5 us
  blocking collectives: 150 us -> 14.4 us
  matrix products: 136 us -> 7.09 us
  Pallas kernels: 0 us -> 76 us
  waiting for transfers between devices: 40.8 us -> 83.6 us
  other arithmetic: 33 us -> 0.61 us
  starting transfers between devices: 22.8 us -> 31.1 us
    all_gather x1, blocking collectives: 150 us -> 14.4 us  [body(): every_member = lax.all_gather(picked[None], 'mem', axis=1, tiled=True)]
    dot_general x25 -> x0, matrix products: 129 us -> none  [the longest x8 62.5 us: group_step(): jnp.einsum('ghpl,fh->gfpl', hidden, kernel_back, preferred_element_type=j...]
    pallas_call x0 -> x7, Pallas kernels: none -> 76 us  [the longest x2 26.3 us: body(): call(first_kernel, (steps,), [pl.BlockSpec((STEP, fields, rows_here, lon_...]
    convert_element_type x4 -> x0, local copies, waits for them, and re-layouts: 55.9 us -> none  [the longest x3 49.4 us: body(): flat_part = region_part.reshape(shape_here[0], shape_here[1] * shape_here...]
    all_to_all x1 -> x2, waiting for transfers between devices: 0.01 us -> 47.1 us  [body(): lax.all_to_all(z, 'mem', split_axis=0, concat_axis=0, tiled=True)]
    another operation x12 -> x0, local copies, waits for them, and re-layouts: 40.1 us -> none  [the longest x2 21.2 us: body(): flat_state = current.reshape(members_here, fields * rows_here * lon_total)]
    concatenate x2, other arithmetic: 15.2 us -> 0.01 us  [the longest x1 0.01 us: body(): jnp.concatenate([call(sample_kernel, (1,), [whole(zshape), whole((1, slot...]
    all_to_all x1 -> x0, local copies, waits for them, and re-layouts: 14.5 us -> none  [body(): lax.all_to_all(current, 'mem', split_axis=3, concat_axis=0, tiled=True)]
  transfers between devices with their start and end apart: 7 -> 10, of which waited for: 6 -> 8; matrix products, arithmetic and copies ran while one was open for 10% -> 6% of each run, Pallas kernels for 0% -> 13%
where the time goes in v1:
time: 242 us; the launch traced here: 241 us
  waiting for transfers between devices  83.6 us (35%)
  Pallas kernels  76 us (31%)
  starting transfers between devices  31.1 us (13%)
  local copies, waits for them, and re-layouts  26.5 us (11%)
  blocking collectives  14.4 us (6%)
  matrix products  7.09 us (3%)
    all_to_all x2, waiting for transfers between devices, body(): lax.all_to_all(z, 'mem', split_axis=0, concat_axis=0, tiled=True)  47.1 us
    pallas_call x2, Pallas kernels, body(): call(first_kernel, (steps,), [pl.BlockSpec((STEP, fields, rows_here, lon_...  26.3 us
    pallas_call x2, Pallas kernels, body(): call(second_kernel, (steps,), [middle, edge, edge] + weight_specs, jax.Sh...  26.1 us
    pallas_call x1, Pallas kernels, body(): call(mix_kernel, (3,), [pl.BlockSpec((mem_count, third, pairs, group, 128...  17.2 us
    all_gather x1, blocking collectives, body(): every_member = lax.all_gather(picked[None], 'mem', axis=1, tiled=True)  14.4 us
    unnamed x52, local copies, waits for them, and re-layouts  12.1 us
    ppermute x2, waiting for transfers between devices, body(): lax.ppermute(top, 'reg', backward)  10 us
    all_to_all x2, starting transfers between devices, body(): lax.all_to_all(z, 'mem', split_axis=0, concat_axis=0, tiled=True)  9.83 us
  transfers between devices with their start and end apart: 10, of which 8 were waited for; matrix products, arithmetic and copies ran while one was open for 6% of the time, Pallas kernels for 13%

profile of v1, /device:TPU:2, one launch (start us, length us, event | category | flops | bytes accessed | tf_op | source)
XLA Modules:
  0.0 241.3 jit_solution(6621701343996489862)
XLA Ops:
  0.0 7.2 %fusion.49 = (bf16[32,69,1,256]{3,2,1,0:T(2,128)(2,1)S(1)}, bf16[32,69,1,256]{3,2,1,0:T(2,128)(2,1)S(1)}) fusion(bf16[32,69,4,256]{3,2,1,0:T(4,128)(2,1)} %x_ref.3), kind=kLoop, calls=%fused_computation.78 | loop fusion | bytes 4521984 | tf_op jit(solution)/shard_map/slice | solution.py:266
  7.4 1.9 collective-permute-start
  9.4 1.3 copy.65
  10.7 3.6 %collective-permute-start.1 = (bf16[32,69,256]{2,0,1:T(8,128)(2,1)}, bf16[32,69,256]{2,0,1:T(8,128)(2,1)}, u32[]{:S(2)}, u32[]{:S(2)}) collective-permute-start(bf16[32,69,256]{2,0,1:T(8,128)(2,1)} %bitcast.83), channel_id=1, source_target_pairs={{1,0},{2,1},{3,2},{4,3},{5,4},{6,5},{7,6},{9,8},{10,9},{11,10},{12... | collective-permute-start | bytes 3391496 | tf_op jit(solution)/shard_map/ppermute | solution.py:266
  15.3 9.3 %collective-permute-done = bf16[32,69,256]{2,0,1:T(8,128)(2,1)} collective-permute-done((bf16[32,69,256]{2,0,1:T(8,128)(2,1)S(1)}, bf16[32,69,256]{2,0,1:T(8,128)(2,1)}, u32[]{:S(2)}, u32[]{:S(2)}) %collective-permute-start) | collective-permute-done | bytes 1130528 | tf_op jit(solution)/shard_map/ppermute | solution.py:265
  24.5 1.9 copy.39.low_ref
  26.4 9.2 %collective-permute-done.1 = bf16[32,69,256]{2,0,1:T(8,128)(2,1)} collective-permute-done((bf16[32,69,256]{2,0,1:T(8,128)(2,1)}, bf16[32,69,256]{2,0,1:T(8,128)(2,1)}, u32[]{:S(2)}, u32[]{:S(2)}) %collective-permute-start.1) | collective-permute-done | bytes 1130528 | tf_op jit(solution)/shard_map/ppermute | solution.py:266
  35.7 1.9 copy.40.high_ref
  37.6 13.3 %shard_map.102 = (bf16[16,4,72,256]{3,2,1,0:T(8,128)(2,1)S(1)}, bf16[16,72,256]{2,1,0:T(8,128)(2,1)S(1)}, bf16[16,72,256]{2,1,0:T(8,128)(2,1)}) custom-call(bf16[32,69,4,256]{3,2,1,0:T(4,128)(2,1)} %x_ref.3, bf16[32,69,256]{2,1,0:T(8,128)(2,1)S(1)} %copy.39.low_ref, bf16[32,69,256]{2,1,0:T(8,128)(2,1)S(1)} %copy.40.high_ref, ...), custom_call_target="tpu_custom_call" | custom-call | flops 2894069760 | bytes 6782976 | tf_op jit(solution)/shard_map/pallas_call | solution.py:277
  50.9 1.4 copy-done.13
  52.3 3.7 %collective-permute-start.4 = (bf16[16,72,256]{2,1,0:T(8,128)(2,1)}, bf16[16,72,256]{2,1,0:T(8,128)(2,1)S(1)}, u32[]{:S(2)}, u32[]{:S(2)}) collective-permute-start(bf16[16,72,256]{2,1,0:T(8,128)(2,1)} %get-tuple-element.37), channel_id=1, source_target_pairs={{0,1},{1,2},{2,3},{3,4},{4,5},{5,6},{6,7},{8,9},{9,10},{10,11},{11... | collective-permute-start | bytes 1769480 | tf_op jit(solution)/shard_map/ppermute | solution.py:300
  56.0 2.1 collective-permute-start.5
  58.1 0.7 copy.68
  58.8 1.0 copy.43.mix_ref
  59.9 4.0 %collective-permute-done.4.low_ref = bf16[16,72,256]{2,1,0:T(8,128)(2,1)S(1)} collective-permute-done((bf16[16,72,256]{2,1,0:T(8,128)(2,1)}, bf16[16,72,256]{2,1,0:T(8,128)(2,1)S(1)}, u32[]{:S(2)}, u32[]{:S(2)}) %collective-permute-start.4) | collective-permute-done | bytes 589856 | tf_op jit(solution)/shard_map/ppermute | solution.py:300
  63.9 5.3 %collective-permute-done.5.high_ref = bf16[16,72,256]{2,1,0:T(8,128)(2,1)S(1)} collective-permute-done((bf16[16,72,256]{2,1,0:T(8,128)(2,1)S(1)}, bf16[16,72,256]{2,1,0:T(8,128)(2,1)S(1)}, u32[]{:S(2)}, u32[]{:S(2)}) %collective-permute-start.5) | collective-permute-done | bytes 589856 | tf_op jit(solution)/shard_map/ppermute | solution.py:300
  69.2 1.7 copy-done.14
  70.9 13.0 %shard_map.103.z_ref = bf16[4,69,2,16,128]{4,3,2,1,0:T(8,128)(2,1)S(1)} custom-call(bf16[16,4,72,256]{3,2,1,0:T(8,128)(2,1)S(1)} %copy-done.14, bf16[16,72,256]{2,1,0:T(8,128)(2,1)S(1)} %collective-permute-done.4.low_ref, bf16[16,72,256]{2,1,0:T(8,128)(2,1)S(1)} %collective-permute-done.5.high_ref, bf16[384,216]{1,0:T(8,128)(2,1)S(1)} %copy.43.mix_ref, ...), custom_call_target="tpu_custom_call" | custom-call | flops 2894069760 | bytes 6782976 | tf_op jit(solution)/shard_map/pallas_call | solution.py:307
  83.9 1.4 copy-done.1
  85.3 4.9 %all-to-all-start.1 = ((bf16[4,69,2,16,128]{4,3,2,1,0:T(8,128)(2,1)}), bf16[4,69,2,16,128]{4,3,2,1,0:T(8,128)(2,1)S(1)}, u32[]{:S(2)}, u32[]{:S(2)}) async-start(bf16[4,69,2,16,128]{4,3,2,1,0:T(8,128)(2,1)} %copy-done.1), calls=%async_computation.1 | async-start | bytes 4521984 | tf_op jit(solution)/shard_map/all_to_all | solution.py:318
  90.2 1.3 copy-done.4
  91.5 0.9 copy-done.8
  92.4 13.0 %shard_map.100 = (bf16[16,4,72,256]{3,2,1,0:T(8,128)(2,1)S(1)}, bf16[16,72,256]{2,1,0:T(8,128)(2,1)}, bf16[16,72,256]{2,1,0:T(8,128)(2,1)}) custom-call(bf16[32,69,4,256]{3,2,1,0:T(4,128)(2,1)} %x_ref.3, bf16[32,69,256]{2,1,0:T(8,128)(2,1)S(1)} %copy.39.low_ref, bf16[32,69,256]{2,1,0:T(8,128)(2,1)S(1)} %copy-done.4, bf16[384,216]{1,0:T(8,128)(2,1)S(1)} %copy-done.8, ...), custom_call_target="tpu_custom_call" | custom-call | flops 2894069760 | bytes 6782976 | tf_op jit(solution)/shard_map/pallas_call | solution.py:277
  105.4 1.4 copy-done.11
  106.8 1.9 collective-permute-start.2
  108.7 3.8 %collective-permute-start.3 = (bf16[16,72,256]{2,1,0:T(8,128)(2,1)}, bf16[16,72,256]{2,1,0:T(8,128)(2,1)S(1)}, u32[]{:S(2)}, u32[]{:S(2)}) collective-permute-start(bf16[16,72,256]{2,1,0:T(8,128)(2,1)} %get-tuple-element.35), channel_id=1, source_target_pairs={{1,0},{2,1},{3,2},{4,3},{5,4},{6,5},{7,6},{9,8},{10,9},{11,10},{12... | collective-permute-start | bytes 1769480 | tf_op jit(solution)/shard_map/ppermute | solution.py:300
  112.6 0.8 constant_dynamic-slice_fusion
  113.4 1.6 copy-done.2
  115.0 3.2 %shard_map.105 = bf16[16,1024]{1,0:T(8,128)(2,1)S(1)} custom-call(bf16[4,69,2,16,128]{4,3,2,1,0:T(8,128)(2,1)S(1)} %copy-done.2, s32[1,1024]{1,0:T(1,128)S(1)} %get-tuple-element.79.cell_ref, s32[1,1024]{1,0:T(1,128)S(1)} %get-tuple-element.78.field_ref), custom_call_target="tpu_custom_call" | custom-call | flops 2315255808 | bytes 2260992 | tf_op jit(solution)/shard_map/pallas_call | solution.py:323
  118.3 4.7 %collective-permute-done.3.high_ref = bf16[16,72,256]{2,1,0:T(8,128)(2,1)S(1)} collective-permute-done((bf16[16,72,256]{2,1,0:T(8,128)(2,1)}, bf16[16,72,256]{2,1,0:T(8,128)(2,1)S(1)}, u32[]{:S(2)}, u32[]{:S(2)}) %collective-permute-start.3) | collective-permute-done | bytes 589856 | tf_op jit(solution)/shard_map/ppermute | solution.py:300
  123.0 13.0 %shard_map.101.z_ref = bf16[4,69,2,16,128]{4,3,2,1,0:T(8,128)(2,1)S(1)} custom-call(bf16[16,4,72,256]{3,2,1,0:T(8,128)(2,1)S(1)} %copy-done.12, bf16[16,72,256]{2,1,0:T(8,128)(2,1)S(1)} %collective-permute-done.2.low_ref, bf16[16,72,256]{2,1,0:T(8,128)(2,1)S(1)} %collective-permute-done.3.high_ref, bf16[384,216]{1,0:T(8,128)(2,1)S(1)} %copy-done.6, ...), custom_call_target="tpu_custom_call" | custom-call | flops 2894069760 | bytes 6782976 | tf_op jit(solution)/shard_map/pallas_call | solution.py:307
  136.1 3.2 %shard_map.104 = bf16[16,1024]{1,0:T(8,128)(2,1)S(1)} custom-call(bf16[4,69,2,16,128]{4,3,2,1,0:T(8,128)(2,1)S(1)} %shard_map.101.z_ref, s32[1,1024]{1,0:T(1,128)S(1)} %get-tuple-element.79.cell_ref, s32[1,1024]{1,0:T(1,128)S(1)} %get-tuple-element.78.field_ref), custom_call_target="tpu_custom_call" | custom-call | flops 2315255808 | bytes 2260992 | tf_op jit(solution)/shard_map/pallas_call | solution.py:323
  139.3 14.4 %all-gather = bf16[128,1024]{1,0:T(8,128)(2,1)S(1)} all-gather(bf16[32,1024]{1,0:T(8,128)(2,1)S(1)} %pad_maximum_fusion.1), channel_id=2, replica_groups=mesh['mem'=4,'reg'=8] {'mem'}, dimensions={0}, use_global_device_ids=true | all-gather | bytes 327680 | tf_op jit(solution)/shard_map/all_gather | solution.py:337
  153.8 1.9 collective-permute-start.7
  155.7 2.4 collective-permute-start.6
  158.1 0.6 dynamic_slice.25
  159.4 1.2 collective-permute-done.7
  160.6 2.8 %collective-permute-done.6 = bf16[1,128,1024]{2,1,0:T(8,128)(2,1)S(1)} collective-permute-done((bf16[1,128,1024]{2,1,0:T(8,128)(2,1)S(1)}, bf16[1,128,1024]{2,1,0:T(8,128)(2,1)S(1)}, u32[]{:S(2)}, u32[]{:S(2)}) %collective-permute-start.6) | collective-permute-done | bytes 262176 | tf_op jit(solution)/shard_map/ppermute | solution.py:340
  163.7 2.3 multiply_reduce_fusion
  166.7 1.4 fusion.19
  168.1 5.0 %all-to-all-start = ((bf16[4,69,2,16,128]{4,3,2,1,0:T(8,128)(2,1)}), bf16[4,69,2,16,128]{4,3,2,1,0:T(8,128)(2,1)}, u32[]{:S(2)}, u32[]{:S(2)}) async-start(bf16[4,69,2,16,128]{4,3,2,1,0:T(8,128)(2,1)} %copy-done), calls=%async_computation | async-start | bytes 4521984 | tf_op jit(solution)/shard_map/all_to_all | solution.py:318
  173.1 3.3 %while.13 = (s32[]{:T(128)}, f32[128,128]{0,1:T(8,128)S(1)}, f32[128,128]{1,0:T(8,128)S(1)}, s32[]{:T(128)}) while((s32[]{:T(128)}, f32[128,128]{0,1:T(8,128)S(1)}, f32[128,128]{1,0:T(8,128)S(1)}, s32[]{:T(128)}) %tuple.34), condition=%wide.region_3.4_spmd.clone, body=%wide.region_2.3_spmd.clone.sunk | while | flops 75563008 | bytes 852021 | solution.py:230
  173.6 0.3 convolution_bitcast_fusion.3
  174.4 0.3 convolution_bitcast_fusion.3
  175.2 0.3 convolution_bitcast_fusion.3
  176.0 0.3 convolution_bitcast_fusion.3
  177.0 47.1 %all-to-all-done.refs_0_ = bf16[4,69,2,16,128]{4,3,2,1,0:T(8,128)(2,1)} async-done(((bf16[4,69,2,16,128]{4,3,2,1,0:T(8,128)(2,1)}), bf16[4,69,2,16,128]{4,3,2,1,0:T(8,128)(2,1)}, u32[]{:S(2)}, u32[]{:S(2)}) %all-to-all-start) | async-done | bytes 2261024 | tf_op jit(solution)/shard_map/all_to_all | solution.py:318
  224.1 17.2 %shard_map.106 = bf16[69,4,64,128]{3,2,1,0:T(8,128)(2,1)} custom-call(bf16[4,69,2,16,128]{4,3,2,1,0:T(8,128)(2,1)} %all-to-all-done.refs_0_, bf16[4,69,2,16,128]{4,3,2,1,0:T(8,128)(2,1)S(1)} %all-to-all-done.1.refs_1_, bf16[256,128]{1,0:T(8,128)(2,1)S(1)} %pad_maximum_fusion.2.refs_2_), custom_call_target="tpu_custom_call" | custom-call | flops 1157627904 | bytes 9043968 | tf_op jit(solution)/shard_map/pallas_call | solution.py:370
  (83 shorter events, 4.4 us)
Async XLA Ops:
  7.4 17.1 %collective-permute-start = (bf16[32,69,256]{2,0,1:T(8,128)(2,1)S(1)}, bf16[32,69,256]{2,0,1:T(8,128)(2,1)}, u32[]{:S(2)}, u32[]{:S(2)}) collective-permute-start(bf16[32,69,256]{2,0,1:T(8,128)(2,1)S(1)} %bitcast.104), channel_id=1, source_target_pairs={{0,1},{1,2},{2,3},{3,4},{4,5},{5,6},{6,7},{8,9},{9,10},{10,11},{11... | collective-permute-start | bytes 3391496 | tf_op jit(solution)/shard_map/ppermute | solution.py:265
  9.4 4.9 %copy-start.17 = (bf16[2,69,128]{2,0,1:T(2,128)(2,1)S(1)}, bf16[2,69,128]{2,0,1:T(2,128)(2,1)}, u32[]{:S(2)}) copy-start(bf16[2,69,128]{2,0,1:T(2,128)(2,1)} %param.15) | copy-start | bytes 105988
  9.4 5.0 %copy-start.20 = (f32[2,128]{1,0:T(2,128)S(1)}, f32[2,128]{1,0:T(2,128)}, u32[]{:S(2)}) copy-start(f32[2,128]{1,0:T(2,128)} %param.14) | copy-start | bytes 3076
  9.4 5.1 %copy-start.15 = (bf16[2,9,128,69]{2,0,3,1:T(2,128)(2,1)S(1)}, bf16[2,9,128,69]{2,0,3,1:T(2,128)(2,1)}, u32[]{:S(2)}) copy-start(bf16[2,9,128,69]{2,0,3,1:T(2,128)(2,1)} %param.13) | copy-start | bytes 953860
  10.7 25.0 %collective-permute-start.1 = (bf16[32,69,256]{2,0,1:T(8,128)(2,1)}, bf16[32,69,256]{2,0,1:T(8,128)(2,1)}, u32[]{:S(2)}, u32[]{:S(2)}) collective-permute-start(bf16[32,69,256]{2,0,1:T(8,128)(2,1)} %bitcast.83), channel_id=1, source_target_pairs={{1,0},{2,1},{3,2},{4,3},{5,4},{6,5},{7,6},{9,8},{10,9},{11,10},{12... | collective-permute-start | bytes 3391496 | tf_op jit(solution)/shard_map/ppermute | solution.py:266
  15.3 22.3 %copy-start.7 = (bf16[384,216]{1,0:T(8,128)(2,1)}, bf16[384,216]{1,0:T(8,128)(2,1)S(1)}, u32[]{:S(2)}) copy-start(bf16[384,216]{1,0:T(8,128)(2,1)S(1)} %copy.41.mix_ref) | copy-start | bytes 497668
  37.6 13.3 %copy-start.3 = (bf16[32,69,256]{2,1,0:T(8,128)(2,1)}, bf16[32,69,256]{2,1,0:T(8,128)(2,1)S(1)}, u32[]{:S(2)}) copy-start(bf16[32,69,256]{2,1,0:T(8,128)(2,1)S(1)} %copy.40.high_ref) | copy-start | bytes 3391492
  50.9 1.4 copy-start.13
  52.3 11.6 %collective-permute-start.4 = (bf16[16,72,256]{2,1,0:T(8,128)(2,1)}, bf16[16,72,256]{2,1,0:T(8,128)(2,1)S(1)}, u32[]{:S(2)}, u32[]{:S(2)}) collective-permute-start(bf16[16,72,256]{2,1,0:T(8,128)(2,1)} %get-tuple-element.37), channel_id=1, source_target_pairs={{0,1},{1,2},{2,3},{3,4},{4,5},{5,6},{6,7},{8,9},{9,10},{10,11},{11... | collective-permute-start | bytes 1769480 | tf_op jit(solution)/shard_map/ppermute | solution.py:300
  56.0 13.2 %collective-permute-start.5 = (bf16[16,72,256]{2,1,0:T(8,128)(2,1)S(1)}, bf16[16,72,256]{2,1,0:T(8,128)(2,1)S(1)}, u32[]{:S(2)}, u32[]{:S(2)}) collective-permute-start(bf16[16,72,256]{2,1,0:T(8,128)(2,1)S(1)} %get-tuple-element.38), channel_id=1, source_target_pairs={{1,0},{2,1},{3,2},{4,3},{5,4},{6,5},{7,6},{9,8},{10,9},{11,10},{12... | collective-permute-start | bytes 1769480 | tf_op jit(solution)/shard_map/ppermute | solution.py:300
  58.1 25.8 %copy-start.9 = (f32[128,1]{1,0:T(8,128)}, f32[128,1]{1,0:T(8,128)S(1)}, u32[]{:S(2)}) copy-start(f32[128,1]{1,0:T(8,128)S(1)} %copy.44.bias_ref) | copy-start | bytes 1540
  59.9 24.0 %copy-start.5 = (bf16[384,216]{1,0:T(8,128)(2,1)}, bf16[384,216]{1,0:T(8,128)(2,1)S(1)}, u32[]{:S(2)}) copy-start(bf16[384,216]{1,0:T(8,128)(2,1)S(1)} %copy.43.mix_ref) | copy-start | bytes 497668
  69.2 1.7 copy-start.14
  83.9 1.4 copy-start.1
  85.3 82.8 %all-to-all-start.1 = ((bf16[4,69,2,16,128]{4,3,2,1,0:T(8,128)(2,1)}), bf16[4,69,2,16,128]{4,3,2,1,0:T(8,128)(2,1)S(1)}, u32[]{:S(2)}, u32[]{:S(2)}) async-start(bf16[4,69,2,16,128]{4,3,2,1,0:T(8,128)(2,1)} %copy-done.1), calls=%async_computation.1 | async-start | bytes 4521984 | tf_op jit(solution)/shard_map/all_to_all | solution.py:318
  90.2 1.3 copy-start.4
  91.4 0.9 copy-start.8
  105.4 1.4 copy-start.11
  106.8 11.4 %collective-permute-start.2 = (bf16[16,72,256]{2,1,0:T(8,128)(2,1)}, bf16[16,72,256]{2,1,0:T(8,128)(2,1)S(1)}, u32[]{:S(2)}, u32[]{:S(2)}) collective-permute-start(bf16[16,72,256]{2,1,0:T(8,128)(2,1)} %get-tuple-element.34), channel_id=1, source_target_pairs={{0,1},{1,2},{2,3},{3,4},{4,5},{5,6},{6,7},{8,9},{9,10},{10,11},{11... | collective-permute-start | bytes 1769480 | tf_op jit(solution)/shard_map/ppermute | solution.py:300
  108.7 14.2 %collective-permute-start.3 = (bf16[16,72,256]{2,1,0:T(8,128)(2,1)}, bf16[16,72,256]{2,1,0:T(8,128)(2,1)S(1)}, u32[]{:S(2)}, u32[]{:S(2)}) collective-permute-start(bf16[16,72,256]{2,1,0:T(8,128)(2,1)} %get-tuple-element.35), channel_id=1, source_target_pairs={{1,0},{2,1},{3,2},{4,3},{5,4},{6,5},{7,6},{9,8},{10,9},{11,10},{12... | collective-permute-start | bytes 1769480 | tf_op jit(solution)/shard_map/ppermute | solution.py:300
  113.4 1.6 copy-start.2
  115.0 7.9 %copy-start.6 = (bf16[384,216]{1,0:T(8,128)(2,1)S(1)}, bf16[384,216]{1,0:T(8,128)(2,1)}, u32[]{:S(2)}) copy-start(bf16[384,216]{1,0:T(8,128)(2,1)} %copy-done.5) | copy-start | bytes 497668
  115.0 7.9 %copy-start.10 = (f32[128,1]{1,0:T(8,128)S(1)}, f32[128,1]{1,0:T(8,128)}, u32[]{:S(2)}) copy-start(f32[128,1]{1,0:T(8,128)} %copy-done.9) | copy-start | bytes 1540
  115.0 7.9 %copy-start.12 = (bf16[16,4,72,256]{3,2,1,0:T(8,128)(2,1)S(1)}, bf16[16,4,72,256]{3,2,1,0:T(8,128)(2,1)}, u32[]{:S(2)}) copy-start(bf16[16,4,72,256]{3,2,1,0:T(8,128)(2,1)} %copy-done.11) | copy-start | bytes 7077892
  136.0 3.3 %copy-start = (bf16[4,69,2,16,128]{4,3,2,1,0:T(8,128)(2,1)}, bf16[4,69,2,16,128]{4,3,2,1,0:T(8,128)(2,1)S(1)}, u32[]{:S(2)}) copy-start(bf16[4,69,2,16,128]{4,3,2,1,0:T(8,128)(2,1)S(1)} %shard_map.101.z_ref) | copy-start | bytes 6782980
  136.0 22.1 %copy-start.22 = (s32[8]{0:T(128)S(1)}, s32[8]{0:T(128)}, u32[]{:S(2)}) copy-start(s32[8]{0:T(128)} %param.21) | copy-start | bytes 100
  136.0 23.3 %copy-start.21 = (s32[8]{0:T(128)S(1)}, s32[8]{0:T(128)}, u32[]{:S(2)}) copy-start(s32[8]{0:T(128)} %param.18) | copy-start | bytes 100
  136.0 27.5 %copy-start.16 = (s32[8,1024]{1,0:T(8,128)S(1)}, s32[8,1024]{1,0:T(8,128)}, u32[]{:S(2)}) copy-start(s32[8,1024]{1,0:T(8,128)} %param.16) | copy-start | bytes 98308
  136.1 27.5 %copy-start.18 = (f32[8,1024]{1,0:T(8,128)S(1)}, f32[8,1024]{1,0:T(8,128)}, u32[]{:S(2)}) copy-start(f32[8,1024]{1,0:T(8,128)} %param.19) | copy-start | bytes 98308
  136.1 27.5 %copy-start.19 = (f32[8,1024]{1,0:T(8,128)S(1)}, f32[8,1024]{1,0:T(8,128)}, u32[]{:S(2)}) copy-start(f32[8,1024]{1,0:T(8,128)} %param.20) | copy-start | bytes 98308
  153.8 6.8 %collective-permute-start.7 = (bf16[1,128,1024]{2,1,0:T(8,128)(2,1)S(1)}, bf16[1,128,1024]{2,1,0:T(8,128)(2,1)S(1)}, u32[]{:S(2)}, u32[]{:S(2)}) collective-permute-start(bf16[1,128,1024]{2,1,0:T(8,128)(2,1)S(1)} %bitcast.105), channel_id=1, source_target_pairs={{1,0},{2,1},{3,2},{4,3},{5,4},{6,5},{7,6},{9,8},{10,9},{11,10},{12... | collective-permute-start | bytes 786440 | tf_op jit(solution)/shard_map/ppermute | solution.py:342
  155.7 7.7 %collective-permute-start.6 = (bf16[1,128,1024]{2,1,0:T(8,128)(2,1)S(1)}, bf16[1,128,1024]{2,1,0:T(8,128)(2,1)S(1)}, u32[]{:S(2)}, u32[]{:S(2)}) collective-permute-start(bf16[1,128,1024]{2,1,0:T(8,128)(2,1)S(1)} %bitcast.106), channel_id=1, source_target_pairs={{0,1},{1,2},{2,3},{3,4},{4,5},{5,6},{6,7},{8,9},{9,10},{10,11},{11... | collective-permute-start | bytes 786440 | tf_op jit(solution)/shard_map/ppermute | solution.py:340
  168.1 56.0 %all-to-all-start = ((bf16[4,69,2,16,128]{4,3,2,1,0:T(8,128)(2,1)}), bf16[4,69,2,16,128]{4,3,2,1,0:T(8,128)(2,1)}, u32[]{:S(2)}, u32[]{:S(2)}) async-start(bf16[4,69,2,16,128]{4,3,2,1,0:T(8,128)(2,1)} %copy-done), calls=%async_computation | async-start | bytes 4521984 | tf_op jit(solution)/shard_map/all_to_all | solution.py:318

commit v2 on v1

--- a/solution.py
+++ b/solution.py
@@ -7,7 +7,7 @@
 
 NBLK = 2
 NS_ITERS = 4
-CHUNKS = 2
+CHUNKS = 4
 FPAD = 72
 STEP = 2
 VMEM = 48 * 1024 * 1024
@@ -46,7 +46,7 @@
     return results
 
 
-def first_kernel(x_ref, low_ref, high_ref, mix_ref, bias_ref, back_ref, y_ref, top_ref, bot_ref, scr):
+def first_kernel(x_ref, low_ref, high_ref, mix_ref, bias_ref, back_ref, _, y_ref, top_ref, bot_ref, scr):
     fields, height = x_ref.shape[1], x_ref.shape[2]
     scr[...] = jnp.zeros_like(scr)
     for u in range(x_ref.shape[0]):
@@ -64,7 +64,7 @@
         bot_ref[u] = out[height - 1].astype(jnp.bfloat16)
 
 
-def second_kernel(y_ref, low_ref, high_ref, mix_ref, bias_ref, back_ref, z_ref, scr):
+def second_kernel(y_ref, low_ref, high_ref, mix_ref, bias_ref, back_ref, _, z_ref, scr):
     height = y_ref.shape[1]
     group, fields = z_ref.shape[3], z_ref.shape[1]
     step = pl.program_id(0)
@@ -93,8 +93,9 @@
                     z_ref[2 * h + 1, rows, pp] = odd.reshape(fields // 3, group, 128)
 
 
-def sample_kernel(z_ref, cell_ref, field_ref, out_ref, hot):
-    quarters, fields, pairs, group, lanes = z_ref.shape
+def sample_kernel(*refs):
+    parts, (cell_ref, field_ref, out_ref, hot) = refs[:-4], refs[-4:]
+    quarters, fields, pairs, group, lanes = parts[0].shape
     slots = cell_ref.shape[1]
     cell = cell_ref[...]
     lane = lax.broadcasted_iota(jnp.int32, (lanes, slots), 0)
@@ -106,32 +107,42 @@
             )
     wanted = field_ref[...]
     block = fields // 3
-
-    def part(i, total):
+    count = len(parts)
+
+    def step(i, total):
         rows = pl.ds(i * block, block)
         left = jnp.concatenate(
             [
-                z_ref[q, rows, pp].reshape(block * group, lanes)
-                for q in range(quarters)
-                for pp in range(pairs)
+                jnp.concatenate(
+                    [
+                        part[q, rows, pp].reshape(block * group, lanes)
+                        for q in range(quarters)
+                        for pp in range(pairs)
+                    ],
+                    axis=1,
+                )
+                for part in parts
             ],
-            axis=1,
+            axis=0,
         )
+        result = []
         for n in range(slots // 256):
             cols = slice(n * 256, (n + 1) * 256)
             found = jnp.dot(left, hot[:, cols], preferred_element_type=jnp.float32)
-            piece = total[n]
+            pieces = [total[n * count + c] for c in range(count)]
             for f in range(block):
-                piece = jnp.where(
-                    wanted[:, cols] == i * block + f, found[f * group : (f + 1) * group], piece
-                )
-            total = total[:n] + (piece,) + total[n + 1 :]
-        return total
-
-    zero = tuple(jnp.zeros((group, 256), jnp.float32) for _ in range(slots // 256))
-    total = lax.fori_loop(0, 3, part, zero)
+                match = wanted[:, cols] == i * block + f
+                for c in range(count):
+                    start = (c * block + f) * group
+                    pieces[c] = jnp.where(match, found[start : start + group], pieces[c])
+            result += pieces
+        return tuple(result)
+
+    zero = tuple(jnp.zeros((group, 256), jnp.float32) for _ in range(count * (slots // 256)))
+    total = lax.fori_loop(0, 3, step, zero)
     for n in range(slots // 256):
-        out_ref[:, n * 256 : (n + 1) * 256] = total[n].astype(jnp.bfloat16)
+        joined = jnp.concatenate(total[n * count : (n + 1) * count], axis=0)
+        out_ref[:, n * 256 : (n + 1) * 256] = joined.astype(jnp.bfloat16)
 
 
 def mix_kernel(*refs):
@@ -152,7 +163,7 @@
             out_ref[f, 2 * pp + 1] = mixed[64:]
         return carry
 
-    lax.fori_loop(0, fields, one, 0)
+    lax.fori_loop(0, fields, one, 0, unroll=True)
 
 
 def call(kernel, grid, in_specs, out_shape, out_specs, scratch=(), flops=0, moved=0):
@@ -262,60 +273,79 @@
     mixes = mixes.reshape(NBLK, 3 * hid, 3 * FPAD)
     backs = jnp.pad(kernel_out, ((0, 0), (0, room), (0, 0)))
     biases = bias_in[:, :, None]
-    low = lax.ppermute(prior_sample_set[:, :, rows_here - 1, :], "reg", forward)
-    high = lax.ppermute(prior_sample_set[:, :, 0, :], "reg", backward)
     flops = group * rows_here * lon_total * hid * fields * 20
     bf = jnp.bfloat16
     steps = group // STEP
     weight_specs = [whole((3 * hid, 3 * FPAD)), whole((hid, 1)), whole((FPAD, hid))]
+    weight_specs = weight_specs + [pl.BlockSpec(memory_space=pl.ANY)]
     edge = pl.BlockSpec((STEP, FPAD, lon_total), lambda i: (i, 0, 0))
     middle = pl.BlockSpec((STEP, rows_here, FPAD, lon_total), lambda i: (i, 0, 0, 0))
-    firsts = []
+    outer = pl.BlockSpec((STEP, fields, lon_total), lambda i: (i, 0, 0))
+    zshape = (mem_count, fields, pairs, group, 128)
+    moved = group * 6 * fields * lon_total * 4
+
+    def first(c, edge_rows, previous):
+        return call(
+            first_kernel,
+            (steps,),
+            [
+                pl.BlockSpec(
+                    (STEP, fields, rows_here, lon_total), lambda i: (i + c * steps, 0, 0, 0)
+                ),
+                outer,
+                outer,
+            ]
+            + weight_specs,
+            [
+                jax.ShapeDtypeStruct((group, rows_here, FPAD, lon_total), bf),
+                jax.ShapeDtypeStruct((group, FPAD, lon_total), bf),
+                jax.ShapeDtypeStruct((group, FPAD, lon_total), bf),
+            ],
+            [middle, edge, edge],
+            [pltpu.VMEM((STEP, rows_here + 2, FPAD, lon_total), jnp.float32)],
+            flops,
+            moved,
+        )(prior_sample_set, *edge_rows, mixes[0], biases[0], backs[0], previous)
+
+    def second(state, edge_rows, previous):
+        return call(
+            second_kernel,
+            (steps,),
+            [middle, edge, edge] + weight_specs,
+            jax.ShapeDtypeStruct(zshape, bf),
+            whole(zshape),
+            [pltpu.VMEM((rows_here, 2, FPAD * group, 128), jnp.float32)],
+            flops,
+            moved,
+        )(state, *edge_rows, mixes[1], biases[1], backs[1], previous)
+
+    def exchange(bottom, top):
+        return lax.ppermute(bottom, "reg", forward), lax.ppermute(top, "reg", backward)
+
+    def spread(z):
+        return lax.all_to_all(z, "mem", split_axis=0, concat_axis=0, tiled=True)
+
+    outer_edges, ends = [], None
     for c in range(CHUNKS):
-        outer = pl.BlockSpec((STEP, fields, lon_total), lambda i, c=c: (i + c * steps, 0, 0))
-        firsts.append(
-            call(
-                first_kernel,
-                (steps,),
-                [
-                    pl.BlockSpec(
-                        (STEP, fields, rows_here, lon_total), lambda i, c=c: (i + c * steps, 0, 0, 0)
-                    ),
-                    outer,
-                    outer,
-                ]
-                + weight_specs,
-                [
-                    jax.ShapeDtypeStruct((group, rows_here, FPAD, lon_total), bf),
-                    jax.ShapeDtypeStruct((group, FPAD, lon_total), bf),
-                    jax.ShapeDtypeStruct((group, FPAD, lon_total), bf),
-                ],
-                [middle, edge, edge],
-                [pltpu.VMEM((STEP, rows_here + 2, FPAD, lon_total), jnp.float32)],
-                flops,
-                group * 6 * fields * lon_total * 4,
-            )(prior_sample_set, low, high, mixes[0], biases[0], backs[0])
-        )
-    edges = [
-        (lax.ppermute(bot, "reg", forward), lax.ppermute(top, "reg", backward))
-        for _, top, bot in firsts
-    ]
-    parts = []
-    zshape = (mem_count, fields, pairs, group, 128)
-    for c in range(CHUNKS):
-        parts.append(
-            call(
-                second_kernel,
-                (steps,),
-                [middle, edge, edge] + weight_specs,
-                jax.ShapeDtypeStruct(zshape, bf),
-                whole(zshape),
-                [pltpu.VMEM((rows_here, 2, FPAD * group, 128), jnp.float32)],
-                flops,
-                group * 6 * fields * lon_total * 4,
-            )(firsts[c][0], edges[c][0], edges[c][1], mixes[1], biases[1], backs[1])
-        )
-    arrived = [lax.all_to_all(z, "mem", split_axis=0, concat_axis=0, tiled=True) for z in parts]
+        own = prior_sample_set[c * group : (c + 1) * group]
+        bottom, top = own[:, :, rows_here - 1, :], own[:, :, 0, :]
+        if ends is not None:
+            bottom, top, _ = lax.optimization_barrier((bottom, top, ends))
+        ends = bottom
+        outer_edges.append(exchange(bottom, top))
+    firsts, parts, arrived = [], [], []
+    previous = bias_in
+    order = [(0, 0), (0, 1)] + [(1 - n % 2, n // 2 + (2 if n % 2 else 0)) for n in range(2 * CHUNKS - 4)]
+    for layer, c in order + [(1, CHUNKS - 2), (1, CHUNKS - 1)]:
+        if layer == 0:
+            state, top, bottom = first(c, outer_edges[c], previous)
+            firsts.append((state, exchange(bottom, top)))
+            previous = top
+        else:
+            parts.append(second(*firsts[c], previous))
+            previous = parts[-1]
+            if c < CHUNKS - 1:
+                arrived.append(spread(parts[-1]))
     field_row = lax.dynamic_slice_in_dim(sensor_position_variable, parallel_strip, 1, 0)
     cell_row = lax.dynamic_slice_in_dim(observed_cell, parallel_strip, 1, 0)
     picked = jnp.concatenate(
@@ -323,18 +353,20 @@
             call(
                 sample_kernel,
                 (1,),
-                [whole(zshape), whole((1, slots)), whole((1, slots))],
-                jax.ShapeDtypeStruct((group, slots), bf),
-                whole((group, slots)),
+                [whole(zshape)] * 2 + [whole((1, slots)), whole((1, slots))],
+                jax.ShapeDtypeStruct((2 * group, slots), bf),
+                whole((2 * group, slots)),
                 [pltpu.VMEM((rows_here * lon_total, slots), bf)],
-                2 * group * fields * 1024 * slots,
-                group * fields * 2048,
-            )(z, cell_row, field_row)
-            for z in parts
+                4 * group * fields * 1024 * slots,
+                group * fields * 4096,
+            )(parts[c], parts[c + 1], cell_row, field_row)
+            for c in range(0, CHUNKS, 2)
         ],
         axis=0,
     )
     every_member = lax.all_gather(picked[None], "mem", axis=1, tiled=True)
+    last, every_member = lax.optimization_barrier((parts[-1], every_member))
+    arrived.append(spread(last))
     three_bands = jnp.concatenate(
         [
             lax.ppermute(every_member, "reg", forward),

time: 242 us -> 229 us (0.946)
  waiting for transfers between devices: 83.6 us -> 26.4 us
  starting transfers between devices: 31.1 us -> 69.4 us
  blocking collectives: 14.4 us -> 18.7 us
  local copies, waits for them, and re-layouts: 26.5 us -> 29.4 us
    ppermute x6 -> x16, waiting for transfers between devices: 32.5 us -> 0.04 us  [the longest x8 0.02 us: exchange(): lax.ppermute(top, 'reg', backward)]
    ppermute x6 -> x16, starting transfers between devices: 17 us -> 46 us  [the longest x8 26.9 us: exchange(): lax.ppermute(bottom, 'reg', forward)]
    all_to_all x2 -> x4, waiting for transfers between devices: 47.1 us -> 22.3 us  [spread(): return lax.all_to_all(z, 'mem', split_axis=0, concat_axis=0, tiled=True)]
    pallas_call x1, Pallas kernels: 17.2 us -> 5.91 us  [body(): call(mix_kernel, (3,), [pl.BlockSpec((mem_count, third, pairs, group, 128...]
    pallas_call x6 -> x10, Pallas kernels: 58.9 us -> 68.2 us  [the longest x4 29.7 us: second(): call(second_kernel, (steps,), [middle, edge, edge] + weight_specs, jax.Sh...]
    all_to_all x2 -> x4, starting transfers between devices: 9.83 us -> 19.2 us  [spread(): return lax.all_to_all(z, 'mem', split_axis=0, concat_axis=0, tiled=True)]
    all_gather x1, blocking collectives: 14.4 us -> 18.7 us  [body(): every_member = lax.all_gather(picked[None], 'mem', axis=1, tiled=True)]
    ppermute x2 -> x0, local copies, waits for them, and re-layouts: 3.76 us -> none  [the longest x1 1.88 us: body(): low = lax.ppermute(prior_sample_set[:, :, rows_here - 1, :], 'reg', forward)]
  transfers between devices with their start and end apart: 10 -> 22, of which waited for: 8 -> 4; matrix products, arithmetic and copies ran while one was open for 6% -> 7% of each run, Pallas kernels for 13% -> 26%
where the time goes in v2:
time: 229 us; the launch traced here: 228 us
  Pallas kernels  74.2 us (32%)
  starting transfers between devices  69.4 us (30%)
  local copies, waits for them, and re-layouts  29.4 us (13%)
  waiting for transfers between devices  26.4 us (12%)
  blocking collectives  18.7 us (8%)
  matrix products  7.1 us (3%)
    pallas_call x4, Pallas kernels, second(): call(second_kernel, (steps,), [middle, edge, edge] + weight_specs, jax.Sh...  29.7 us
    pallas_call x4, Pallas kernels, first(): call(first_kernel, (steps,), [pl.BlockSpec((STEP, fields, rows_here, lon_...  29.3 us
    ppermute x8, starting transfers between devices, exchange(): lax.ppermute(bottom, 'reg', forward)  26.9 us
    all_to_all x4, waiting for transfers between devices, spread(): return lax.all_to_all(z, 'mem', split_axis=0, concat_axis=0, tiled=True)  22.3 us
    all_to_all x4, starting transfers between devices, spread(): return lax.all_to_all(z, 'mem', split_axis=0, concat_axis=0, tiled=True)  19.2 us
    ppermute x8, starting transfers between devices, exchange(): lax.ppermute(top, 'reg', backward)  19.1 us
    all_gather x1, blocking collectives, body(): every_member = lax.all_gather(picked[None], 'mem', axis=1, tiled=True)  18.7 us
    unnamed x66, local copies, waits for them, and re-layouts  13.2 us
  transfers between devices with their start and end apart: 22, of which 4 were waited for; matrix products, arithmetic and copies ran while one was open for 7% of the time, Pallas kernels for 26%

profile of v2, /device:TPU:2, one launch (start us, length us, event | category | flops | bytes accessed | tf_op | source)
XLA Modules:
  0.0 227.9 jit_solution(11721286421756849300)
XLA Ops:
  0.0 9.0 %fusion.49 = (bf16[8,69,1,256]{3,2,1,0:T(2,128)(2,1)}, bf16[8,69,1,256]{3,2,1,0:T(2,128)(2,1)}, bf16[8,69,1,256]{3,2,1,0:T(2,128)(2,1)}, bf16[8,69,1,256]{3,2,1,...) fusion(bf16[32,69,4,256]{3,2,1,0:T(4,128)(2,1)} %x_ref.7), kind=kLoop, calls=%fused_computation.84 | loop fusion | bytes 4521984 | tf_op jit(solution)/shard_map/slice | solution.py:331
  9.8 1.9 collective-permute-start
  12.5 3.6 %collective-permute-start.1 = (bf16[8,69,256]{2,1,0:T(8,128)(2,1)}, bf16[8,69,256]{2,1,0:T(8,128)(2,1)S(1)}, u32[]{:S(2)}, u32[]{:S(2)}) collective-permute-start(bf16[8,69,256]{2,1,0:T(8,128)(2,1)} %bitcast.96), channel_id=1, source_target_pairs={{1,0},{2,1},{3,2},{4,3},{5,4},{6,5},{7,6},{9,8},{10,9},{11,10},{12... | collective-permute-start | bytes 847880 | tf_op jit(solution)/shard_map/ppermute | solution.py:323
  17.1 1.9 collective-permute-start.5
  19.0 2.4 %collective-permute-start.4 = (bf16[8,69,256]{2,1,0:T(8,128)(2,1)}, bf16[8,69,256]{2,1,0:T(8,128)(2,1)S(1)}, u32[]{:S(2)}, u32[]{:S(2)}) collective-permute-start(bf16[8,69,256]{2,1,0:T(8,128)(2,1)} %get-tuple-element.50), channel_id=1, source_target_pairs={{0,1},{1,2},{2,3},{3,4},{4,5},{5,6},{6,7},{8,9},{9,10},{10,11},{11... | collective-permute-start | bytes 847880 | tf_op jit(solution)/shard_map/ppermute | solution.py:323
  21.6 1.2 pad.24
  24.0 7.3 %shard_map.100 = (bf16[8,4,72,256]{3,2,1,0:T(8,128)(2,1)S(1)}, bf16[8,72,256]{2,1,0:T(8,128)(2,1)S(1)}, bf16[8,72,256]{2,1,0:T(8,128)(2,1)}) custom-call(bf16[32,69,4,256]{3,2,1,0:T(4,128)(2,1)} %x_ref.7, bf16[8,69,256]{2,1,0:T(8,128)(2,1)S(1)} %collective-permute-done.low_ref, bf16[8,69,256]{2,1,0:T(8,128)(2,1)S(1)} %collective-permute-done.1.high_ref, ...), custom_call_target="tpu_custom_call" | custom-call | flops 1447034880 | bytes 3391488 | tf_op jit(solution)/shard_map/pallas_call | solution.py:288
  31.3 1.0 copy-done.14
  32.4 3.9 %collective-permute-start.2 = (bf16[8,72,256]{2,1,0:T(8,128)(2,1)}, bf16[8,72,256]{2,1,0:T(8,128)(2,1)S(1)}, u32[]{:S(2)}, u32[]{:S(2)}) collective-permute-start(bf16[8,72,256]{2,1,0:T(8,128)(2,1)} %get-tuple-element.48), channel_id=1, source_target_pairs={{0,1},{1,2},{2,3},{3,4},{4,5},{5,6},{6,7},{8,9},{9,10},{10,11},{11... | collective-permute-start | bytes 884744 | tf_op jit(solution)/shard_map/ppermute | solution.py:323
  36.3 1.9 collective-permute-start.3
  39.5 7.3 %shard_map.101 = (bf16[8,4,72,256]{3,2,1,0:T(8,128)(2,1)S(1)}, bf16[8,72,256]{2,1,0:T(8,128)(2,1)}, bf16[8,72,256]{2,1,0:T(8,128)(2,1)S(1)}) custom-call(bf16[32,69,4,256]{3,2,1,0:T(4,128)(2,1)} %x_ref.7, bf16[8,69,256]{2,1,0:T(8,128)(2,1)S(1)} %collective-permute-done.4.low_ref, bf16[8,69,256]{2,1,0:T(8,128)(2,1)S(1)} %collective-permute-done.5.high_ref, ...), custom_call_target="tpu_custom_call" | custom-call | flops 1447034880 | bytes 3391488 | tf_op jit(solution)/shard_map/pallas_call | solution.py:288
  46.8 1.1 copy-done.10
  50.2 8.1 %shard_map.102._.refs_0_ = bf16[4,69,2,8,128]{4,3,2,1,0:T(8,128)(2,1)} custom-call(bf16[8,4,72,256]{3,2,1,0:T(8,128)(2,1)S(1)} %copy-done.15, bf16[8,72,256]{2,1,0:T(8,128)(2,1)S(1)} %copy-done.20, bf16[8,72,256]{2,1,0:T(8,128)(2,1)} %collective-permute-done.3.high_ref, bf16[384,216]{1,0:T(8,128)(2,1)S(1)} %copy.41.mix_ref, f32[128,1]{1,0:T(8,128)S(1)} %copy.42.bias_ref, ...), custom_call_target="tpu_custom_call" | custom-call | flops 1447034880 | bytes 3391488 | tf_op jit(solution)/shard_map/pallas_call | solution.py:311
  58.4 5.0 %all-to-all-start = ((bf16[4,69,2,8,128]{4,3,2,1,0:T(8,128)(2,1)}), bf16[4,69,2,8,128]{4,3,2,1,0:T(8,128)(2,1)S(1)}, u32[]{:S(2)}, u32[]{:S(2)}) async-start(bf16[4,69,2,8,128]{4,3,2,1,0:T(8,128)(2,1)} %shard_map.102._.refs_0_), calls=%async_computation | async-start | bytes 2260992 | tf_op jit(solution)/shard_map/all_to_all | solution.py:326
  63.5 1.9 collective-permute-start.9
  65.4 2.4 %collective-permute-start.8 = (bf16[8,69,256]{2,1,0:T(8,128)(2,1)S(1)}, bf16[8,69,256]{2,1,0:T(8,128)(2,1)S(1)}, u32[]{:S(2)}, u32[]{:S(2)}) collective-permute-start(bf16[8,69,256]{2,1,0:T(8,128)(2,1)S(1)} %get-tuple-element.55), channel_id=1, source_target_pairs={{0,1},{1,2},{2,3},{3,4},{4,5},{5,6},{6,7},{8,9},{9,10},{10,11},{11... | collective-permute-start | bytes 847880 | tf_op jit(solution)/shard_map/ppermute | solution.py:323
  67.8 4.7 %collective-permute-start.6 = (bf16[8,72,256]{2,1,0:T(8,128)(2,1)S(1)}, bf16[8,72,256]{2,1,0:T(8,128)(2,1)S(1)}, u32[]{:S(2)}, u32[]{:S(2)}) collective-permute-start(bf16[8,72,256]{2,1,0:T(8,128)(2,1)S(1)} %copy-done.18), channel_id=1, source_target_pairs={{0,1},{1,2},{2,3},{3,4},{4,5},{5,6},{6,7},{8,9},{9,10},{10,11},{11... | collective-permute-start | bytes 884744 | tf_op jit(solution)/shard_map/ppermute | solution.py:323
  72.5 1.9 collective-permute-start.7
  74.5 7.2 %shard_map.103 = (bf16[8,4,72,256]{3,2,1,0:T(8,128)(2,1)S(1)}, bf16[8,72,256]{2,1,0:T(8,128)(2,1)}, bf16[8,72,256]{2,1,0:T(8,128)(2,1)S(1)}) custom-call(bf16[32,69,4,256]{3,2,1,0:T(4,128)(2,1)} %x_ref.7, bf16[8,69,256]{2,1,0:T(8,128)(2,1)S(1)} %collective-permute-done.8.low_ref, bf16[8,69,256]{2,1,0:T(8,128)(2,1)S(1)} %collective-permute-done.9.high_ref, ...), custom_call_target="tpu_custom_call" | custom-call | flops 1447034880 | bytes 3391488 | tf_op jit(solution)/shard_map/pallas_call | solution.py:288
  81.7 1.0 copy-done.8
  83.4 6.2 %shard_map.104._.refs_1_ = bf16[4,69,2,8,128]{4,3,2,1,0:T(8,128)(2,1)S(1)} custom-call(bf16[8,4,72,256]{3,2,1,0:T(8,128)(2,1)S(1)} %copy-done.11, bf16[8,72,256]{2,1,0:T(8,128)(2,1)S(1)} %collective-permute-done.6.low_ref, bf16[8,72,256]{2,1,0:T(8,128)(2,1)S(1)} %collective-permute-done.7.high_ref, bf16[384,216]{1,0:T(8,128)(2,1)S(1)} %copy.41.mix_ref, ...), custom_call_target="tpu_custom_call" | custom-call | flops 1447034880 | bytes 3391488 | tf_op jit(solution)/shard_map/pallas_call | solution.py:311
  89.6 1.0 copy-done
  91.5 4.4 %all-to-all-start.1 = ((bf16[4,69,2,8,128]{4,3,2,1,0:T(8,128)(2,1)}), bf16[4,69,2,8,128]{4,3,2,1,0:T(8,128)(2,1)S(1)}, u32[]{:S(2)}, u32[]{:S(2)}) async-start(bf16[4,69,2,8,128]{4,3,2,1,0:T(8,128)(2,1)} %copy-done), calls=%async_computation.1 | async-start | bytes 2260992 | tf_op jit(solution)/shard_map/all_to_all | solution.py:326
  95.9 2.0 copy_bitcast_fusion.1
  97.9 2.1 collective-permute-start.12
  100.0 3.4 %collective-permute-start.13 = (bf16[8,69,256]{2,1,0:T(8,128)(2,1)}, bf16[8,69,256]{2,1,0:T(8,128)(2,1)S(1)}, u32[]{:S(2)}, u32[]{:S(2)}) collective-permute-start(bf16[8,69,256]{2,1,0:T(8,128)(2,1)} %get-tuple-element.61), channel_id=1, source_target_pairs={{1,0},{2,1},{3,2},{4,3},{5,4},{6,5},{7,6},{9,8},{10,9},{11,10},{12... | collective-permute-start | bytes 847880 | tf_op jit(solution)/shard_map/ppermute | solution.py:323
  103.5 3.3 %collective-permute-start.10 = (bf16[8,72,256]{2,1,0:T(8,128)(2,1)}, bf16[8,72,256]{2,1,0:T(8,128)(2,1)}, u32[]{:S(2)}, u32[]{:S(2)}) collective-permute-start(bf16[8,72,256]{2,1,0:T(8,128)(2,1)} %copy-done.16), channel_id=1, source_target_pairs={{0,1},{1,2},{2,3},{3,4},{4,5},{5,6},{6,7},{8,9},{9,10},{10,11},{11... | collective-permute-start | bytes 884744 | tf_op jit(solution)/shard_map/ppermute | solution.py:323
  106.8 2.4 %collective-permute-start.11 = (bf16[8,72,256]{2,1,0:T(8,128)(2,1)}, bf16[8,72,256]{2,1,0:T(8,128)(2,1)}, u32[]{:S(2)}, u32[]{:S(2)}) collective-permute-start(bf16[8,72,256]{2,1,0:T(8,128)(2,1)} %get-tuple-element.57._), channel_id=1, source_target_pairs={{1,0},{2,1},{3,2},{4,3},{5,4},{6,5},{7,6},{9,8},{10,9},{11,10},{12... | collective-permute-start | bytes 884744 | tf_op jit(solution)/shard_map/ppermute | solution.py:323
  110.0 1.2 copy-done.1
  111.3 7.4 %shard_map.105 = (bf16[8,4,72,256]{3,2,1,0:T(8,128)(2,1)S(1)}, bf16[8,72,256]{2,1,0:T(8,128)(2,1)}, bf16[8,72,256]{2,1,0:T(8,128)(2,1)}) custom-call(bf16[32,69,4,256]{3,2,1,0:T(4,128)(2,1)} %x_ref.7, bf16[8,69,256]{2,1,0:T(8,128)(2,1)S(1)} %collective-permute-done.12.low_ref, bf16[8,69,256]{2,1,0:T(8,128)(2,1)S(1)} %collective-permute-done.13.high_ref, ...), custom_call_target="tpu_custom_call" | custom-call | flops 1447034880 | bytes 3391488 | tf_op jit(solution)/shard_map/pallas_call | solution.py:288
  118.7 1.1 copy-done.12
  119.8 6.2 %collective-permute-start.14 = (bf16[8,72,256]{2,1,0:T(8,128)(2,1)}, bf16[8,72,256]{2,1,0:T(8,128)(2,1)}, u32[]{:S(2)}, u32[]{:S(2)}) collective-permute-start(bf16[8,72,256]{2,1,0:T(8,128)(2,1)} %get-tuple-element.64), channel_id=1, source_target_pairs={{0,1},{1,2},{2,3},{3,4},{4,5},{5,6},{6,7},{8,9},{9,10},{10,11},{11... | collective-permute-start | bytes 884744 | tf_op jit(solution)/shard_map/ppermute | solution.py:323
  125.9 1.9 collective-permute-start.15
  127.9 7.2 %shard_map.106._.refs_0_ = bf16[4,69,2,8,128]{4,3,2,1,0:T(8,128)(2,1)S(1)} custom-call(bf16[8,4,72,256]{3,2,1,0:T(8,128)(2,1)S(1)} %copy-done.9, bf16[8,72,256]{2,1,0:T(8,128)(2,1)} %collective-permute-done.10.low_ref, bf16[8,72,256]{2,1,0:T(8,128)(2,1)} %collective-permute-done.11.high_ref, bf16[384,216]{1,0:T(8,128)(2,1)S(1)} %copy.41.mix_ref, ...), custom_call_target="tpu_custom_call" | custom-call | flops 1447034880 | bytes 3391488 | tf_op jit(solution)/shard_map/pallas_call | solution.py:311
  136.1 4.9 %all-to-all-start.2 = ((bf16[4,69,2,8,128]{4,3,2,1,0:T(8,128)(2,1)}), bf16[4,69,2,8,128]{4,3,2,1,0:T(8,128)(2,1)}, u32[]{:S(2)}, u32[]{:S(2)}) async-start(bf16[4,69,2,8,128]{4,3,2,1,0:T(8,128)(2,1)} %copy-done.3), calls=%async_computation.2 | async-start | bytes 2260992 | tf_op jit(solution)/shard_map/all_to_all | solution.py:326
  141.0 4.7 %shard_map.108 = bf16[16,1024]{1,0:T(8,128)(2,1)S(1)} custom-call(bf16[4,69,2,8,128]{4,3,2,1,0:T(8,128)(2,1)} %shard_map.102._.refs_0_, bf16[4,69,2,8,128]{4,3,2,1,0:T(8,128)(2,1)S(1)} %copy-done.2, s32[1,1024]{1,0:T(1,128)S(1)} %get-tuple-element.116.refs_2_, s32[1,1024]{1,0:T(1,128)S(1)} %get-tuple-element.115.refs_3_), custom_call_target="tpu_custom_call" | custom-call | flops 2315255808 | bytes 2260992 | tf_op jit(solution)/shard_map/pallas_call | solution.py:353
  145.8 8.2 %shard_map.107.refs_1_ = bf16[4,69,2,8,128]{4,3,2,1,0:T(8,128)(2,1)} custom-call(bf16[8,4,72,256]{3,2,1,0:T(8,128)(2,1)S(1)} %copy-done.13, bf16[8,72,256]{2,1,0:T(8,128)(2,1)} %collective-permute-done.14.low_ref, bf16[8,72,256]{2,1,0:T(8,128)(2,1)} %collective-permute-done.15.high_ref, bf16[384,216]{1,0:T(8,128)(2,1)S(1)} %copy-done.6, ...), custom_call_target="tpu_custom_call" | custom-call | flops 1447034880 | bytes 3391488 | tf_op jit(solution)/shard_map/pallas_call | solution.py:311
  154.0 4.6 %shard_map.109 = bf16[16,1024]{1,0:T(8,128)(2,1)S(1)} custom-call(bf16[4,69,2,8,128]{4,3,2,1,0:T(8,128)(2,1)S(1)} %copy-done.4, bf16[4,69,2,8,128]{4,3,2,1,0:T(8,128)(2,1)} %shard_map.107.refs_1_, s32[1,1024]{1,0:T(1,128)S(1)} %get-tuple-element.116.refs_2_, s32[1,1024]{1,0:T(1,128)S(1)} %get-tuple-element.115.refs_3_), custom_call_target="tpu_custom_call" | custom-call | flops 2315255808 | bytes 2260992 | tf_op jit(solution)/shard_map/pallas_call | solution.py:353
  158.6 18.7 %all-gather = bf16[128,1024]{1,0:T(8,128)(2,1)S(1)} all-gather(bf16[32,1024]{1,0:T(8,128)(2,1)S(1)} %pad_maximum_fusion.1), channel_id=2, replica_groups=mesh['mem'=4,'reg'=8] {'mem'}, dimensions={0}, use_global_device_ids=true | all-gather | bytes 327680 | tf_op jit(solution)/shard_map/all_gather | solution.py:367
  177.3 1.9 collective-permute-start.17
  179.2 2.4 %collective-permute-start.16 = (bf16[1,128,1024]{2,1,0:T(8,128)(2,1)S(1)}, bf16[1,128,1024]{2,1,0:T(8,128)(2,1)S(1)}, u32[]{:S(2)}, u32[]{:S(2)}) collective-permute-start(bf16[1,128,1024]{2,1,0:T(8,128)(2,1)S(1)} %bitcast.117), channel_id=1, source_target_pairs={{0,1},{1,2},{2,3},{3,4},{4,5},{5,6},{6,7},{8,9},{9,10},{10,11},{11... | collective-permute-start | bytes 786440 | tf_op jit(solution)/shard_map/ppermute | solution.py:372
  183.8 3.1 %collective-permute-done.16 = bf16[1,128,1024]{2,1,0:T(8,128)(2,1)S(1)} collective-permute-done((bf16[1,128,1024]{2,1,0:T(8,128)(2,1)S(1)}, bf16[1,128,1024]{2,1,0:T(8,128)(2,1)S(1)}, u32[]{:S(2)}, u32[]{:S(2)}) %collective-permute-start.16) | collective-permute-done | bytes 262176 | tf_op jit(solution)/shard_map/ppermute | solution.py:372
  187.2 2.3 %multiply_reduce_fusion = (f32[]{:T(128)}, f32[128,128]{1,0:T(8,128)S(1)}) fusion(f32[3,1024]{1,0:T(4,128)S(1)} %get-tuple-element.104, bf16[1,128,1024]{2,1,0:T(8,128)(2,1)S(1)} %collective-permute-done.17, bf16[1,128,1024]{2,1,0:T(8,128)(2,1)S(1)} %bitcast.119, bf16[1,128,1024]{2,1,0:T(8,128)(2,1)S(1)} %collective-permute-done.16, ...), kind=kOutput, calls=%fused_computation.38 | convolution fusion | flops 607600640 | bytes 876548 | tf_op jit(solution)/shard_map/dot_general | solution.py:225
  190.2 4.9 %all-to-all-start.3 = ((bf16[4,69,2,8,128]{4,3,2,1,0:T(8,128)(2,1)}), bf16[4,69,2,8,128]{4,3,2,1,0:T(8,128)(2,1)}, u32[]{:S(2)}, u32[]{:S(2)}) async-start(bf16[4,69,2,8,128]{4,3,2,1,0:T(8,128)(2,1)} %shard_map.107.refs_1_), calls=%async_computation.3 | async-start | bytes 2260992 | tf_op jit(solution)/shard_map/all_to_all | solution.py:326
  195.1 3.3 %while.13 = (s32[]{:T(128)}, f32[128,128]{0,1:T(8,128)S(1)}, f32[128,128]{1,0:T(8,128)S(1)}, s32[]{:T(128)}) while((s32[]{:T(128)}, f32[128,128]{0,1:T(8,128)S(1)}, f32[128,128]{1,0:T(8,128)S(1)}, s32[]{:T(128)}) %tuple.50), condition=%wide.region_3.4_spmd.clone, body=%wide.region_2.3_spmd.clone.sunk | while | flops 75563008 | bytes 852021 | solution.py:241
  198.4 1.4 fusion.19
  200.5 21.5 %all-to-all-done.3.refs_3_ = bf16[4,69,2,8,128]{4,3,2,1,0:T(8,128)(2,1)} async-done(((bf16[4,69,2,8,128]{4,3,2,1,0:T(8,128)(2,1)}), bf16[4,69,2,8,128]{4,3,2,1,0:T(8,128)(2,1)}, u32[]{:S(2)}, u32[]{:S(2)}) %all-to-all-start.3) | async-done | bytes 1130528 | tf_op jit(solution)/shard_map/all_to_all | solution.py:326
  221.9 5.9 %shard_map.110 = bf16[69,4,64,128]{3,2,1,0:T(8,128)(2,1)} custom-call(bf16[4,69,2,8,128]{4,3,2,1,0:T(8,128)(2,1)S(1)} %all-to-all-done.refs_0_, bf16[4,69,2,8,128]{4,3,2,1,0:T(8,128)(2,1)S(1)} %all-to-all-done.1.refs_1_, bf16[4,69,2,8,128]{4,3,2,1,0:T(8,128)(2,1)} %all-to-all-done.2.refs_2_, bf16[4,69,2,8,128]{4,3,2,1,0:T(8,128)(2,1)} %all-to-all-done.3.refs_3_, ...), custom_call_target="tpu_custom_call" | custom-call | flops 1157627904 | bytes 9043968 | tf_op jit(solution)/shard_map/pallas_call | solution.py:402
  (126 shorter events, 16.6 us)
Async XLA Ops:
  9.0 12.4 %copy-start.7 = (f32[2,128]{1,0:T(2,128)S(1)}, f32[2,128]{1,0:T(2,128)}, u32[]{:S(2)}) copy-start(f32[2,128]{1,0:T(2,128)} %_.1) | copy-start | bytes 3076
  9.0 12.4 %copy-start.25 = (bf16[2,69,128]{2,0,1:T(2,128)(2,1)S(1)}, bf16[2,69,128]{2,0,1:T(2,128)(2,1)}, u32[]{:S(2)}) copy-start(bf16[2,69,128]{2,0,1:T(2,128)(2,1)} %param.15) | copy-start | bytes 105988
  9.8 14.2 %collective-permute-start = (bf16[8,69,256]{2,1,0:T(8,128)(2,1)}, bf16[8,69,256]{2,1,0:T(8,128)(2,1)S(1)}, u32[]{:S(2)}, u32[]{:S(2)}) collective-permute-start(bf16[8,69,256]{2,1,0:T(8,128)(2,1)} %bitcast.97), channel_id=1, source_target_pairs={{0,1},{1,2},{2,3},{3,4},{4,5},{5,6},{6,7},{8,9},{9,10},{10,11},{11... | collective-permute-start | bytes 847880 | tf_op jit(solution)/shard_map/ppermute | solution.py:323
  12.5 11.5 %collective-permute-start.1 = (bf16[8,69,256]{2,1,0:T(8,128)(2,1)}, bf16[8,69,256]{2,1,0:T(8,128)(2,1)S(1)}, u32[]{:S(2)}, u32[]{:S(2)}) collective-permute-start(bf16[8,69,256]{2,1,0:T(8,128)(2,1)} %bitcast.96), channel_id=1, source_target_pairs={{1,0},{2,1},{3,2},{4,3},{5,4},{6,5},{7,6},{9,8},{10,9},{11,10},{12... | collective-permute-start | bytes 847880 | tf_op jit(solution)/shard_map/ppermute | solution.py:323
  17.1 22.4 %collective-permute-start.5 = (bf16[8,69,256]{2,1,0:T(8,128)(2,1)}, bf16[8,69,256]{2,1,0:T(8,128)(2,1)S(1)}, u32[]{:S(2)}, u32[]{:S(2)}) collective-permute-start(bf16[8,69,256]{2,1,0:T(8,128)(2,1)} %get-tuple-element.51), channel_id=1, source_target_pairs={{1,0},{2,1},{3,2},{4,3},{5,4},{6,5},{7,6},{9,8},{10,9},{11,10},{12... | collective-permute-start | bytes 847880 | tf_op jit(solution)/shard_map/ppermute | solution.py:323
  19.0 20.5 %collective-permute-start.4 = (bf16[8,69,256]{2,1,0:T(8,128)(2,1)}, bf16[8,69,256]{2,1,0:T(8,128)(2,1)S(1)}, u32[]{:S(2)}, u32[]{:S(2)}) collective-permute-start(bf16[8,69,256]{2,1,0:T(8,128)(2,1)} %get-tuple-element.50), channel_id=1, source_target_pairs={{0,1},{1,2},{2,3},{3,4},{4,5},{5,6},{6,7},{8,9},{9,10},{10,11},{11... | collective-permute-start | bytes 847880 | tf_op jit(solution)/shard_map/ppermute | solution.py:323
  31.3 1.0 copy-start.14
  32.4 16.2 %collective-permute-start.2 = (bf16[8,72,256]{2,1,0:T(8,128)(2,1)}, bf16[8,72,256]{2,1,0:T(8,128)(2,1)S(1)}, u32[]{:S(2)}, u32[]{:S(2)}) collective-permute-start(bf16[8,72,256]{2,1,0:T(8,128)(2,1)} %get-tuple-element.48), channel_id=1, source_target_pairs={{0,1},{1,2},{2,3},{3,4},{4,5},{5,6},{6,7},{8,9},{9,10},{10,11},{11... | collective-permute-start | bytes 884744 | tf_op jit(solution)/shard_map/ppermute | solution.py:323
  36.3 13.0 %collective-permute-start.3 = (bf16[8,72,256]{2,1,0:T(8,128)(2,1)S(1)}, bf16[8,72,256]{2,1,0:T(8,128)(2,1)}, u32[]{:S(2)}, u32[]{:S(2)}) collective-permute-start(bf16[8,72,256]{2,1,0:T(8,128)(2,1)S(1)} %get-tuple-element.49._), channel_id=1, source_target_pairs={{1,0},{2,1},{3,2},{4,3},{5,4},{6,5},{7,6},{9,8},{10,9},{11,10},{12... | collective-permute-start | bytes 884744 | tf_op jit(solution)/shard_map/ppermute | solution.py:323
  39.4 88.5 %copy-start.5 = (bf16[384,216]{1,0:T(8,128)(2,1)}, bf16[384,216]{1,0:T(8,128)(2,1)S(1)}, u32[]{:S(2)}) copy-start(bf16[384,216]{1,0:T(8,128)(2,1)S(1)} %copy.41.mix_ref) | copy-start | bytes 497668
  39.4 9.8 %copy-start.15 = (bf16[8,4,72,256]{3,2,1,0:T(8,128)(2,1)S(1)}, bf16[8,4,72,256]{3,2,1,0:T(8,128)(2,1)}, u32[]{:S(2)}) copy-start(bf16[8,4,72,256]{3,2,1,0:T(8,128)(2,1)} %copy-done.14) | copy-start | bytes 3538948
  46.8 1.1 copy-start.10
  58.3 5.0 %copy-start.22 = (bf16[8,69,1,256]{3,2,1,0:T(2,128)(2,1)S(1)}, bf16[8,69,1,256]{3,2,1,0:T(2,128)(2,1)}, u32[]{:S(2)}) copy-start(bf16[8,69,1,256]{3,2,1,0:T(2,128)(2,1)} %get-tuple-element.94) | copy-start | bytes 847876
  58.3 5.0 %copy-start.23 = (bf16[8,69,1,256]{3,2,1,0:T(2,128)(2,1)S(1)}, bf16[8,69,1,256]{3,2,1,0:T(2,128)(2,1)}, u32[]{:S(2)}) copy-start(bf16[8,69,1,256]{3,2,1,0:T(2,128)(2,1)} %get-tuple-element.95) | copy-start | bytes 847876
  58.3 9.5 %copy-start.18 = (bf16[8,72,256]{2,1,0:T(8,128)(2,1)S(1)}, bf16[8,72,256]{2,1,0:T(8,128)(2,1)}, u32[]{:S(2)}) copy-start(bf16[8,72,256]{2,1,0:T(8,128)(2,1)} %copy-done.17) | copy-start | bytes 884740
  58.4 33.1 %all-to-all-start = ((bf16[4,69,2,8,128]{4,3,2,1,0:T(8,128)(2,1)}), bf16[4,69,2,8,128]{4,3,2,1,0:T(8,128)(2,1)S(1)}, u32[]{:S(2)}, u32[]{:S(2)}) async-start(bf16[4,69,2,8,128]{4,3,2,1,0:T(8,128)(2,1)} %shard_map.102._.refs_0_), calls=%async_computation | async-start | bytes 2260992 | tf_op jit(solution)/shard_map/all_to_all | solution.py:326
  63.5 11.0 %collective-permute-start.9 = (bf16[8,69,256]{2,1,0:T(8,128)(2,1)S(1)}, bf16[8,69,256]{2,1,0:T(8,128)(2,1)S(1)}, u32[]{:S(2)}, u32[]{:S(2)}) collective-permute-start(bf16[8,69,256]{2,1,0:T(8,128)(2,1)S(1)} %get-tuple-element.56), channel_id=1, source_target_pairs={{1,0},{2,1},{3,2},{4,3},{5,4},{6,5},{7,6},{9,8},{10,9},{11,10},{12... | collective-permute-start | bytes 847880 | tf_op jit(solution)/shard_map/ppermute | solution.py:323
  65.4 9.1 %collective-permute-start.8 = (bf16[8,69,256]{2,1,0:T(8,128)(2,1)S(1)}, bf16[8,69,256]{2,1,0:T(8,128)(2,1)S(1)}, u32[]{:S(2)}, u32[]{:S(2)}) collective-permute-start(bf16[8,69,256]{2,1,0:T(8,128)(2,1)S(1)} %get-tuple-element.55), channel_id=1, source_target_pairs={{0,1},{1,2},{2,3},{3,4},{4,5},{5,6},{6,7},{8,9},{9,10},{10,11},{11... | collective-permute-start | bytes 847880 | tf_op jit(solution)/shard_map/ppermute | solution.py:323
  67.8 15.6 %copy-start.11 = (bf16[8,4,72,256]{3,2,1,0:T(8,128)(2,1)S(1)}, bf16[8,4,72,256]{3,2,1,0:T(8,128)(2,1)}, u32[]{:S(2)}) copy-start(bf16[8,4,72,256]{3,2,1,0:T(8,128)(2,1)} %copy-done.10) | copy-start | bytes 3538948
  67.8 14.9 %collective-permute-start.6 = (bf16[8,72,256]{2,1,0:T(8,128)(2,1)S(1)}, bf16[8,72,256]{2,1,0:T(8,128)(2,1)S(1)}, u32[]{:S(2)}, u32[]{:S(2)}) collective-permute-start(bf16[8,72,256]{2,1,0:T(8,128)(2,1)S(1)} %copy-done.18), channel_id=1, source_target_pairs={{0,1},{1,2},{2,3},{3,4},{4,5},{5,6},{6,7},{8,9},{9,10},{10,11},{11... | collective-permute-start | bytes 884744 | tf_op jit(solution)/shard_map/ppermute | solution.py:323
  72.5 10.2 %collective-permute-start.7 = (bf16[8,72,256]{2,1,0:T(8,128)(2,1)}, bf16[8,72,256]{2,1,0:T(8,128)(2,1)S(1)}, u32[]{:S(2)}, u32[]{:S(2)}) collective-permute-start(bf16[8,72,256]{2,1,0:T(8,128)(2,1)} %get-tuple-element.52._), channel_id=1, source_target_pairs={{1,0},{2,1},{3,2},{4,3},{5,4},{6,5},{7,6},{9,8},{10,9},{11,10},{12... | collective-permute-start | bytes 884744 | tf_op jit(solution)/shard_map/ppermute | solution.py:323
  81.7 1.0 copy-start.8
  89.6 1.0 copy-start
  90.6 5.2 %copy-start.21 = (bf16[8,69,1,256]{3,2,1,0:T(2,128)(2,1)S(1)}, bf16[8,69,1,256]{3,2,1,0:T(2,128)(2,1)}, u32[]{:S(2)}) copy-start(bf16[8,69,1,256]{3,2,1,0:T(2,128)(2,1)} %get-tuple-element.92) | copy-start | bytes 847876
  90.6 18.6 %copy-start.24 = (s32[8,1024]{1,0:T(8,128)S(1)}, s32[8,1024]{1,0:T(8,128)}, u32[]{:S(2)}) copy-start(s32[8,1024]{1,0:T(8,128)} %param.16) | copy-start | bytes 98308
  91.5 44.6 %all-to-all-start.1 = ((bf16[4,69,2,8,128]{4,3,2,1,0:T(8,128)(2,1)}), bf16[4,69,2,8,128]{4,3,2,1,0:T(8,128)(2,1)S(1)}, u32[]{:S(2)}, u32[]{:S(2)}) async-start(bf16[4,69,2,8,128]{4,3,2,1,0:T(8,128)(2,1)} %copy-done), calls=%async_computation.1 | async-start | bytes 2260992 | tf_op jit(solution)/shard_map/all_to_all | solution.py:326
  97.9 12.1 %collective-permute-start.12 = (bf16[8,69,256]{2,1,0:T(8,128)(2,1)}, bf16[8,69,256]{2,1,0:T(8,128)(2,1)S(1)}, u32[]{:S(2)}, u32[]{:S(2)}) collective-permute-start(bf16[8,69,256]{2,1,0:T(8,128)(2,1)} %get-tuple-element.60), channel_id=1, source_target_pairs={{0,1},{1,2},{2,3},{3,4},{4,5},{5,6},{6,7},{8,9},{9,10},{10,11},{11... | collective-permute-start | bytes 847880 | tf_op jit(solution)/shard_map/ppermute | solution.py:323
  100.0 10.0 %collective-permute-start.13 = (bf16[8,69,256]{2,1,0:T(8,128)(2,1)}, bf16[8,69,256]{2,1,0:T(8,128)(2,1)S(1)}, u32[]{:S(2)}, u32[]{:S(2)}) collective-permute-start(bf16[8,69,256]{2,1,0:T(8,128)(2,1)} %get-tuple-element.61), channel_id=1, source_target_pairs={{1,0},{2,1},{3,2},{4,3},{5,4},{6,5},{7,6},{9,8},{10,9},{11,10},{12... | collective-permute-start | bytes 847880 | tf_op jit(solution)/shard_map/ppermute | solution.py:323
  103.5 24.4 %collective-permute-start.10 = (bf16[8,72,256]{2,1,0:T(8,128)(2,1)}, bf16[8,72,256]{2,1,0:T(8,128)(2,1)}, u32[]{:S(2)}, u32[]{:S(2)}) collective-permute-start(bf16[8,72,256]{2,1,0:T(8,128)(2,1)} %copy-done.16), channel_id=1, source_target_pairs={{0,1},{1,2},{2,3},{3,4},{4,5},{5,6},{6,7},{8,9},{9,10},{10,11},{11... | collective-permute-start | bytes 884744 | tf_op jit(solution)/shard_map/ppermute | solution.py:323
  106.8 21.1 %collective-permute-start.11 = (bf16[8,72,256]{2,1,0:T(8,128)(2,1)}, bf16[8,72,256]{2,1,0:T(8,128)(2,1)}, u32[]{:S(2)}, u32[]{:S(2)}) collective-permute-start(bf16[8,72,256]{2,1,0:T(8,128)(2,1)} %get-tuple-element.57._), channel_id=1, source_target_pairs={{1,0},{2,1},{3,2},{4,3},{5,4},{6,5},{7,6},{9,8},{10,9},{11,10},{12... | collective-permute-start | bytes 884744 | tf_op jit(solution)/shard_map/ppermute | solution.py:323
  110.0 1.3 copy-start.1
  111.3 16.6 %copy-start.9 = (bf16[8,4,72,256]{3,2,1,0:T(8,128)(2,1)S(1)}, bf16[8,4,72,256]{3,2,1,0:T(8,128)(2,1)}, u32[]{:S(2)}) copy-start(bf16[8,4,72,256]{3,2,1,0:T(8,128)(2,1)} %copy-done.8) | copy-start | bytes 3538948
  118.7 1.1 copy-start.12
  119.8 26.0 %collective-permute-start.14 = (bf16[8,72,256]{2,1,0:T(8,128)(2,1)}, bf16[8,72,256]{2,1,0:T(8,128)(2,1)}, u32[]{:S(2)}, u32[]{:S(2)}) collective-permute-start(bf16[8,72,256]{2,1,0:T(8,128)(2,1)} %get-tuple-element.64), channel_id=1, source_target_pairs={{0,1},{1,2},{2,3},{3,4},{4,5},{5,6},{6,7},{8,9},{9,10},{10,11},{11... | collective-permute-start | bytes 884744 | tf_op jit(solution)/shard_map/ppermute | solution.py:323
  125.9 19.8 %collective-permute-start.15 = (bf16[8,72,256]{2,1,0:T(8,128)(2,1)}, bf16[8,72,256]{2,1,0:T(8,128)(2,1)}, u32[]{:S(2)}, u32[]{:S(2)}) collective-permute-start(bf16[8,72,256]{2,1,0:T(8,128)(2,1)} %get-tuple-element.62._), channel_id=1, source_target_pairs={{1,0},{2,1},{3,2},{4,3},{5,4},{6,5},{7,6},{9,8},{10,9},{11,10},{12... | collective-permute-start | bytes 884744 | tf_op jit(solution)/shard_map/ppermute | solution.py:323
  135.1 1.0 copy-start.3
  136.1 4.9 %copy-start.2 = (bf16[4,69,2,8,128]{4,3,2,1,0:T(8,128)(2,1)S(1)}, bf16[4,69,2,8,128]{4,3,2,1,0:T(8,128)(2,1)}, u32[]{:S(2)}) copy-start(bf16[4,69,2,8,128]{4,3,2,1,0:T(8,128)(2,1)} %copy-done) | copy-start | bytes 3391492
  136.1 54.1 %all-to-all-start.2 = ((bf16[4,69,2,8,128]{4,3,2,1,0:T(8,128)(2,1)}), bf16[4,69,2,8,128]{4,3,2,1,0:T(8,128)(2,1)}, u32[]{:S(2)}, u32[]{:S(2)}) async-start(bf16[4,69,2,8,128]{4,3,2,1,0:T(8,128)(2,1)} %copy-done.3), calls=%async_computation.2 | async-start | bytes 2260992 | tf_op jit(solution)/shard_map/all_to_all | solution.py:326
  141.0 4.8 %copy-start.4 = (bf16[4,69,2,8,128]{4,3,2,1,0:T(8,128)(2,1)S(1)}, bf16[4,69,2,8,128]{4,3,2,1,0:T(8,128)(2,1)}, u32[]{:S(2)}) copy-start(bf16[4,69,2,8,128]{4,3,2,1,0:T(8,128)(2,1)} %copy-done.3) | copy-start | bytes 3391492
  141.0 4.8 %copy-start.6 = (bf16[384,216]{1,0:T(8,128)(2,1)S(1)}, bf16[384,216]{1,0:T(8,128)(2,1)}, u32[]{:S(2)}) copy-start(bf16[384,216]{1,0:T(8,128)(2,1)} %copy-done.5) | copy-start | bytes 497668
  141.0 4.8 %copy-start.13 = (bf16[8,4,72,256]{3,2,1,0:T(8,128)(2,1)S(1)}, bf16[8,4,72,256]{3,2,1,0:T(8,128)(2,1)}, u32[]{:S(2)}) copy-start(bf16[8,4,72,256]{3,2,1,0:T(8,128)(2,1)} %copy-done.12) | copy-start | bytes 3538948
  154.0 27.7 %copy-start.29 = (s32[8]{0:T(128)S(1)}, s32[8]{0:T(128)}, u32[]{:S(2)}) copy-start(s32[8]{0:T(128)} %param.21) | copy-start | bytes 100
  154.0 28.9 %copy-start.28 = (s32[8]{0:T(128)S(1)}, s32[8]{0:T(128)}, u32[]{:S(2)}) copy-start(s32[8]{0:T(128)} %param.18) | copy-start | bytes 100
  154.0 33.1 %copy-start.26 = (f32[8,1024]{1,0:T(8,128)S(1)}, f32[8,1024]{1,0:T(8,128)}, u32[]{:S(2)}) copy-start(f32[8,1024]{1,0:T(8,128)} %param.19) | copy-start | bytes 98308
  154.0 33.1 %copy-start.27 = (f32[8,1024]{1,0:T(8,128)S(1)}, f32[8,1024]{1,0:T(8,128)}, u32[]{:S(2)}) copy-start(f32[8,1024]{1,0:T(8,128)} %param.20) | copy-start | bytes 98308
  177.3 6.5 %collective-permute-start.17 = (bf16[1,128,1024]{2,1,0:T(8,128)(2,1)S(1)}, bf16[1,128,1024]{2,1,0:T(8,128)(2,1)S(1)}, u32[]{:S(2)}, u32[]{:S(2)}) collective-permute-start(bf16[1,128,1024]{2,1,0:T(8,128)(2,1)S(1)} %bitcast.116), channel_id=1, source_target_pairs={{1,0},{2,1},{3,2},{4,3},{5,4},{6,5},{7,6},{9,8},{10,9},{11,10},{12... | collective-permute-start | bytes 786440 | tf_op jit(solution)/shard_map/ppermute | solution.py:374
  179.2 7.7 %collective-permute-start.16 = (bf16[1,128,1024]{2,1,0:T(8,128)(2,1)S(1)}, bf16[1,128,1024]{2,1,0:T(8,128)(2,1)S(1)}, u32[]{:S(2)}, u32[]{:S(2)}) collective-permute-start(bf16[1,128,1024]{2,1,0:T(8,128)(2,1)S(1)} %bitcast.117), channel_id=1, source_target_pairs={{0,1},{1,2},{2,3},{3,4},{4,5},{5,6},{6,7},{8,9},{9,10},{10,11},{11... | collective-permute-start | bytes 786440 | tf_op jit(solution)/shard_map/ppermute | solution.py:372
  190.2 31.7 %all-to-all-start.3 = ((bf16[4,69,2,8,128]{4,3,2,1,0:T(8,128)(2,1)}), bf16[4,69,2,8,128]{4,3,2,1,0:T(8,128)(2,1)}, u32[]{:S(2)}, u32[]{:S(2)}) async-start(bf16[4,69,2,8,128]{4,3,2,1,0:T(8,128)(2,1)} %shard_map.107.refs_1_), calls=%async_computation.3 | async-start | bytes 2260992 | tf_op jit(solution)/shard_map/all_to_all | solution.py:326
  (4 other events, 3.1 us)

commit v3 on v2

--- a/solution.py
+++ b/solution.py
@@ -46,39 +46,35 @@
     return results
 
 
-def first_kernel(x_ref, low_ref, high_ref, mix_ref, bias_ref, back_ref, _, y_ref, top_ref, bot_ref, scr):
+def forecast_kernel(
+    x_ref, low_ref, high_ref, live_ref, mix_ref, bias_ref, back_ref, _, z_ref, states, scr
+):
     fields, height = x_ref.shape[1], x_ref.shape[2]
-    scr[...] = jnp.zeros_like(scr)
+    group = z_ref.shape[3]
+    halo = low_ref.shape[2]
+    step = pl.program_id(0)
+    states[...] = jnp.zeros_like(states)
     for u in range(x_ref.shape[0]):
-        x = x_ref[u].astype(jnp.float32)
-        scr[u, 0, 0:fields, :] = low_ref[u].astype(jnp.float32)
-        scr[u, height + 1, 0:fields, :] = high_ref[u].astype(jnp.float32)
-        for p in range(height):
-            scr[u, p + 1, 0:fields, :] = x[:, p, :]
+        row = 0
+        for ref, count in ((low_ref, halo), (x_ref, height), (high_ref, halo)):
+            block = ref[u].astype(jnp.float32)
+            for p in range(count):
+                states[u, row, 0:fields, :] = block[:, p, :]
+                row += 1
     for u in range(x_ref.shape[0]):
-        rows = [scr[u, s] for s in range(height + 2)]
-        out = conv_rows(rows, mix_ref[...], bias_ref[...], back_ref[...])
-        for p in range(height):
-            y_ref[u, p] = out[p].astype(jnp.bfloat16)
-        top_ref[u] = out[0].astype(jnp.bfloat16)
-        bot_ref[u] = out[height - 1].astype(jnp.bfloat16)
-
-
-def second_kernel(y_ref, low_ref, high_ref, mix_ref, bias_ref, back_ref, _, z_ref, scr):
-    height = y_ref.shape[1]
-    group, fields = z_ref.shape[3], z_ref.shape[1]
-    step = pl.program_id(0)
-    for u in range(y_ref.shape[0]):
-        rows = [low_ref[u]] + [y_ref[u, p] for p in range(height)] + [high_ref[u]]
-        rows = [row.astype(jnp.float32) for row in rows]
-        out = conv_rows(rows, mix_ref[...], bias_ref[...], back_ref[...])
-        member = step * y_ref.shape[0] + u
+        rows = [states[u, s] for s in range(height + 2 * halo)]
+        rows = conv_rows(rows, mix_ref[0], bias_ref[0], back_ref[0])
+        rows = [row.astype(jnp.bfloat16).astype(jnp.float32) for row in rows]
+        rows[0] = rows[0] * live_ref[0:1, :]
+        rows[-1] = rows[-1] * live_ref[1:2, :]
+        out = conv_rows(rows, mix_ref[1], bias_ref[1], back_ref[1])
+        member = step * x_ref.shape[0] + u
         for p in range(height):
             for h in range(2):
                 scr[p, h, pl.ds(member, FPAD, stride=group), :] = out[p][:, h * 128 : (h + 1) * 128]
 
     @pl.when(step == pl.num_programs(0) - 1)
-    def _():
+    def store():
         span = (fields // 3) * group
         keep = lax.broadcasted_iota(jnp.int32, (span, 128), 1) < 64
         for part in range(3):
@@ -276,17 +272,15 @@
     flops = group * rows_here * lon_total * hid * fields * 20
     bf = jnp.bfloat16
     steps = group // STEP
-    weight_specs = [whole((3 * hid, 3 * FPAD)), whole((hid, 1)), whole((FPAD, hid))]
-    weight_specs = weight_specs + [pl.BlockSpec(memory_space=pl.ANY)]
-    edge = pl.BlockSpec((STEP, FPAD, lon_total), lambda i: (i, 0, 0))
-    middle = pl.BlockSpec((STEP, rows_here, FPAD, lon_total), lambda i: (i, 0, 0, 0))
-    outer = pl.BlockSpec((STEP, fields, lon_total), lambda i: (i, 0, 0))
+    halo = 2
+    live = jnp.stack([parallel_strip > 0, parallel_strip < lax.axis_size("reg") - 1])
+    live = jnp.broadcast_to(live.astype(jnp.float32)[:, None], (2, lon_total))
+    outer = pl.BlockSpec((STEP, fields, halo, lon_total), lambda i: (i, 0, 0, 0))
     zshape = (mem_count, fields, pairs, group, 128)
-    moved = group * 6 * fields * lon_total * 4
-
-    def first(c, edge_rows, previous):
+
+    def forecast(c, low, high, previous):
         return call(
-            first_kernel,
+            forecast_kernel,
             (steps,),
             [
                 pl.BlockSpec(
@@ -294,58 +288,38 @@
                 ),
                 outer,
                 outer,
-            ]
-            + weight_specs,
-            [
-                jax.ShapeDtypeStruct((group, rows_here, FPAD, lon_total), bf),
-                jax.ShapeDtypeStruct((group, FPAD, lon_total), bf),
-                jax.ShapeDtypeStruct((group, FPAD, lon_total), bf),
+                whole(live.shape),
+                whole(mixes.shape),
+                whole(biases.shape),
+                whole(backs.shape),
+                pl.BlockSpec(memory_space=pl.ANY),
             ],
-            [middle, edge, edge],
-            [pltpu.VMEM((STEP, rows_here + 2, FPAD, lon_total), jnp.float32)],
-            flops,
-            moved,
-        )(prior_sample_set, *edge_rows, mixes[0], biases[0], backs[0], previous)
-
-    def second(state, edge_rows, previous):
-        return call(
-            second_kernel,
-            (steps,),
-            [middle, edge, edge] + weight_specs,
             jax.ShapeDtypeStruct(zshape, bf),
             whole(zshape),
-            [pltpu.VMEM((rows_here, 2, FPAD * group, 128), jnp.float32)],
-            flops,
-            moved,
-        )(state, *edge_rows, mixes[1], biases[1], backs[1], previous)
-
-    def exchange(bottom, top):
-        return lax.ppermute(bottom, "reg", forward), lax.ppermute(top, "reg", backward)
+            [
+                pltpu.VMEM((STEP, rows_here + 2 * halo, FPAD, lon_total), jnp.float32),
+                pltpu.VMEM((rows_here, 2, FPAD * group, 128), jnp.float32),
+            ],
+            flops * 5 // 2,
+            group * 12 * fields * lon_total * 2,
+        )(prior_sample_set, low, high, live, mixes, biases, backs, previous)
 
     def spread(z):
         return lax.all_to_all(z, "mem", split_axis=0, concat_axis=0, tiled=True)
 
-    outer_edges, ends = [], None
+    edges = []
     for c in range(CHUNKS):
         own = prior_sample_set[c * group : (c + 1) * group]
-        bottom, top = own[:, :, rows_here - 1, :], own[:, :, 0, :]
-        if ends is not None:
-            bottom, top, _ = lax.optimization_barrier((bottom, top, ends))
-        ends = bottom
-        outer_edges.append(exchange(bottom, top))
-    firsts, parts, arrived = [], [], []
+        low = lax.ppermute(own[:, :, rows_here - halo :, :], "reg", forward)
+        high = lax.ppermute(own[:, :, :halo, :], "reg", backward)
+        edges.append((low, high))
+    parts, arrived = [], []
     previous = bias_in
-    order = [(0, 0), (0, 1)] + [(1 - n % 2, n // 2 + (2 if n % 2 else 0)) for n in range(2 * CHUNKS - 4)]
-    for layer, c in order + [(1, CHUNKS - 2), (1, CHUNKS - 1)]:
-        if layer == 0:
-            state, top, bottom = first(c, outer_edges[c], previous)
-            firsts.append((state, exchange(bottom, top)))
-            previous = top
-        else:
-            parts.append(second(*firsts[c], previous))
-            previous = parts[-1]
-            if c < CHUNKS - 1:
-                arrived.append(spread(parts[-1]))
+    for c in range(CHUNKS):
+        parts.append(forecast(c, *edges[c], previous))
+        previous = parts[-1]
+        if c < CHUNKS - 1:
+            arrived.append(spread(parts[-1]))
     field_row = lax.dynamic_slice_in_dim(sensor_position_variable, parallel_strip, 1, 0)
     cell_row = lax.dynamic_slice_in_dim(observed_cell, parallel_strip, 1, 0)
     picked = jnp.concatenate(

time: 229 us -> 238 us (1.039)
  starting transfers between devices: 69.4 us -> 38.2 us
  blocking collectives: 18.7 us -> 47.4 us
  waiting for transfers between devices: 26.4 us -> 47.9 us
  Pallas kernels: 74.2 us -> 64.4 us
  local copies, waits for them, and re-layouts: 29.4 us -> 24.1 us
  other arithmetic: 0.61 us -> 3.17 us
  matrix products: 7.1 us -> 9.57 us
    all_to_all x0 -> x1, blocking collectives: none -> 32.5 us  [spread(): return lax.all_to_all(z, 'mem', split_axis=0, concat_axis=0, tiled=True)]
    ppermute x16 -> x8, starting transfers between devices: 46 us -> 21.5 us  [the longest x4 11.6 us: body(): low = lax.ppermute(own[:, :, rows_here - halo:, :], 'reg', forward)]
    all_to_all x4 -> x3, waiting for transfers between devices: 22.3 us -> 43.6 us  [spread(): return lax.all_to_all(z, 'mem', split_axis=0, concat_axis=0, tiled=True)]
    all_to_all x4 -> x3, starting transfers between devices: 19.2 us -> 12.3 us  [spread(): return lax.all_to_all(z, 'mem', split_axis=0, concat_axis=0, tiled=True)]
    pallas_call x8 -> x4, Pallas kernels: 58.9 us -> 52.3 us  [forecast(): call(forecast_kernel, (steps,), [pl.BlockSpec((STEP, fields, rows_here, l...]
    all_gather x1, blocking collectives: 18.7 us -> 14.9 us  [body(): every_member = lax.all_gather(picked[None], 'mem', axis=1, tiled=True)]
    squeeze x9 -> x0, local copies, waits for them, and re-layouts: 3.59 us -> none  [the longest x3 3.07 us: body(): bottom, top = (own[:, :, rows_here - 1, :], own[:, :, 0, :])]
    pallas_call x2, Pallas kernels: 9.32 us -> 6.65 us  [body(): call(sample_kernel, (1,), [whole(zshape)] * 2 + [whole((1, slots)), whole...]
  transfers between devices with their start and end apart: 22 -> 13, of which waited for: 4 -> 4; matrix products, arithmetic and copies ran while one was open for 7% -> 7% of each run, Pallas kernels for 26% -> 19%
where the time goes in v3:
time: 238 us; the launch traced here: 237 us
  Pallas kernels  64.4 us (27%)
  waiting for transfers between devices  47.9 us (20%)
  blocking collectives  47.4 us (20%)
  starting transfers between devices  38.2 us (16%)
  local copies, waits for them, and re-layouts  24.1 us (10%)
  matrix products  9.57 us (4%)
  other arithmetic  3.17 us (1%)
    pallas_call x4, Pallas kernels, forecast(): call(forecast_kernel, (steps,), [pl.BlockSpec((STEP, fields, rows_here, l...  52.3 us
    all_to_all x3, waiting for transfers between devices, spread(): return lax.all_to_all(z, 'mem', split_axis=0, concat_axis=0, tiled=True)  43.6 us
    all_to_all x1, blocking collectives, spread(): return lax.all_to_all(z, 'mem', split_axis=0, concat_axis=0, tiled=True)  32.5 us
    all_gather x1, blocking collectives, body(): every_member = lax.all_gather(picked[None], 'mem', axis=1, tiled=True)  14.9 us
    unnamed x56, local copies, waits for them, and re-layouts  12.6 us
    all_to_all x3, starting transfers between devices, spread(): return lax.all_to_all(z, 'mem', split_axis=0, concat_axis=0, tiled=True)  12.3 us
    ppermute x4, starting transfers between devices, body(): low = lax.ppermute(own[:, :, rows_here - halo:, :], 'reg', forward)  11.6 us
    ppermute x4, starting transfers between devices, body(): high = lax.ppermute(own[:, :, :halo, :], 'reg', backward)  9.92 us
  transfers between devices with their start and end apart: 13, of which 4 were waited for; matrix products, arithmetic and copies ran while one was open for 7% of the time, Pallas kernels for 19%

profile of v3, /device:TPU:2, one launch (start us, length us, event | category | flops | bytes accessed | tf_op | source)
XLA Modules:
  0.0 236.8 jit_solution(16141172827541760547)
XLA Ops:
  0.0 8.9 %fusion.47 = (bf16[8,69,2,256]{3,2,1,0:T(2,128)(2,1)}, bf16[8,69,2,256]{3,2,1,0:T(2,128)(2,1)}, bf16[8,69,2,256]{3,2,1,0:T(2,128)(2,1)}, bf16[8,69,2,256]{3,2,1,...) fusion(bf16[32,69,4,256]{3,2,1,0:T(4,128)(2,1)} %x_ref.7), kind=kLoop, calls=%fused_computation.69 | loop fusion | bytes 9043968 | tf_op jit(solution)/shard_map/slice | solution.py:314
  8.9 1.9 collective-permute-start.1
  10.8 2.4 %collective-permute-start = (bf16[8,69,2,256]{3,2,1,0:T(2,128)(2,1)S(1)}, bf16[8,69,2,256]{3,2,1,0:T(2,128)(2,1)S(1)}, u32[]{:S(2)}, u32[]{:S(2)}) collective-permute-start(bf16[8,69,2,256]{3,2,1,0:T(2,128)(2,1)S(1)} %get-tuple-element.63), channel_id=1, source_target_pairs={{0,1},{1,2},{2,3},{3,4},{4,5},{5,6},{6,7},{8,9},{9,10},{10,11},{11... | collective-permute-start | bytes 1695752 | tf_op jit(solution)/shard_map/ppermute | solution.py:313
  13.2 3.2 %collective-permute-start.3 = (bf16[8,69,2,256]{3,2,1,0:T(2,128)(2,1)}, bf16[8,69,2,256]{3,2,1,0:T(2,128)(2,1)S(1)}, u32[]{:S(2)}, u32[]{:S(2)}) collective-permute-start(bf16[8,69,2,256]{3,2,1,0:T(2,128)(2,1)} %get-tuple-element.60), channel_id=1, source_target_pairs={{1,0},{2,1},{3,2},{4,3},{5,4},{6,5},{7,6},{9,8},{10,9},{11,10},{12... | collective-permute-start | bytes 1695752 | tf_op jit(solution)/shard_map/ppermute | solution.py:314
  16.4 2.6 %collective-permute-start.2 = (bf16[8,69,2,256]{3,2,1,0:T(2,128)(2,1)}, bf16[8,69,2,256]{3,2,1,0:T(2,128)(2,1)}, u32[]{:S(2)}, u32[]{:S(2)}) collective-permute-start(bf16[8,69,2,256]{3,2,1,0:T(2,128)(2,1)} %get-tuple-element.61), channel_id=1, source_target_pairs={{0,1},{1,2},{2,3},{3,4},{4,5},{5,6},{6,7},{8,9},{9,10},{10,11},{11... | collective-permute-start | bytes 1695752 | tf_op jit(solution)/shard_map/ppermute | solution.py:313
  19.1 2.9 %collective-permute-start.5 = (bf16[8,69,2,256]{3,2,1,0:T(2,128)(2,1)}, bf16[8,69,2,256]{3,2,1,0:T(2,128)(2,1)}, u32[]{:S(2)}, u32[]{:S(2)}) collective-permute-start(bf16[8,69,2,256]{3,2,1,0:T(2,128)(2,1)} %get-tuple-element.58), channel_id=1, source_target_pairs={{1,0},{2,1},{3,2},{4,3},{5,4},{6,5},{7,6},{9,8},{10,9},{11,10},{12... | collective-permute-start | bytes 1695752 | tf_op jit(solution)/shard_map/ppermute | solution.py:314
  23.2 0.9 copy-done.17
  24.1 3.8 %collective-permute-start.4 = (bf16[8,69,2,256]{3,2,1,0:T(2,128)(2,1)}, bf16[8,69,2,256]{3,2,1,0:T(2,128)(2,1)S(1)}, u32[]{:S(2)}, u32[]{:S(2)}) collective-permute-start(bf16[8,69,2,256]{3,2,1,0:T(2,128)(2,1)} %get-tuple-element.59), channel_id=1, source_target_pairs={{0,1},{1,2},{2,3},{3,4},{4,5},{5,6},{6,7},{8,9},{9,10},{10,11},{11... | collective-permute-start | bytes 1695752 | tf_op jit(solution)/shard_map/ppermute | solution.py:313
  27.9 0.8 copy-done.19
  28.8 1.1 copy-done.18
  29.9 1.1 copy-done.20
  30.9 12.8 %shard_map.100._.refs_0_ = bf16[4,69,2,8,128]{4,3,2,1,0:T(8,128)(2,1)S(1)} custom-call(bf16[32,69,4,256]{3,2,1,0:T(4,128)(2,1)} %x_ref.7, bf16[8,69,2,256]{3,2,1,0:T(2,128)(2,1)S(1)} %copy-done.20, bf16[8,69,2,256]{3,2,1,0:T(2,128)(2,1)S(1)} %copy-done.18, f32[2,256]{1,0:T(2,128)S(1)} %broadcast_in_dim.9.live_ref, bf16[2,384,216]{2,1,0:T(8,128)(2,1)S(1)} %copy.17.mix_ref, ...), custom_call_target="tpu_custom_call" | custom-call | flops 3617587200 | bytes 3391488 | tf_op jit(solution)/shard_map/pallas_call | solution.py:282
  43.8 0.8 copy-done.15
  44.6 1.0 copy-done.9
  45.6 0.8 copy-done.12
  46.4 1.1 copy-done.16
  47.5 13.0 %shard_map.101._.refs_1_ = bf16[4,69,2,8,128]{4,3,2,1,0:T(8,128)(2,1)S(1)} custom-call(bf16[32,69,4,256]{3,2,1,0:T(4,128)(2,1)} %x_ref.7, bf16[8,69,2,256]{3,2,1,0:T(2,128)(2,1)} %collective-permute-done.2.low_ref, bf16[8,69,2,256]{3,2,1,0:T(2,128)(2,1)S(1)} %copy-done.16, f32[2,256]{1,0:T(2,128)S(1)} %broadcast_in_dim.9.live_ref, ...), custom_call_target="tpu_custom_call" | custom-call | flops 3617587200 | bytes 3391488 | tf_op jit(solution)/shard_map/pallas_call | solution.py:282
  60.6 13.4 %shard_map.102._.refs_0_ = bf16[4,69,2,8,128]{4,3,2,1,0:T(8,128)(2,1)S(1)} custom-call(bf16[32,69,4,256]{3,2,1,0:T(4,128)(2,1)} %x_ref.7, bf16[8,69,2,256]{3,2,1,0:T(2,128)(2,1)S(1)} %collective-permute-done.4.low_ref, bf16[8,69,2,256]{3,2,1,0:T(2,128)(2,1)} %collective-permute-done.5.high_ref, f32[2,256]{1,0:T(2,128)S(1)} %broadcast_in_dim.9.live_ref, ...), custom_call_target="tpu_custom_call" | custom-call | flops 3617587200 | bytes 3391488 | tf_op jit(solution)/shard_map/pallas_call | solution.py:282
  74.0 32.5 %all_to_all.20.refs_2_ = bf16[4,69,2,8,128]{4,3,2,1,0:T(8,128)(2,1)S(1)} all-to-all(bf16[4,69,2,8,128]{4,3,2,1,0:T(8,128)(2,1)S(1)} %shard_map.102._.refs_0_), channel_id=1, replica_groups=mesh['mem'=4,'reg'=8] {'mem'}, dimensions={0} | all-to-all | bytes 2260992 | tf_op jit(solution)/shard_map/all_to_all | solution.py:308
  106.6 1.0 copy-done.5
  107.6 3.5 %all-to-all-start.1 = ((bf16[4,69,2,8,128]{4,3,2,1,0:T(8,128)(2,1)}), bf16[4,69,2,8,128]{4,3,2,1,0:T(8,128)(2,1)S(1)}, u32[]{:S(2)}, u32[]{:S(2)}) async-start(bf16[4,69,2,8,128]{4,3,2,1,0:T(8,128)(2,1)} %copy-done.3), calls=%async_computation.1 | async-start | bytes 2260992 | tf_op jit(solution)/shard_map/all_to_all | solution.py:308
  111.1 1.9 collective-permute-start.7
  113.0 2.8 %collective-permute-start.6 = (bf16[8,69,2,256]{3,2,1,0:T(2,128)(2,1)}, bf16[8,69,2,256]{3,2,1,0:T(2,128)(2,1)}, u32[]{:S(2)}, u32[]{:S(2)}) collective-permute-start(bf16[8,69,2,256]{3,2,1,0:T(2,128)(2,1)} %get-tuple-element.57), channel_id=1, source_target_pairs={{0,1},{1,2},{2,3},{3,4},{4,5},{5,6},{6,7},{8,9},{9,10},{10,11},{11... | collective-permute-start | bytes 1695752 | tf_op jit(solution)/shard_map/ppermute | solution.py:313
  115.8 0.8 constant_dynamic-slice_fusion
  116.6 23.2 %all-to-all-done.1.refs_1_ = bf16[4,69,2,8,128]{4,3,2,1,0:T(8,128)(2,1)S(1)} async-done(((bf16[4,69,2,8,128]{4,3,2,1,0:T(8,128)(2,1)}), bf16[4,69,2,8,128]{4,3,2,1,0:T(8,128)(2,1)S(1)}, u32[]{:S(2)}, u32[]{:S(2)}) %all-to-all-start.1) | async-done | bytes 1130528 | tf_op jit(solution)/shard_map/all_to_all | solution.py:308
  139.8 3.7 %all-to-all-start = ((bf16[4,69,2,8,128]{4,3,2,1,0:T(8,128)(2,1)}), bf16[4,69,2,8,128]{4,3,2,1,0:T(8,128)(2,1)S(1)}, u32[]{:S(2)}, u32[]{:S(2)}) async-start(bf16[4,69,2,8,128]{4,3,2,1,0:T(8,128)(2,1)} %copy-done.1), calls=%async_computation | async-start | bytes 2260992 | tf_op jit(solution)/shard_map/all_to_all | solution.py:308
  143.6 1.4 copy-done.6
  145.0 1.0 copy-done.10
  146.0 0.8 copy-done.13
  146.8 12.9 %shard_map.103.refs_1_ = bf16[4,69,2,8,128]{4,3,2,1,0:T(8,128)(2,1)S(1)} custom-call(bf16[32,69,4,256]{3,2,1,0:T(4,128)(2,1)} %x_ref.7, bf16[8,69,2,256]{3,2,1,0:T(2,128)(2,1)} %collective-permute-done.6.low_ref, bf16[8,69,2,256]{3,2,1,0:T(2,128)(2,1)} %collective-permute-done.7.high_ref, f32[2,256]{1,0:T(2,128)S(1)} %broadcast_in_dim.9.live_ref, ...), custom_call_target="tpu_custom_call" | custom-call | flops 3617587200 | bytes 3391488 | tf_op jit(solution)/shard_map/pallas_call | solution.py:282
  159.8 3.3 %shard_map.104 = bf16[16,1024]{1,0:T(8,128)(2,1)S(1)} custom-call(bf16[4,69,2,8,128]{4,3,2,1,0:T(8,128)(2,1)S(1)} %copy-done.2, bf16[4,69,2,8,128]{4,3,2,1,0:T(8,128)(2,1)S(1)} %copy-done.4, s32[1,1024]{1,0:T(1,128)S(1)} %get-tuple-element.68.refs_2_, s32[1,1024]{1,0:T(1,128)S(1)} %get-tuple-element.67.refs_3_), custom_call_target="tpu_custom_call" | custom-call | flops 2315255808 | bytes 2260992 | tf_op jit(solution)/shard_map/pallas_call | solution.py:327
  163.2 3.3 %shard_map.105 = bf16[16,1024]{1,0:T(8,128)(2,1)S(1)} custom-call(bf16[4,69,2,8,128]{4,3,2,1,0:T(8,128)(2,1)S(1)} %copy-done.7, bf16[4,69,2,8,128]{4,3,2,1,0:T(8,128)(2,1)S(1)} %shard_map.103.refs_1_, s32[1,1024]{1,0:T(1,128)S(1)} %get-tuple-element.68.refs_2_, s32[1,1024]{1,0:T(1,128)S(1)} %get-tuple-element.67.refs_3_), custom_call_target="tpu_custom_call" | custom-call | flops 2315255808 | bytes 2260992 | tf_op jit(solution)/shard_map/pallas_call | solution.py:327
  166.5 14.9 %all-gather = bf16[128,1024]{1,0:T(8,128)(2,1)} all-gather(bf16[32,1024]{1,0:T(8,128)(2,1)S(1)} %pad_maximum_fusion.1), channel_id=2, replica_groups=mesh['mem'=4,'reg'=8] {'mem'}, dimensions={0}, use_global_device_ids=true | all-gather | bytes 327680 | tf_op jit(solution)/shard_map/all_gather | solution.py:341
  181.4 1.9 collective-permute-start.9
  183.4 2.4 %collective-permute-start.8 = (bf16[1,128,1024]{2,1,0:T(8,128)(2,1)}, bf16[1,128,1024]{2,1,0:T(8,128)(2,1)}, u32[]{:S(2)}, u32[]{:S(2)}) collective-permute-start(bf16[1,128,1024]{2,1,0:T(8,128)(2,1)} %bitcast.5), channel_id=1, source_target_pairs={{0,1},{1,2},{2,3},{3,4},{4,5},{5,6},{6,7},{8,9},{9,10},{10,11},{11... | collective-permute-start | bytes 786440 | tf_op jit(solution)/shard_map/ppermute | solution.py:346
  185.8 0.6 dynamic_slice.25
  187.1 1.3 collective-permute-done.9
  188.4 3.0 %collective-permute-done.8 = bf16[1,128,1024]{2,1,0:T(8,128)(2,1)} collective-permute-done((bf16[1,128,1024]{2,1,0:T(8,128)(2,1)}, bf16[1,128,1024]{2,1,0:T(8,128)(2,1)}, u32[]{:S(2)}, u32[]{:S(2)}) %collective-permute-start.8) | collective-permute-done | bytes 262176 | tf_op jit(solution)/shard_map/ppermute | solution.py:346
  191.4 1.3 convert_reduce_fusion
  192.6 0.9 fusion.40
  193.5 3.7 %multiply_reduce_fusion = (f32[]{:T(128)}, f32[128,128]{1,0:T(8,128)S(1)}) fusion(f32[3,1024]{1,0:T(4,128)S(1)} %get-tuple-element.64, bf16[1,128,1024]{2,1,0:T(8,128)(2,1)} %collective-permute-done.9, bf16[1,128,1024]{2,1,0:T(8,128)(2,1)} %bitcast.5, bf16[1,128,1024]{2,1,0:T(8,128)(2,1)} %collective-permute-done.8, f32[3,1024]{1,0:T(4,128)S(1)} %get-tuple-element.55), kind=kOutput, calls=%fused_computation.28 | convolution fusion | flops 607600640 | bytes 876548 | tf_op jit(solution)/shard_map/dot_general | solution.py:221
  197.8 0.6 broadcast_divide_fusion
  198.5 0.9 copy.25
  199.4 5.1 %all-to-all-start.3 = ((bf16[4,69,2,8,128]{4,3,2,1,0:T(8,128)(2,1)}), bf16[4,69,2,8,128]{4,3,2,1,0:T(8,128)(2,1)}, u32[]{:S(2)}, u32[]{:S(2)}) async-start(bf16[4,69,2,8,128]{4,3,2,1,0:T(8,128)(2,1)} %copy-done), calls=%async_computation.3 | async-start | bytes 2260992 | tf_op jit(solution)/shard_map/all_to_all | solution.py:308
  204.5 3.3 %while.13 = (s32[]{:T(128)}, f32[128,128]{0,1:T(8,128)S(1)}, f32[128,128]{1,0:T(8,128)S(1)}, s32[]{:T(128)}) while((s32[]{:T(128)}, f32[128,128]{0,1:T(8,128)S(1)}, f32[128,128]{1,0:T(8,128)S(1)}, s32[]{:T(128)}) %tuple.38), condition=%wide.region_3.4_spmd.clone, body=%wide.region_2.3_spmd.clone.sunk | while | flops 75563008 | bytes 852021 | solution.py:237
  207.8 2.5 %fusion.19 = f32[128,1]{0,1:T(1,128)S(1)} fusion(f32[3,1024]{1,0:T(4,128)S(1)} %get-tuple-element.64, f32[3,1024,1]{1,0,2:T(4,128)S(1)} %get-tuple-element.54, bf16[1,128,1024]{2,1,0:T(8,128)(2,1)} %collective-permute-done.9, bf16[1,128,1024]{2,1,0:T(8,128)(2,1)} %bitcast.5, bf16[1,128,1024]{2,1,0:T(8,128)(2,1)} %collective-permute-done.8), kind=kOutput, calls=%fused_computation.15 | convolution fusion | flops 6291456 | bytes 811520 | tf_op jit(solution)/shard_map/dot_general | solution.py:239
  210.9 20.4 %all-to-all-done.3.refs_3_ = bf16[4,69,2,8,128]{4,3,2,1,0:T(8,128)(2,1)} async-done(((bf16[4,69,2,8,128]{4,3,2,1,0:T(8,128)(2,1)}), bf16[4,69,2,8,128]{4,3,2,1,0:T(8,128)(2,1)}, u32[]{:S(2)}, u32[]{:S(2)}) %all-to-all-start.3) | async-done | bytes 1130528 | tf_op jit(solution)/shard_map/all_to_all | solution.py:308
  231.3 5.5 %shard_map.106 = bf16[69,4,64,128]{3,2,1,0:T(8,128)(2,1)} custom-call(bf16[4,69,2,8,128]{4,3,2,1,0:T(8,128)(2,1)S(1)} %all-to-all-done.refs_0_, bf16[4,69,2,8,128]{4,3,2,1,0:T(8,128)(2,1)S(1)} %all-to-all-done.1.refs_1_, bf16[4,69,2,8,128]{4,3,2,1,0:T(8,128)(2,1)S(1)} %all_to_all.20.refs_2_, bf16[4,69,2,8,128]{4,3,2,1,0:T(8,128)(2,1)} %all-to-all-done.3.refs_3_, ...), custom_call_target="tpu_custom_call" | custom-call | flops 1157627904 | bytes 9043968 | tf_op jit(solution)/shard_map/pallas_call | solution.py:376
  (91 shorter events, 5.1 us)
Async XLA Ops:
  0.0 22.0 %copy-start.23 = (bf16[2,69,128]{2,0,1:T(2,128)(2,1)S(1)}, bf16[2,69,128]{2,0,1:T(2,128)(2,1)}, u32[]{:S(2)}) copy-start(bf16[2,69,128]{2,0,1:T(2,128)(2,1)} %param.15) | copy-start | bytes 105988
  0.0 22.0 %copy-start.14 = (f32[2,128]{1,0:T(2,128)S(1)}, f32[2,128]{1,0:T(2,128)}, u32[]{:S(2)}) copy-start(f32[2,128]{1,0:T(2,128)} %_.1) | copy-start | bytes 3076
  0.0 22.2 %copy-start.21 = (bf16[2,9,128,69]{2,0,3,1:T(2,128)(2,1)S(1)}, bf16[2,9,128,69]{2,0,3,1:T(2,128)(2,1)}, u32[]{:S(2)}) copy-start(bf16[2,9,128,69]{2,0,3,1:T(2,128)(2,1)} %param.13) | copy-start | bytes 953860
  8.9 14.3 %collective-permute-start.1 = (bf16[8,69,2,256]{3,2,1,0:T(2,128)(2,1)}, bf16[8,69,2,256]{3,2,1,0:T(2,128)(2,1)S(1)}, u32[]{:S(2)}, u32[]{:S(2)}) collective-permute-start(bf16[8,69,2,256]{3,2,1,0:T(2,128)(2,1)} %get-tuple-element.62), channel_id=1, source_target_pairs={{1,0},{2,1},{3,2},{4,3},{5,4},{6,5},{7,6},{9,8},{10,9},{11,10},{12... | collective-permute-start | bytes 1695752 | tf_op jit(solution)/shard_map/ppermute | solution.py:314
  10.8 17.1 %collective-permute-start = (bf16[8,69,2,256]{3,2,1,0:T(2,128)(2,1)S(1)}, bf16[8,69,2,256]{3,2,1,0:T(2,128)(2,1)S(1)}, u32[]{:S(2)}, u32[]{:S(2)}) collective-permute-start(bf16[8,69,2,256]{3,2,1,0:T(2,128)(2,1)S(1)} %get-tuple-element.63), channel_id=1, source_target_pairs={{0,1},{1,2},{2,3},{3,4},{4,5},{5,6},{6,7},{8,9},{9,10},{10,11},{11... | collective-permute-start | bytes 1695752 | tf_op jit(solution)/shard_map/ppermute | solution.py:313
  13.2 30.5 %collective-permute-start.3 = (bf16[8,69,2,256]{3,2,1,0:T(2,128)(2,1)}, bf16[8,69,2,256]{3,2,1,0:T(2,128)(2,1)S(1)}, u32[]{:S(2)}, u32[]{:S(2)}) collective-permute-start(bf16[8,69,2,256]{3,2,1,0:T(2,128)(2,1)} %get-tuple-element.60), channel_id=1, source_target_pairs={{1,0},{2,1},{3,2},{4,3},{5,4},{6,5},{7,6},{9,8},{10,9},{11,10},{12... | collective-permute-start | bytes 1695752 | tf_op jit(solution)/shard_map/ppermute | solution.py:314
  16.4 28.2 %collective-permute-start.2 = (bf16[8,69,2,256]{3,2,1,0:T(2,128)(2,1)}, bf16[8,69,2,256]{3,2,1,0:T(2,128)(2,1)}, u32[]{:S(2)}, u32[]{:S(2)}) collective-permute-start(bf16[8,69,2,256]{3,2,1,0:T(2,128)(2,1)} %get-tuple-element.61), channel_id=1, source_target_pairs={{0,1},{1,2},{2,3},{3,4},{4,5},{5,6},{6,7},{8,9},{9,10},{10,11},{11... | collective-permute-start | bytes 1695752 | tf_op jit(solution)/shard_map/ppermute | solution.py:313
  19.1 41.5 %collective-permute-start.5 = (bf16[8,69,2,256]{3,2,1,0:T(2,128)(2,1)}, bf16[8,69,2,256]{3,2,1,0:T(2,128)(2,1)}, u32[]{:S(2)}, u32[]{:S(2)}) collective-permute-start(bf16[8,69,2,256]{3,2,1,0:T(2,128)(2,1)} %get-tuple-element.58), channel_id=1, source_target_pairs={{1,0},{2,1},{3,2},{4,3},{5,4},{6,5},{7,6},{9,8},{10,9},{11,10},{12... | collective-permute-start | bytes 1695752 | tf_op jit(solution)/shard_map/ppermute | solution.py:314
  22.2 21.6 %copy-start.11 = (bf16[2,72,128]{2,1,0:T(8,128)(2,1)}, bf16[2,72,128]{2,1,0:T(8,128)(2,1)S(1)}, u32[]{:S(2)}) copy-start(bf16[2,72,128]{2,1,0:T(8,128)(2,1)S(1)} %pad.25.back_ref) | copy-start | bytes 110596
  23.1 20.6 %copy-start.8 = (bf16[2,384,216]{2,1,0:T(8,128)(2,1)}, bf16[2,384,216]{2,1,0:T(8,128)(2,1)S(1)}, u32[]{:S(2)}) copy-start(bf16[2,384,216]{2,1,0:T(8,128)(2,1)S(1)} %copy.17.mix_ref) | copy-start | bytes 995332
  23.2 0.9 copy-start.17
  24.1 36.4 %collective-permute-start.4 = (bf16[8,69,2,256]{3,2,1,0:T(2,128)(2,1)}, bf16[8,69,2,256]{3,2,1,0:T(2,128)(2,1)S(1)}, u32[]{:S(2)}, u32[]{:S(2)}) collective-permute-start(bf16[8,69,2,256]{3,2,1,0:T(2,128)(2,1)} %get-tuple-element.59), channel_id=1, source_target_pairs={{0,1},{1,2},{2,3},{3,4},{4,5},{5,6},{6,7},{8,9},{9,10},{10,11},{11... | collective-permute-start | bytes 1695752 | tf_op jit(solution)/shard_map/ppermute | solution.py:313
  27.9 0.8 copy-start.19
  28.8 1.1 copy-start.18
  29.9 1.1 copy-start.20
  43.8 16.7 %copy-start.1 = (bf16[4,69,2,8,128]{4,3,2,1,0:T(8,128)(2,1)}, bf16[4,69,2,8,128]{4,3,2,1,0:T(8,128)(2,1)S(1)}, u32[]{:S(2)}) copy-start(bf16[4,69,2,8,128]{4,3,2,1,0:T(8,128)(2,1)S(1)} %shard_map.100._.refs_0_) | copy-start | bytes 3391492
  43.8 0.8 copy-start.15
  44.6 1.0 copy-start.9
  45.6 0.8 copy-start.12
  46.4 1.1 copy-start.16
  60.5 13.5 %copy-start.3 = (bf16[4,69,2,8,128]{4,3,2,1,0:T(8,128)(2,1)}, bf16[4,69,2,8,128]{4,3,2,1,0:T(8,128)(2,1)S(1)}, u32[]{:S(2)}) copy-start(bf16[4,69,2,8,128]{4,3,2,1,0:T(8,128)(2,1)S(1)} %shard_map.101._.refs_1_) | copy-start | bytes 3391492
  106.5 1.0 copy-start.5
  107.6 32.3 %all-to-all-start.1 = ((bf16[4,69,2,8,128]{4,3,2,1,0:T(8,128)(2,1)}), bf16[4,69,2,8,128]{4,3,2,1,0:T(8,128)(2,1)S(1)}, u32[]{:S(2)}, u32[]{:S(2)}) async-start(bf16[4,69,2,8,128]{4,3,2,1,0:T(8,128)(2,1)} %copy-done.3), calls=%async_computation.1 | async-start | bytes 2260992 | tf_op jit(solution)/shard_map/all_to_all | solution.py:308
  111.1 32.5 %collective-permute-start.7 = (bf16[8,69,2,256]{3,2,1,0:T(2,128)(2,1)}, bf16[8,69,2,256]{3,2,1,0:T(2,128)(2,1)}, u32[]{:S(2)}, u32[]{:S(2)}) collective-permute-start(bf16[8,69,2,256]{3,2,1,0:T(2,128)(2,1)} %get-tuple-element.56), channel_id=1, source_target_pairs={{1,0},{2,1},{3,2},{4,3},{5,4},{6,5},{7,6},{9,8},{10,9},{11,10},{12... | collective-permute-start | bytes 1695752 | tf_op jit(solution)/shard_map/ppermute | solution.py:314
  113.0 30.6 %collective-permute-start.6 = (bf16[8,69,2,256]{3,2,1,0:T(2,128)(2,1)}, bf16[8,69,2,256]{3,2,1,0:T(2,128)(2,1)}, u32[]{:S(2)}, u32[]{:S(2)}) collective-permute-start(bf16[8,69,2,256]{3,2,1,0:T(2,128)(2,1)} %get-tuple-element.57), channel_id=1, source_target_pairs={{0,1},{1,2},{2,3},{3,4},{4,5},{5,6},{6,7},{8,9},{9,10},{10,11},{11... | collective-permute-start | bytes 1695752 | tf_op jit(solution)/shard_map/ppermute | solution.py:313
  139.8 59.6 %all-to-all-start = ((bf16[4,69,2,8,128]{4,3,2,1,0:T(8,128)(2,1)}), bf16[4,69,2,8,128]{4,3,2,1,0:T(8,128)(2,1)S(1)}, u32[]{:S(2)}, u32[]{:S(2)}) async-start(bf16[4,69,2,8,128]{4,3,2,1,0:T(8,128)(2,1)} %copy-done.1), calls=%async_computation | async-start | bytes 2260992 | tf_op jit(solution)/shard_map/all_to_all | solution.py:308
  143.6 16.2 %copy-start.2 = (bf16[4,69,2,8,128]{4,3,2,1,0:T(8,128)(2,1)S(1)}, bf16[4,69,2,8,128]{4,3,2,1,0:T(8,128)(2,1)}, u32[]{:S(2)}) copy-start(bf16[4,69,2,8,128]{4,3,2,1,0:T(8,128)(2,1)} %copy-done.1) | copy-start | bytes 3391492
  143.6 16.2 %copy-start.4 = (bf16[4,69,2,8,128]{4,3,2,1,0:T(8,128)(2,1)S(1)}, bf16[4,69,2,8,128]{4,3,2,1,0:T(8,128)(2,1)}, u32[]{:S(2)}) copy-start(bf16[4,69,2,8,128]{4,3,2,1,0:T(8,128)(2,1)} %copy-done.3) | copy-start | bytes 3391492
  143.6 1.4 copy-start.6
  145.0 1.0 copy-start.10
  146.0 0.8 copy-start.13
  159.7 3.4 %copy-start = (bf16[4,69,2,8,128]{4,3,2,1,0:T(8,128)(2,1)}, bf16[4,69,2,8,128]{4,3,2,1,0:T(8,128)(2,1)S(1)}, u32[]{:S(2)}) copy-start(bf16[4,69,2,8,128]{4,3,2,1,0:T(8,128)(2,1)S(1)} %shard_map.103.refs_1_) | copy-start | bytes 3391492
  159.8 3.4 %copy-start.7 = (bf16[4,69,2,8,128]{4,3,2,1,0:T(8,128)(2,1)S(1)}, bf16[4,69,2,8,128]{4,3,2,1,0:T(8,128)(2,1)}, u32[]{:S(2)}) copy-start(bf16[4,69,2,8,128]{4,3,2,1,0:T(8,128)(2,1)} %copy-done.5) | copy-start | bytes 3391492
  163.1 22.7 %copy-start.26 = (s32[8]{0:T(128)S(1)}, s32[8]{0:T(128)}, u32[]{:S(2)}) copy-start(s32[8]{0:T(128)} %param.21) | copy-start | bytes 100
  163.1 23.9 %copy-start.25 = (s32[8]{0:T(128)S(1)}, s32[8]{0:T(128)}, u32[]{:S(2)}) copy-start(s32[8]{0:T(128)} %param.18) | copy-start | bytes 100
  163.2 29.5 %copy-start.22 = (s32[8,1024]{1,0:T(8,128)S(1)}, s32[8,1024]{1,0:T(8,128)}, u32[]{:S(2)}) copy-start(s32[8,1024]{1,0:T(8,128)} %param.16) | copy-start | bytes 98308
  163.2 29.5 %copy-start.24 = (f32[8,1024]{1,0:T(8,128)S(1)}, f32[8,1024]{1,0:T(8,128)}, u32[]{:S(2)}) copy-start(f32[8,1024]{1,0:T(8,128)} %param.19) | copy-start | bytes 98308
  181.4 7.0 %collective-permute-start.9 = (bf16[1,128,1024]{2,1,0:T(8,128)(2,1)}, bf16[1,128,1024]{2,1,0:T(8,128)(2,1)}, u32[]{:S(2)}, u32[]{:S(2)}) collective-permute-start(bf16[1,128,1024]{2,1,0:T(8,128)(2,1)} %bitcast.5), channel_id=1, source_target_pairs={{1,0},{2,1},{3,2},{4,3},{5,4},{6,5},{7,6},{9,8},{10,9},{11,10},{12... | collective-permute-start | bytes 786440 | tf_op jit(solution)/shard_map/ppermute | solution.py:348
  183.4 8.0 %collective-permute-start.8 = (bf16[1,128,1024]{2,1,0:T(8,128)(2,1)}, bf16[1,128,1024]{2,1,0:T(8,128)(2,1)}, u32[]{:S(2)}, u32[]{:S(2)}) collective-permute-start(bf16[1,128,1024]{2,1,0:T(8,128)(2,1)} %bitcast.5), channel_id=1, source_target_pairs={{0,1},{1,2},{2,3},{3,4},{4,5},{5,6},{6,7},{8,9},{9,10},{10,11},{11... | collective-permute-start | bytes 786440 | tf_op jit(solution)/shard_map/ppermute | solution.py:346
  199.4 31.9 %all-to-all-start.3 = ((bf16[4,69,2,8,128]{4,3,2,1,0:T(8,128)(2,1)}), bf16[4,69,2,8,128]{4,3,2,1,0:T(8,128)(2,1)}, u32[]{:S(2)}, u32[]{:S(2)}) async-start(bf16[4,69,2,8,128]{4,3,2,1,0:T(8,128)(2,1)} %copy-done), calls=%async_computation.3 | async-start | bytes 2260992 | tf_op jit(solution)/shard_map/all_to_all | solution.py:308

commit v4 on v3

--- a/solution.py
+++ b/solution.py
@@ -317,9 +317,9 @@
     previous = bias_in
     for c in range(CHUNKS):
         parts.append(forecast(c, *edges[c], previous))
-        previous = parts[-1]
         if c < CHUNKS - 1:
             arrived.append(spread(parts[-1]))
+        previous = arrived[c - 1] if c > 0 else parts[0]
     field_row = lax.dynamic_slice_in_dim(sensor_position_variable, parallel_strip, 1, 0)
     cell_row = lax.dynamic_slice_in_dim(observed_cell, parallel_strip, 1, 0)
     picked = jnp.concatenate(

time: 238 us -> 211 us (0.89)
  blocking collectives: 47.4 us -> 18.7 us
  starting transfers between devices: 38.2 us -> 49.5 us
  waiting for transfers between devices: 47.9 us -> 39 us
  local copies, waits for them, and re-layouts: 24.1 us -> 16.6 us
  Pallas kernels: 64.4 us -> 68.2 us
    all_to_all x1 -> x0, blocking collectives: 32.5 us -> none  [spread(): return lax.all_to_all(z, 'mem', split_axis=0, concat_axis=0, tiled=True)]
    all_to_all x3 -> x4, waiting for transfers between devices: 43.6 us -> 22.1 us  [spread(): return lax.all_to_all(z, 'mem', split_axis=0, concat_axis=0, tiled=True)]
    ppermute x4, waiting for transfers between devices: 0.01 us -> 9.15 us  [body(): high = lax.ppermute(own[:, :, :halo, :], 'reg', backward)]
    unnamed x56 -> x36, local copies, waits for them, and re-layouts: 12.6 us -> 4.51 us
    ppermute x4, starting transfers between devices: 11.6 us -> 19.1 us  [body(): low = lax.ppermute(own[:, :, rows_here - halo:, :], 'reg', forward)]
    all_to_all x3 -> x4, starting transfers between devices: 12.3 us -> 18.3 us  [spread(): return lax.all_to_all(z, 'mem', split_axis=0, concat_axis=0, tiled=True)]
    ppermute x4, waiting for transfers between devices: 0.01 us -> 4.93 us  [body(): low = lax.ppermute(own[:, :, rows_here - halo:, :], 'reg', forward)]
    all_gather x1, blocking collectives: 14.9 us -> 18.7 us  [body(): every_member = lax.all_gather(picked[None], 'mem', axis=1, tiled=True)]
  transfers between devices with their start and end apart: 13 -> 14, of which waited for: 4 -> 7; matrix products, arithmetic and copies ran while one was open for 7% -> 8% of each run, Pallas kernels for 19% -> 23%
where the time goes in v4:
time: 211 us; the launch traced here: 207 us
  Pallas kernels  68.2 us (32%)
  starting transfers between devices  49.5 us (23%)
  waiting for transfers between devices  39 us (18%)
  blocking collectives  18.7 us (9%)
  local copies, waits for them, and re-layouts  16.6 us (8%)
  matrix products  9.63 us (5%)
  other arithmetic  3.86 us (2%)
    pallas_call x4, Pallas kernels, forecast(): call(forecast_kernel, (steps,), [pl.BlockSpec((STEP, fields, rows_here, l...  54.4 us
    all_to_all x4, waiting for transfers between devices, spread(): return lax.all_to_all(z, 'mem', split_axis=0, concat_axis=0, tiled=True)  22.1 us
    ppermute x4, starting transfers between devices, body(): low = lax.ppermute(own[:, :, rows_here - halo:, :], 'reg', forward)  19.1 us
    all_gather x1, blocking collectives, body(): every_member = lax.all_gather(picked[None], 'mem', axis=1, tiled=True)  18.7 us
    all_to_all x4, starting transfers between devices, spread(): return lax.all_to_all(z, 'mem', split_axis=0, concat_axis=0, tiled=True)  18.3 us
    ppermute x4, waiting for transfers between devices, body(): high = lax.ppermute(own[:, :, :halo, :], 'reg', backward)  9.15 us
    slice x1, local copies, waits for them, and re-layouts, body(): high = lax.ppermute(own[:, :, :halo, :], 'reg', backward)  8.83 us
    pallas_call x2, Pallas kernels, body(): call(sample_kernel, (1,), [whole(zshape)] * 2 + [whole((1, slots)), whole...  8.24 us
  transfers between devices with their start and end apart: 14, of which 7 were waited for; matrix products, arithmetic and copies ran while one was open for 8% of the time, Pallas kernels for 23%

profile of v4, /device:TPU:2, one launch (start us, length us, event | category | flops | bytes accessed | tf_op | source)
XLA Modules:
  0.0 207.5 jit_solution(6565404187076577457)
XLA Ops:
  0.0 8.8 %fusion.47 = (bf16[8,69,2,256]{3,2,1,0:T(2,128)(2,1)}, bf16[8,69,2,256]{3,2,1,0:T(2,128)(2,1)}, bf16[8,69,2,256]{3,2,1,0:T(2,128)(2,1)}, bf16[8,69,2,256]{3,2,1,...) fusion(bf16[32,69,4,256]{3,2,1,0:T(4,128)(2,1)} %x_ref.7), kind=kLoop, calls=%fused_computation.69 | loop fusion | bytes 9043968 | tf_op jit(solution)/shard_map/slice | solution.py:314
  8.8 1.9 collective-permute-start.1
  10.8 2.4 %collective-permute-start = (bf16[8,69,2,256]{3,2,1,0:T(2,128)(2,1)}, bf16[8,69,2,256]{3,2,1,0:T(2,128)(2,1)S(1)}, u32[]{:S(2)}, u32[]{:S(2)}) collective-permute-start(bf16[8,69,2,256]{3,2,1,0:T(2,128)(2,1)} %get-tuple-element.63), channel_id=1, source_target_pairs={{0,1},{1,2},{2,3},{3,4},{4,5},{5,6},{6,7},{8,9},{9,10},{10,11},{11... | collective-permute-start | bytes 1695752 | tf_op jit(solution)/shard_map/ppermute | solution.py:313
  13.8 0.3 reshape.59
  14.4 6.1 %collective-permute-done.1.high_ref = bf16[8,69,2,256]{3,2,1,0:T(2,128)(2,1)S(1)} collective-permute-done((bf16[8,69,2,256]{3,2,1,0:T(2,128)(2,1)}, bf16[8,69,2,256]{3,2,1,0:T(2,128)(2,1)S(1)}, u32[]{:S(2)}, u32[]{:S(2)}) %collective-permute-start.1) | collective-permute-done | bytes 565280 | tf_op jit(solution)/shard_map/ppermute | solution.py:314
  20.5 1.4 collective-permute-done.low_ref
  22.0 14.0 %shard_map.100._.refs_0_ = bf16[4,69,2,8,128]{4,3,2,1,0:T(8,128)(2,1)} custom-call(bf16[32,69,4,256]{3,2,1,0:T(4,128)(2,1)} %x_ref.7, bf16[8,69,2,256]{3,2,1,0:T(2,128)(2,1)S(1)} %collective-permute-done.low_ref, bf16[8,69,2,256]{3,2,1,0:T(2,128)(2,1)S(1)} %collective-permute-done.1.high_ref, f32[2,256]{1,0:T(2,128)S(1)} %broadcast_in_dim.9.live_ref, ...), custom_call_target="tpu_custom_call" | custom-call | flops 3617587200 | bytes 3391488 | tf_op jit(solution)/shard_map/pallas_call | solution.py:282
  36.0 4.9 %all-to-all-start = ((bf16[4,69,2,8,128]{4,3,2,1,0:T(8,128)(2,1)}), bf16[4,69,2,8,128]{4,3,2,1,0:T(8,128)(2,1)S(1)}, u32[]{:S(2)}, u32[]{:S(2)}) async-start(bf16[4,69,2,8,128]{4,3,2,1,0:T(8,128)(2,1)} %shard_map.100._.refs_0_), calls=%async_computation | async-start | bytes 2260992 | tf_op jit(solution)/shard_map/all_to_all | solution.py:308
  40.9 2.0 collective-permute-start.3
  42.9 4.4 %collective-permute-start.2 = (bf16[8,69,2,256]{3,2,1,0:T(2,128)(2,1)S(1)}, bf16[8,69,2,256]{3,2,1,0:T(2,128)(2,1)S(1)}, u32[]{:S(2)}, u32[]{:S(2)}) collective-permute-start(bf16[8,69,2,256]{3,2,1,0:T(2,128)(2,1)S(1)} %get-tuple-element.61), channel_id=1, source_target_pairs={{0,1},{1,2},{2,3},{3,4},{4,5},{5,6},{6,7},{8,9},{9,10},{10,11},{11... | collective-permute-start | bytes 1695752 | tf_op jit(solution)/shard_map/ppermute | solution.py:313
  47.3 3.1 %collective-permute-done.3.high_ref = bf16[8,69,2,256]{3,2,1,0:T(2,128)(2,1)S(1)} collective-permute-done((bf16[8,69,2,256]{3,2,1,0:T(2,128)(2,1)}, bf16[8,69,2,256]{3,2,1,0:T(2,128)(2,1)S(1)}, u32[]{:S(2)}, u32[]{:S(2)}) %collective-permute-start.3) | collective-permute-done | bytes 565280 | tf_op jit(solution)/shard_map/ppermute | solution.py:314
  50.3 3.5 %collective-permute-done.2.low_ref = bf16[8,69,2,256]{3,2,1,0:T(2,128)(2,1)S(1)} collective-permute-done((bf16[8,69,2,256]{3,2,1,0:T(2,128)(2,1)S(1)}, bf16[8,69,2,256]{3,2,1,0:T(2,128)(2,1)S(1)}, u32[]{:S(2)}, u32[]{:S(2)}) %collective-permute-start.2) | collective-permute-done | bytes 565280 | tf_op jit(solution)/shard_map/ppermute | solution.py:313
  53.8 14.0 %shard_map.101.refs_1_ = bf16[4,69,2,8,128]{4,3,2,1,0:T(8,128)(2,1)} custom-call(bf16[32,69,4,256]{3,2,1,0:T(4,128)(2,1)} %x_ref.7, bf16[8,69,2,256]{3,2,1,0:T(2,128)(2,1)S(1)} %collective-permute-done.2.low_ref, bf16[8,69,2,256]{3,2,1,0:T(2,128)(2,1)S(1)} %collective-permute-done.3.high_ref, f32[2,256]{1,0:T(2,128)S(1)} %broadcast_in_dim.9.live_ref, ...), custom_call_target="tpu_custom_call" | custom-call | flops 3617587200 | bytes 3391488 | tf_op jit(solution)/shard_map/pallas_call | solution.py:282
  67.8 0.9 all-to-all-done._.refs_0_
  68.7 4.1 %all-to-all-start.1 = ((bf16[4,69,2,8,128]{4,3,2,1,0:T(8,128)(2,1)}), bf16[4,69,2,8,128]{4,3,2,1,0:T(8,128)(2,1)S(1)}, u32[]{:S(2)}, u32[]{:S(2)}) async-start(bf16[4,69,2,8,128]{4,3,2,1,0:T(8,128)(2,1)} %shard_map.101.refs_1_), calls=%async_computation.1 | async-start | bytes 2260992 | tf_op jit(solution)/shard_map/all_to_all | solution.py:308
  72.8 1.9 collective-permute-start.5
  74.8 7.6 %collective-permute-start.4 = (bf16[8,69,2,256]{3,2,1,0:T(2,128)(2,1)}, bf16[8,69,2,256]{3,2,1,0:T(2,128)(2,1)}, u32[]{:S(2)}, u32[]{:S(2)}) collective-permute-start(bf16[8,69,2,256]{3,2,1,0:T(2,128)(2,1)} %get-tuple-element.59), channel_id=1, source_target_pairs={{0,1},{1,2},{2,3},{3,4},{4,5},{5,6},{6,7},{8,9},{9,10},{10,11},{11... | collective-permute-start | bytes 1695752 | tf_op jit(solution)/shard_map/ppermute | solution.py:313
  82.4 1.9 collective-permute-start.7
  84.3 4.7 %collective-permute-start.6 = (bf16[8,69,2,256]{3,2,1,0:T(2,128)(2,1)}, bf16[8,69,2,256]{3,2,1,0:T(2,128)(2,1)}, u32[]{:S(2)}, u32[]{:S(2)}) collective-permute-start(bf16[8,69,2,256]{3,2,1,0:T(2,128)(2,1)} %get-tuple-element.57), channel_id=1, source_target_pairs={{0,1},{1,2},{2,3},{3,4},{4,5},{5,6},{6,7},{8,9},{9,10},{10,11},{11... | collective-permute-start | bytes 1695752 | tf_op jit(solution)/shard_map/ppermute | solution.py:313
  89.0 0.8 constant_dynamic-slice_fusion
  89.9 4.9 %shard_map.104 = bf16[16,1024]{1,0:T(8,128)(2,1)S(1)} custom-call(bf16[4,69,2,8,128]{4,3,2,1,0:T(8,128)(2,1)} %shard_map.100._.refs_0_, bf16[4,69,2,8,128]{4,3,2,1,0:T(8,128)(2,1)} %shard_map.101.refs_1_, s32[1,1024]{1,0:T(1,128)S(1)} %get-tuple-element.68.refs_2_, s32[1,1024]{1,0:T(1,128)S(1)} %get-tuple-element.67.refs_3_), custom_call_target="tpu_custom_call" | custom-call | flops 2315255808 | bytes 2260992 | tf_op jit(solution)/shard_map/pallas_call | solution.py:327
  94.8 13.1 %shard_map.102.refs_0_ = bf16[4,69,2,8,128]{4,3,2,1,0:T(8,128)(2,1)S(1)} custom-call(bf16[32,69,4,256]{3,2,1,0:T(4,128)(2,1)} %x_ref.7, bf16[8,69,2,256]{3,2,1,0:T(2,128)(2,1)} %collective-permute-done.4.low_ref, bf16[8,69,2,256]{3,2,1,0:T(2,128)(2,1)S(1)} %collective-permute-done.5.high_ref, f32[2,256]{1,0:T(2,128)S(1)} %broadcast_in_dim.9.live_ref, ...), custom_call_target="tpu_custom_call" | custom-call | flops 3617587200 | bytes 3391488 | tf_op jit(solution)/shard_map/pallas_call | solution.py:282
  108.0 1.0 copy-done.1
  108.9 4.8 %all-to-all-start.2 = ((bf16[4,69,2,8,128]{4,3,2,1,0:T(8,128)(2,1)}), bf16[4,69,2,8,128]{4,3,2,1,0:T(8,128)(2,1)S(1)}, u32[]{:S(2)}, u32[]{:S(2)}) async-start(bf16[4,69,2,8,128]{4,3,2,1,0:T(8,128)(2,1)} %copy-done.1), calls=%async_computation.2 | async-start | bytes 2260992 | tf_op jit(solution)/shard_map/all_to_all | solution.py:308
  113.8 1.1 copy-done.4
  114.9 0.8 copy-done.6
  115.6 0.7 copy-done.12
  116.3 13.3 %shard_map.103.refs_1_ = bf16[4,69,2,8,128]{4,3,2,1,0:T(8,128)(2,1)S(1)} custom-call(bf16[32,69,4,256]{3,2,1,0:T(4,128)(2,1)} %x_ref.7, bf16[8,69,2,256]{3,2,1,0:T(2,128)(2,1)} %collective-permute-done.6.low_ref, bf16[8,69,2,256]{3,2,1,0:T(2,128)(2,1)} %collective-permute-done.7.high_ref, f32[2,256]{1,0:T(2,128)S(1)} %copy-done.12, ...), custom_call_target="tpu_custom_call" | custom-call | flops 3617587200 | bytes 3391488 | tf_op jit(solution)/shard_map/pallas_call | solution.py:282
  129.7 3.3 %shard_map.105 = bf16[16,1024]{1,0:T(8,128)(2,1)S(1)} custom-call(bf16[4,69,2,8,128]{4,3,2,1,0:T(8,128)(2,1)S(1)} %copy-done.2, bf16[4,69,2,8,128]{4,3,2,1,0:T(8,128)(2,1)S(1)} %shard_map.103.refs_1_, s32[1,1024]{1,0:T(1,128)S(1)} %copy-done.10, s32[1,1024]{1,0:T(1,128)S(1)} %copy-done.8), custom_call_target="tpu_custom_call" | custom-call | flops 2315255808 | bytes 2260992 | tf_op jit(solution)/shard_map/pallas_call | solution.py:327
  133.0 18.7 %all-gather = bf16[128,1024]{1,0:T(8,128)(2,1)} all-gather(bf16[32,1024]{1,0:T(8,128)(2,1)S(1)} %pad_maximum_fusion.1), channel_id=2, replica_groups=mesh['mem'=4,'reg'=8] {'mem'}, dimensions={0}, use_global_device_ids=true | all-gather | bytes 327680 | tf_op jit(solution)/shard_map/all_gather | solution.py:341
  151.7 1.9 collective-permute-start.9
  153.6 2.4 %collective-permute-start.8 = (bf16[1,128,1024]{2,1,0:T(8,128)(2,1)}, bf16[1,128,1024]{2,1,0:T(8,128)(2,1)}, u32[]{:S(2)}, u32[]{:S(2)}) collective-permute-start(bf16[1,128,1024]{2,1,0:T(8,128)(2,1)} %bitcast.5), channel_id=1, source_target_pairs={{0,1},{1,2},{2,3},{3,4},{4,5},{5,6},{6,7},{8,9},{9,10},{10,11},{11... | collective-permute-start | bytes 786440 | tf_op jit(solution)/shard_map/ppermute | solution.py:346
  156.1 1.3 dynamic_slice.25
  158.0 0.7 add_multiply_fusion
  158.8 2.9 %collective-permute-done.8 = bf16[1,128,1024]{2,1,0:T(8,128)(2,1)} collective-permute-done((bf16[1,128,1024]{2,1,0:T(8,128)(2,1)}, bf16[1,128,1024]{2,1,0:T(8,128)(2,1)}, u32[]{:S(2)}, u32[]{:S(2)}) %collective-permute-start.8) | collective-permute-done | bytes 262176 | tf_op jit(solution)/shard_map/ppermute | solution.py:346
  161.7 1.3 convert_reduce_fusion
  162.9 0.9 fusion.40
  163.8 3.7 %multiply_reduce_fusion = (f32[]{:T(128)}, f32[128,128]{1,0:T(8,128)S(1)}) fusion(f32[3,1024]{1,0:T(4,128)S(1)} %get-tuple-element.64, bf16[1,128,1024]{2,1,0:T(8,128)(2,1)} %collective-permute-done.9, bf16[1,128,1024]{2,1,0:T(8,128)(2,1)} %bitcast.5, bf16[1,128,1024]{2,1,0:T(8,128)(2,1)} %collective-permute-done.8, f32[3,1024]{1,0:T(4,128)S(1)} %get-tuple-element.55), kind=kOutput, calls=%fused_computation.28 | convolution fusion | flops 607600640 | bytes 876548 | tf_op jit(solution)/shard_map/dot_general | solution.py:221
  168.2 0.6 broadcast_divide_fusion
  168.8 0.9 copy.25
  169.8 4.5 %all-to-all-start.3 = ((bf16[4,69,2,8,128]{4,3,2,1,0:T(8,128)(2,1)}), bf16[4,69,2,8,128]{4,3,2,1,0:T(8,128)(2,1)}, u32[]{:S(2)}, u32[]{:S(2)}) async-start(bf16[4,69,2,8,128]{4,3,2,1,0:T(8,128)(2,1)} %copy-done), calls=%async_computation.3 | async-start | bytes 2260992 | tf_op jit(solution)/shard_map/all_to_all | solution.py:308
  174.3 3.3 %while.13 = (s32[]{:T(128)}, f32[128,128]{0,1:T(8,128)S(1)}, f32[128,128]{1,0:T(8,128)S(1)}, s32[]{:T(128)}) while((s32[]{:T(128)}, f32[128,128]{0,1:T(8,128)S(1)}, f32[128,128]{1,0:T(8,128)S(1)}, s32[]{:T(128)}) %tuple.38), condition=%wide.region_3.4_spmd.clone, body=%wide.region_2.3_spmd.clone.sunk | while | flops 75563008 | bytes 852021 | solution.py:237
  174.8 0.3 convolution_bitcast_fusion.3
  175.6 0.3 convolution_bitcast_fusion.3
  177.2 0.3 convolution_bitcast_fusion.3
  177.6 2.5 %fusion.19 = f32[128,1]{0,1:T(1,128)S(1)} fusion(f32[3,1024]{1,0:T(4,128)S(1)} %get-tuple-element.64, f32[3,1024,1]{1,0,2:T(4,128)S(1)} %get-tuple-element.54, bf16[1,128,1024]{2,1,0:T(8,128)(2,1)} %collective-permute-done.9, bf16[1,128,1024]{2,1,0:T(8,128)(2,1)} %bitcast.5, bf16[1,128,1024]{2,1,0:T(8,128)(2,1)} %collective-permute-done.8), kind=kOutput, calls=%fused_computation.15 | convolution fusion | flops 6291456 | bytes 811520 | tf_op jit(solution)/shard_map/dot_general | solution.py:239
  180.8 21.2 %all-to-all-done.3.refs_3_ = bf16[4,69,2,8,128]{4,3,2,1,0:T(8,128)(2,1)} async-done(((bf16[4,69,2,8,128]{4,3,2,1,0:T(8,128)(2,1)}), bf16[4,69,2,8,128]{4,3,2,1,0:T(8,128)(2,1)}, u32[]{:S(2)}, u32[]{:S(2)}) %all-to-all-start.3) | async-done | bytes 1130528 | tf_op jit(solution)/shard_map/all_to_all | solution.py:308
  202.0 5.5 %shard_map.106 = bf16[69,4,64,128]{3,2,1,0:T(8,128)(2,1)} custom-call(bf16[4,69,2,8,128]{4,3,2,1,0:T(8,128)(2,1)S(1)} %all-to-all-done._.refs_0_, bf16[4,69,2,8,128]{4,3,2,1,0:T(8,128)(2,1)S(1)} %all-to-all-done.1._.refs_1_, bf16[4,69,2,8,128]{4,3,2,1,0:T(8,128)(2,1)S(1)} %all-to-all-done.2.refs_2_, bf16[4,69,2,8,128]{4,3,2,1,0:T(8,128)(2,1)} %all-to-all-done.3.refs_3_, ...), custom_call_target="tpu_custom_call" | custom-call | flops 1157627904 | bytes 9043968 | tf_op jit(solution)/shard_map/pallas_call | solution.py:376
  (72 shorter events, 3.9 us)
Async XLA Ops:
  0.0 13.2 %copy-start.16 = (bf16[2,69,128]{2,0,1:T(2,128)(2,1)S(1)}, bf16[2,69,128]{2,0,1:T(2,128)(2,1)}, u32[]{:S(2)}) copy-start(bf16[2,69,128]{2,0,1:T(2,128)(2,1)} %param.15) | copy-start | bytes 105988
  0.0 13.2 %copy-start.13 = (f32[2,128]{1,0:T(2,128)S(1)}, f32[2,128]{1,0:T(2,128)}, u32[]{:S(2)}) copy-start(f32[2,128]{1,0:T(2,128)} %_.1) | copy-start | bytes 3076
  0.0 13.4 %copy-start.14 = (bf16[2,9,128,69]{2,0,3,1:T(2,128)(2,1)S(1)}, bf16[2,9,128,69]{2,0,3,1:T(2,128)(2,1)}, u32[]{:S(2)}) copy-start(bf16[2,9,128,69]{2,0,3,1:T(2,128)(2,1)} %param.13) | copy-start | bytes 953860
  8.8 11.7 %collective-permute-start.1 = (bf16[8,69,2,256]{3,2,1,0:T(2,128)(2,1)}, bf16[8,69,2,256]{3,2,1,0:T(2,128)(2,1)S(1)}, u32[]{:S(2)}, u32[]{:S(2)}) collective-permute-start(bf16[8,69,2,256]{3,2,1,0:T(2,128)(2,1)} %get-tuple-element.62), channel_id=1, source_target_pairs={{1,0},{2,1},{3,2},{4,3},{5,4},{6,5},{7,6},{9,8},{10,9},{11,10},{12... | collective-permute-start | bytes 1695752 | tf_op jit(solution)/shard_map/ppermute | solution.py:314
  10.8 11.1 %collective-permute-start = (bf16[8,69,2,256]{3,2,1,0:T(2,128)(2,1)}, bf16[8,69,2,256]{3,2,1,0:T(2,128)(2,1)S(1)}, u32[]{:S(2)}, u32[]{:S(2)}) collective-permute-start(bf16[8,69,2,256]{3,2,1,0:T(2,128)(2,1)} %get-tuple-element.63), channel_id=1, source_target_pairs={{0,1},{1,2},{2,3},{3,4},{4,5},{5,6},{6,7},{8,9},{9,10},{10,11},{11... | collective-permute-start | bytes 1695752 | tf_op jit(solution)/shard_map/ppermute | solution.py:313
  13.4 81.4 %copy-start.5 = (bf16[2,72,128]{2,1,0:T(8,128)(2,1)}, bf16[2,72,128]{2,1,0:T(8,128)(2,1)S(1)}, u32[]{:S(2)}) copy-start(bf16[2,72,128]{2,1,0:T(8,128)(2,1)S(1)} %pad.25.back_ref) | copy-start | bytes 110596
  14.3 80.5 %copy-start.3 = (bf16[2,384,216]{2,1,0:T(8,128)(2,1)}, bf16[2,384,216]{2,1,0:T(8,128)(2,1)S(1)}, u32[]{:S(2)}) copy-start(bf16[2,384,216]{2,1,0:T(8,128)(2,1)S(1)} %copy.17.mix_ref) | copy-start | bytes 995332
  22.0 72.8 %copy-start.11 = (f32[2,256]{1,0:T(2,128)}, f32[2,256]{1,0:T(2,128)S(1)}, u32[]{:S(2)}) copy-start(f32[2,256]{1,0:T(2,128)S(1)} %broadcast_in_dim.9.live_ref) | copy-start | bytes 6148
  36.0 32.7 %all-to-all-start = ((bf16[4,69,2,8,128]{4,3,2,1,0:T(8,128)(2,1)}), bf16[4,69,2,8,128]{4,3,2,1,0:T(8,128)(2,1)S(1)}, u32[]{:S(2)}, u32[]{:S(2)}) async-start(bf16[4,69,2,8,128]{4,3,2,1,0:T(8,128)(2,1)} %shard_map.100._.refs_0_), calls=%async_computation | async-start | bytes 2260992 | tf_op jit(solution)/shard_map/all_to_all | solution.py:308
  40.9 9.4 %collective-permute-start.3 = (bf16[8,69,2,256]{3,2,1,0:T(2,128)(2,1)}, bf16[8,69,2,256]{3,2,1,0:T(2,128)(2,1)S(1)}, u32[]{:S(2)}, u32[]{:S(2)}) collective-permute-start(bf16[8,69,2,256]{3,2,1,0:T(2,128)(2,1)} %get-tuple-element.60), channel_id=1, source_target_pairs={{1,0},{2,1},{3,2},{4,3},{5,4},{6,5},{7,6},{9,8},{10,9},{11,10},{12... | collective-permute-start | bytes 1695752 | tf_op jit(solution)/shard_map/ppermute | solution.py:314
  42.9 10.9 %collective-permute-start.2 = (bf16[8,69,2,256]{3,2,1,0:T(2,128)(2,1)S(1)}, bf16[8,69,2,256]{3,2,1,0:T(2,128)(2,1)S(1)}, u32[]{:S(2)}, u32[]{:S(2)}) collective-permute-start(bf16[8,69,2,256]{3,2,1,0:T(2,128)(2,1)S(1)} %get-tuple-element.61), channel_id=1, source_target_pairs={{0,1},{1,2},{2,3},{3,4},{4,5},{5,6},{6,7},{8,9},{9,10},{10,11},{11... | collective-permute-start | bytes 1695752 | tf_op jit(solution)/shard_map/ppermute | solution.py:313
  68.7 40.2 %all-to-all-start.1 = ((bf16[4,69,2,8,128]{4,3,2,1,0:T(8,128)(2,1)}), bf16[4,69,2,8,128]{4,3,2,1,0:T(8,128)(2,1)S(1)}, u32[]{:S(2)}, u32[]{:S(2)}) async-start(bf16[4,69,2,8,128]{4,3,2,1,0:T(8,128)(2,1)} %shard_map.101.refs_1_), calls=%async_computation.1 | async-start | bytes 2260992 | tf_op jit(solution)/shard_map/all_to_all | solution.py:308
  72.8 22.0 %collective-permute-start.5 = (bf16[8,69,2,256]{3,2,1,0:T(2,128)(2,1)}, bf16[8,69,2,256]{3,2,1,0:T(2,128)(2,1)S(1)}, u32[]{:S(2)}, u32[]{:S(2)}) collective-permute-start(bf16[8,69,2,256]{3,2,1,0:T(2,128)(2,1)} %get-tuple-element.58), channel_id=1, source_target_pairs={{1,0},{2,1},{3,2},{4,3},{5,4},{6,5},{7,6},{9,8},{10,9},{11,10},{12... | collective-permute-start | bytes 1695752 | tf_op jit(solution)/shard_map/ppermute | solution.py:314
  74.8 20.1 %collective-permute-start.4 = (bf16[8,69,2,256]{3,2,1,0:T(2,128)(2,1)}, bf16[8,69,2,256]{3,2,1,0:T(2,128)(2,1)}, u32[]{:S(2)}, u32[]{:S(2)}) collective-permute-start(bf16[8,69,2,256]{3,2,1,0:T(2,128)(2,1)} %get-tuple-element.59), channel_id=1, source_target_pairs={{0,1},{1,2},{2,3},{3,4},{4,5},{5,6},{6,7},{8,9},{9,10},{10,11},{11... | collective-permute-start | bytes 1695752 | tf_op jit(solution)/shard_map/ppermute | solution.py:313
  82.4 31.4 %collective-permute-start.7 = (bf16[8,69,2,256]{3,2,1,0:T(2,128)(2,1)}, bf16[8,69,2,256]{3,2,1,0:T(2,128)(2,1)}, u32[]{:S(2)}, u32[]{:S(2)}) collective-permute-start(bf16[8,69,2,256]{3,2,1,0:T(2,128)(2,1)} %get-tuple-element.56), channel_id=1, source_target_pairs={{1,0},{2,1},{3,2},{4,3},{5,4},{6,5},{7,6},{9,8},{10,9},{11,10},{12... | collective-permute-start | bytes 1695752 | tf_op jit(solution)/shard_map/ppermute | solution.py:314
  84.3 29.4 %collective-permute-start.6 = (bf16[8,69,2,256]{3,2,1,0:T(2,128)(2,1)}, bf16[8,69,2,256]{3,2,1,0:T(2,128)(2,1)}, u32[]{:S(2)}, u32[]{:S(2)}) collective-permute-start(bf16[8,69,2,256]{3,2,1,0:T(2,128)(2,1)} %get-tuple-element.57), channel_id=1, source_target_pairs={{0,1},{1,2},{2,3},{3,4},{4,5},{5,6},{6,7},{8,9},{9,10},{10,11},{11... | collective-permute-start | bytes 1695752 | tf_op jit(solution)/shard_map/ppermute | solution.py:313
  89.8 4.9 %copy-start.7 = (s32[1,1024]{1,0:T(1,128)}, s32[1,1024]{1,0:T(1,128)S(1)}, u32[]{:S(2)}) copy-start(s32[1,1024]{1,0:T(1,128)S(1)} %get-tuple-element.67.refs_3_) | copy-start | bytes 12292
  89.9 4.9 %copy-start.9 = (s32[1,1024]{1,0:T(1,128)}, s32[1,1024]{1,0:T(1,128)S(1)}, u32[]{:S(2)}) copy-start(s32[1,1024]{1,0:T(1,128)S(1)} %get-tuple-element.68.refs_2_) | copy-start | bytes 12292
  107.9 1.0 copy-start.1
  108.9 60.8 %all-to-all-start.2 = ((bf16[4,69,2,8,128]{4,3,2,1,0:T(8,128)(2,1)}), bf16[4,69,2,8,128]{4,3,2,1,0:T(8,128)(2,1)S(1)}, u32[]{:S(2)}, u32[]{:S(2)}) async-start(bf16[4,69,2,8,128]{4,3,2,1,0:T(8,128)(2,1)} %copy-done.1), calls=%async_computation.2 | async-start | bytes 2260992 | tf_op jit(solution)/shard_map/all_to_all | solution.py:308
  113.8 15.9 %copy-start.2 = (bf16[4,69,2,8,128]{4,3,2,1,0:T(8,128)(2,1)S(1)}, bf16[4,69,2,8,128]{4,3,2,1,0:T(8,128)(2,1)}, u32[]{:S(2)}) copy-start(bf16[4,69,2,8,128]{4,3,2,1,0:T(8,128)(2,1)} %copy-done.1) | copy-start | bytes 3391492
  113.8 1.1 copy-start.4
  114.9 0.8 copy-start.6
  115.6 0.7 copy-start.12
  116.3 13.3 %copy-start.8 = (s32[1,1024]{1,0:T(1,128)S(1)}, s32[1,1024]{1,0:T(1,128)}, u32[]{:S(2)}) copy-start(s32[1,1024]{1,0:T(1,128)} %copy-done.7) | copy-start | bytes 12292
  116.3 13.4 %copy-start.10 = (s32[1,1024]{1,0:T(1,128)S(1)}, s32[1,1024]{1,0:T(1,128)}, u32[]{:S(2)}) copy-start(s32[1,1024]{1,0:T(1,128)} %copy-done.9) | copy-start | bytes 12292
  129.7 3.4 %copy-start = (bf16[4,69,2,8,128]{4,3,2,1,0:T(8,128)(2,1)}, bf16[4,69,2,8,128]{4,3,2,1,0:T(8,128)(2,1)S(1)}, u32[]{:S(2)}) copy-start(bf16[4,69,2,8,128]{4,3,2,1,0:T(8,128)(2,1)S(1)} %shard_map.103.refs_1_) | copy-start | bytes 3391492
  129.7 33.2 %copy-start.15 = (s32[8,1024]{1,0:T(8,128)S(1)}, s32[8,1024]{1,0:T(8,128)}, u32[]{:S(2)}) copy-start(s32[8,1024]{1,0:T(8,128)} %param.16) | copy-start | bytes 98308
  151.7 7.0 %collective-permute-start.9 = (bf16[1,128,1024]{2,1,0:T(8,128)(2,1)}, bf16[1,128,1024]{2,1,0:T(8,128)(2,1)}, u32[]{:S(2)}, u32[]{:S(2)}) collective-permute-start(bf16[1,128,1024]{2,1,0:T(8,128)(2,1)} %bitcast.5), channel_id=1, source_target_pairs={{1,0},{2,1},{3,2},{4,3},{5,4},{6,5},{7,6},{9,8},{10,9},{11,10},{12... | collective-permute-start | bytes 786440 | tf_op jit(solution)/shard_map/ppermute | solution.py:348
  153.6 8.0 %collective-permute-start.8 = (bf16[1,128,1024]{2,1,0:T(8,128)(2,1)}, bf16[1,128,1024]{2,1,0:T(8,128)(2,1)}, u32[]{:S(2)}, u32[]{:S(2)}) collective-permute-start(bf16[1,128,1024]{2,1,0:T(8,128)(2,1)} %bitcast.5), channel_id=1, source_target_pairs={{0,1},{1,2},{2,3},{3,4},{4,5},{5,6},{6,7},{8,9},{9,10},{10,11},{11... | collective-permute-start | bytes 786440 | tf_op jit(solution)/shard_map/ppermute | solution.py:346
  169.8 32.2 %all-to-all-start.3 = ((bf16[4,69,2,8,128]{4,3,2,1,0:T(8,128)(2,1)}), bf16[4,69,2,8,128]{4,3,2,1,0:T(8,128)(2,1)}, u32[]{:S(2)}, u32[]{:S(2)}) async-start(bf16[4,69,2,8,128]{4,3,2,1,0:T(8,128)(2,1)} %copy-done), calls=%async_computation.3 | async-start | bytes 2260992 | tf_op jit(solution)/shard_map/all_to_all | solution.py:308
